TPU v7x, 128 devices: a whole 4x4x4 slice. The times are simulated.
128 devices in a mesh: dp: 4 (over x_lo, core), tm: 32 (over x_hi, y, z).
Axes of the slice: x: 4 (x_hi: 2, x_lo: 2; x = x_hi * 2 + x_lo), y: 4, z: 4, core: 2. Of those that a mesh axis runs over, the one named last changes fastest.
Arguments:
- queries: bfloat16 [8192, 2560], P('tm', 'dp'), may hold values from -30 to 30
- keys: bfloat16 [8192, 2560], P('tm', 'dp'), may hold values from -30 to 30
- values: bfloat16 [8192, 2560], P('tm', 'dp'), may hold values from -6 to 6
- query_tangent: bfloat16 [8192, 2560], P('tm', 'dp'), may hold values from -6 to 6
- key_tangent: bfloat16 [8192, 2560], P('tm', 'dp'), may hold values from -6 to 6
- value_tangent: bfloat16 [8192, 2560], P('tm', 'dp'), may hold values from -6 to 6
- out_weight: bfloat16 [2560, 5120], P('dp'), may hold values from -0.75 to 0.75
Outputs:
- attended: bfloat16 [8192, 5120], P('tm', 'dp')
- attended_tangent: bfloat16 [8192, 5120], P('tm', 'dp')
All inputs are finite; a program needn't handle non-finite values.
Results may differ from a plain program's by a relative error of at most 0.017.
Values may be sent and summed in bfloat16 or wider, within the bound.
No kernel may reach another device: no remote copies, remote signals or barrier semaphores. Data moves between devices by JAX's collectives and lax.ppermute only.
A program may use at most 320 MiB of HBM per device.

v0:
```python
import math

import jax
import jax.numpy as jnp
from jax import lax
from jax.sharding import PartitionSpec as P

DH = 128


def block_sums(carry, pieces, query_heads, dquery_heads):
    running, total, slope, acc, acc_tangent = carry
    key_rows, value_rows, dkey_rows, dvalue_rows = pieces
    scale = 1.0 / DH**0.5
    count = key_rows.shape[0]
    key_heads = key_rows.reshape(count, -1, DH)
    dkey_heads = dkey_rows.reshape(count, -1, DH)
    value_heads = value_rows.reshape(count, -1, DH)
    dvalue_heads = dvalue_rows.reshape(count, -1, DH)
    scores = (
        jnp.einsum("qhd,khd->hqk", query_heads, key_heads, preferred_element_type=jnp.float32)
        * scale
    )
    slope_scores = (
        jnp.einsum("qhd,khd->hqk", dquery_heads, key_heads, preferred_element_type=jnp.float32)
        + jnp.einsum("qhd,khd->hqk", query_heads, dkey_heads, preferred_element_type=jnp.float32)
    ) * scale
    new_max = jnp.maximum(running, jnp.max(scores, axis=2))
    factor = jnp.exp(running - new_max)
    expo = jnp.exp(scores - new_max[:, :, None])
    weighted = expo * slope_scores
    weight16 = expo.astype(jnp.bfloat16)
    tangent16 = weighted.astype(jnp.bfloat16)
    total = total * factor + jnp.sum(expo, axis=2)
    slope = slope * factor + jnp.sum(weighted, axis=2)
    acc = acc * factor[:, :, None] + jnp.einsum(
        "hqk,khd->hqd", weight16, value_heads, preferred_element_type=jnp.float32
    )
    acc_tangent = (
        acc_tangent * factor[:, :, None]
        + jnp.einsum("hqk,khd->hqd", tangent16, value_heads, preferred_element_type=jnp.float32)
        + jnp.einsum("hqk,khd->hqd", weight16, dvalue_heads, preferred_element_type=jnp.float32)
    )
    return (new_max, total, slope, acc, acc_tangent)


def per_device(queries, keys, values, query_tangent, key_tangent, value_tangent, out_weight):
    local_rows = queries.shape[0]
    head_count = queries.shape[1] // DH
    query_heads = queries.reshape(local_rows, head_count, DH)
    dquery_heads = query_tangent.reshape(local_rows, head_count, DH)
    start_max = jnp.full((head_count, local_rows), -jnp.inf, jnp.float32)
    zero_rows = jnp.zeros((head_count, local_rows), jnp.float32)
    zero_acc = jnp.zeros((head_count, local_rows, DH), jnp.float32)
    start_sums = (start_max, zero_rows, zero_rows, zero_acc, zero_acc)
    gathered = (
        lax.all_gather(keys, "tm", axis=0, tiled=True),
        lax.all_gather(values, "tm", axis=0, tiled=True),
        lax.all_gather(key_tangent, "tm", axis=0, tiled=True),
        lax.all_gather(value_tangent, "tm", axis=0, tiled=True),
    )
    whole = gathered[0].shape[0]
    block = math.gcd(whole, 512)
    blocked = tuple((g.reshape(whole // block, block, g.shape[1]) for g in gathered))

    def sum_step(carry, pieces):
        return (block_sums(carry, pieces, query_heads, dquery_heads), None)

    sums, unused = lax.scan(sum_step, start_sums, blocked)
    running, total, slope, acc, acc_tangent = sums
    heads_out = (acc / total[:, :, None]).astype(jnp.bfloat16)
    heads_tangent = ((acc_tangent - (slope / total)[:, :, None] * acc) / total[:, :, None]).astype(
        jnp.bfloat16
    )
    heads_out = heads_out.transpose(1, 0, 2).reshape(local_rows, head_count * DH)
    heads_tangent = heads_tangent.transpose(1, 0, 2).reshape(local_rows, head_count * DH)
    out_terms = jnp.dot(heads_out, out_weight, preferred_element_type=jnp.float32)
    tangent_terms = jnp.dot(heads_tangent, out_weight, preferred_element_type=jnp.float32)
    attended, attended_tangent = (
        lax.psum_scatter(
            out_terms.astype(jnp.bfloat16), "dp", scatter_dimension=1, tiled=True
        ).astype(jnp.float32),
        lax.psum_scatter(
            tangent_terms.astype(jnp.bfloat16), "dp", scatter_dimension=1, tiled=True
        ).astype(jnp.float32),
    )
    return (attended.astype(jnp.bfloat16), attended_tangent.astype(jnp.bfloat16))


def solution(mesh):
    in_specs = (
        P("tm", "dp"),
        P("tm", "dp"),
        P("tm", "dp"),
        P("tm", "dp"),
        P("tm", "dp"),
        P("tm", "dp"),
        P("dp", None),
    )
    out_specs = (P("tm", "dp"), P("tm", "dp"))
    return jax.shard_map(
        per_device, mesh=mesh, in_specs=in_specs, out_specs=out_specs, check_vma=False
    )
```

profile of v0, /device:TPU:1, one launch (start us, length us, event | category | flops | bytes accessed | tf_op | source)
XLA Modules:
  0.0 983.5 jit_solution(3788711265124049431)
XLA Ops:
  13.2 117.9 %all-gather.5.cloned.1.call-done = bf16[8192,640]{1,0:T(8,128)(2,1)} async-done(((bf16[256,640]{1,0:T(8,128)(2,1)}), bf16[8192,640]{1,0:T(8,128)(2,1)}) %all-gather.5.cloned.1.call-update) | async-done | bytes 10485776 | tf_op jit(solution)/shard_map/all_gather | solution.py:57
  131.1 118.2 %all-gather.7.cloned.1.call-done = bf16[8192,640]{1,0:T(8,128)(2,1)} async-done(((bf16[256,640]{1,0:T(8,128)(2,1)}), bf16[8192,640]{1,0:T(8,128)(2,1)}) %all-gather.7.cloned.1.call-update) | async-done | bytes 10485776 | tf_op jit(solution)/shard_map/all_gather | solution.py:59
  249.3 118.2 %all-gather.9.cloned.1.call-done = bf16[8192,640]{1,0:T(8,128)(2,1)} async-done(((bf16[256,640]{1,0:T(8,128)(2,1)}), bf16[8192,640]{1,0:T(8,128)(2,1)}) %all-gather.9.cloned.1.call-update) | async-done | bytes 10485776 | tf_op jit(solution)/shard_map/all_gather | solution.py:58
  367.6 118.1 %all-gather.11.cloned.1.call-done = bf16[8192,640]{1,0:T(8,128)(2,1)} async-done(((bf16[256,640]{1,0:T(8,128)(2,1)}), bf16[8192,640]{1,0:T(8,128)(2,1)}) %all-gather.11.cloned.1.call-update) | async-done | bytes 10485776 | tf_op jit(solution)/shard_map/all_gather | solution.py:60
  485.7 414.0 %while.19 = (s32[]{:T(128)}, f32[5,256]{1,0:T(8,128)S(1)}, f32[5,256]{1,0:T(8,128)S(1)}, f32[5,256]{1,0:T(8,128)S(1)}, f32[5,256,128]{2,1,0:T(8,128)}, /*index=5...) while((s32[]{:T(128)}, f32[5,256]{1,0:T(8,128)S(1)}, ...), condition=%wide.region_4.5_spmd.clone, body=%wide.region_0.4_spmd.clone.sunk | while | flops 1019585280 | bytes 45670608 | solution.py:69
  489.7 3.0 fusion.61
  494.1 3.9 fusion.62
  519.8 3.9 fusion.62
  545.7 3.9 fusion.62
  571.6 3.9 fusion.62
  593.1 3.0 fusion.61
  597.5 3.9 fusion.62
  623.4 3.9 fusion.62
  644.9 3.0 fusion.61
  649.3 3.9 fusion.62
  675.1 3.9 fusion.62
  696.6 3.0 fusion.61
  701.0 3.9 fusion.62
  726.9 3.9 fusion.62
  748.4 3.0 fusion.61
  752.8 3.9 fusion.62
  778.7 3.9 fusion.62
  800.2 3.0 fusion.61
  804.5 3.9 fusion.62
  830.4 3.9 fusion.62
  851.9 3.0 fusion.61
  856.3 3.9 fusion.62
  882.2 3.9 fusion.62
  902.5 6.6 convolution_convert_fusion.1
  909.1 6.6 convolution_convert_fusion
  915.8 24.6 %reduce-scatter.3.cloned.1.call-done = bf16[256,1280]{1,0:T(8,128)(2,1)} async-done(((bf16[256,5120]{1,0:T(8,128)(2,1)}), bf16[256,1280]{1,0:T(8,128)(2,1)}) %reduce-scatter.3.cloned.1.call-update) | async-done | bytes 655376 | tf_op jit(solution)/shard_map/reduce_scatter | solution.py:80
  940.4 36.3 %reduce-scatter.5.cloned.1.call-done = bf16[256,1280]{1,0:T(8,128)(2,1)} async-done(((bf16[256,5120]{1,0:T(8,128)(2,1)}), bf16[256,1280]{1,0:T(8,128)(2,1)}) %reduce-scatter.5.cloned.1.call-update) | async-done | bytes 655376 | tf_op jit(solution)/shard_map/reduce_scatter | solution.py:83
  (340 shorter events, 337.9 us)
Async XLA Ops:
  7.2 4.9 copy-start.2
  7.2 123.9 %all-gather.5.cloned.1.call-start = ((), (), s32[]{:S(2)}) async-start(), calls=%async_computation.2 | async-start | bytes 10813440 | tf_op jit(solution)/shard_map/all_gather | solution.py:57
  7.9 241.4 %all-gather.7.cloned.1.call-start = ((), (), s32[]{:S(2)}) async-start(), calls=%async_computation.3 | async-start | bytes 10813440 | tf_op jit(solution)/shard_map/all_gather | solution.py:59
  8.7 358.9 %all-gather.9.cloned.1.call-start = ((), (), s32[]{:S(2)}) async-start(), calls=%async_computation.4 | async-start | bytes 10813440 | tf_op jit(solution)/shard_map/all_gather | solution.py:58
  9.4 476.3 %all-gather.11.cloned.1.call-start = ((), (), s32[]{:S(2)}) async-start(), calls=%async_computation.5 | async-start | bytes 10813440 | tf_op jit(solution)/shard_map/all_gather | solution.py:60
  10.0 930.4 %reduce-scatter.3.cloned.1.call-start = ((), (), s32[]{:S(2)}) async-start(), calls=%async_computation.6 | async-start | bytes 3276800 | tf_op jit(solution)/shard_map/reduce_scatter | solution.py:80
  506.8 2.9 copy-start
  510.6 0.8 copy-start.1
  532.7 2.9 copy-start
  536.4 0.8 copy-start.1
  558.6 2.9 copy-start
  562.3 0.8 copy-start.1
  584.4 2.9 copy-start
  588.2 0.8 copy-start.1
  610.3 2.9 copy-start
  636.2 2.9 copy-start
  640.0 0.8 copy-start.1
  662.1 2.9 copy-start
  688.0 2.9 copy-start
  713.8 2.9 copy-start
  739.7 2.9 copy-start
  743.5 0.8 copy-start.1
  765.6 2.9 copy-start
  769.4 0.8 copy-start.1
  791.5 2.9 copy-start
  817.4 2.9 copy-start
  843.3 2.9 copy-start
  847.0 0.8 copy-start.1
  869.1 2.9 copy-start
  872.9 0.8 copy-start.1
  895.0 2.9 copy-start
  909.1 67.6 %reduce-scatter.5.cloned.1.call-start = ((), (), s32[]{:S(2)}) async-start(), calls=%async_computation.7 | async-start | bytes 3276800 | tf_op jit(solution)/shard_map/reduce_scatter | solution.py:83
  (7 other events, 5.9 us)
Sparse Core Ops, SparseCore 0:
  11.2 119.8 all-gather.4
  134.3 115.0 all-gather.6
  252.5 115.0 all-gather.8
  370.6 115.0 all-gather.10
  909.2 31.0 reduce-scatter.2
  943.2 33.4 reduce-scatter.4
where the time goes:
time: 989 us; the launch traced here: 984 us
  waiting for transfers between devices  536 us (54%)
  matrix products  256 us (26%)
  local copies, waits for them, and re-layouts  169 us (17%)
  between operations  14.2 us (1%)
    dynamic_slice x96, local copies, waits for them, and re-layouts, per_device(): sums, unused = lax.scan(sum_step, start_sums, blocked)  157 us
    all_gather x1, waiting for transfers between devices, per_device(): lax.all_gather(values, 'tm', axis=0, tiled=True)  118 us
    all_gather x1, waiting for transfers between devices, per_device(): lax.all_gather(key_tangent, 'tm', axis=0, tiled=True)  118 us
    all_gather x1, waiting for transfers between devices, per_device(): lax.all_gather(value_tangent, 'tm', axis=0, tiled=True)  118 us
    all_gather x1, waiting for transfers between devices, per_device(): lax.all_gather(keys, 'tm', axis=0, tiled=True)  118 us
    dot_general x16, matrix products, block_sums(): jnp.einsum('qhd,khd->hqk', query_heads, dkey_heads, preferred_element_typ...  62.5 us
    dot_general x16, matrix products, block_sums(): jnp.einsum('qhd,khd->hqk', dquery_heads, key_heads, preferred_element_typ...  48.7 us
    dot_general x16, matrix products, block_sums(): jnp.einsum('hqk,khd->hqd', tangent16, value_heads, preferred_element_type...  46.7 us
  transfers between devices with their start and end apart: 6, of which 6 were waited for; matrix products, arithmetic and copies ran while one was open for 1% of the time, Pallas kernels for 0%

commit v1 on v0

v1 whole, which is shorter than its diff:
```python
import functools
import math

import jax
import jax.numpy as jnp
from jax import lax
from jax.experimental import pallas as pl
from jax.experimental.pallas import tpu as pltpu
from jax.sharding import Mesh, PartitionSpec as P

DH = 128
ROWS = 256
SCALE = 1.0 / DH**0.5
LOG2_SCALE = SCALE * math.log2(math.e)
NEAR = 4
STAT_LANES = 8
GROUPS = ((0, 5, "y", "z"),)

SWAP = ((0, 0), (1, 2), (2, 1), (3, 3))
CROSS = tuple(
    ((xl * 2 + co) * 2 + xh, ((1 - xl) * 2 + xh) * 2 + co)
    for xl in range(2)
    for co in range(2)
    for xh in range(2)
)
DIAGONAL = ((0, 3), (1, 2), (2, 1), (3, 0))


def shift(array, axis, by):
    return lax.ppermute(array, axis, [(i, (i + by) % NEAR) for i in range(NEAR)])


def other(array, axis):
    return lax.ppermute(array, axis, [(0, 1), (1, 0)])


def dot_t(a, b):
    return lax.dot_general(a, b, (((1,), (1,)), ((), ())), preferred_element_type=jnp.float32)


def slice_sums(query, dquery, keys, values, old):
    zero = jnp.zeros_like(query)
    lhs = jnp.concatenate(
        [jnp.concatenate([query, zero], axis=1), jnp.concatenate([dquery, query], axis=1)], axis=0
    )
    scores = []
    slopes = []
    for key in keys:
        both = dot_t(lhs, jnp.concatenate([key[0:ROWS], key[ROWS : 2 * ROWS]], axis=1))
        scores.append(both[:ROWS])
        slopes.append(both[ROWS:])
    top = functools.reduce(jnp.maximum, scores)
    new_max = jnp.max(top, axis=1, keepdims=True)
    if old is not None:
        new_max = jnp.maximum(new_max, old[0])
    offset = new_max * LOG2_SCALE
    total = slope = primal = tangent = None
    for value, score, slope_score in zip(values, scores, slopes):
        expo = jnp.exp2(score * LOG2_SCALE - offset)
        weighted = expo * slope_score
        total = expo if total is None else total + expo
        slope = weighted if slope is None else slope + weighted
        lhs = jnp.concatenate([expo.astype(jnp.bfloat16), weighted.astype(jnp.bfloat16)], axis=0)
        rhs = jnp.concatenate([value[0:ROWS], value[ROWS : 2 * ROWS]], axis=1)
        both = jnp.dot(lhs, rhs, preferred_element_type=jnp.float32)
        primal = both[:ROWS] if primal is None else primal + both[:ROWS]
        tangent = both[ROWS:, :DH] if tangent is None else tangent + both[ROWS:, :DH]
    total = jnp.sum(total, axis=1, keepdims=True)
    slope = jnp.sum(slope, axis=1, keepdims=True) * SCALE
    acc = primal[:, :DH]
    acc_tangent = primal[:, DH:] + tangent * SCALE
    if old is not None:
        factor = jnp.exp2(old[0] * LOG2_SCALE - offset)
        total = total + old[1] * factor
        slope = slope + old[2] * factor
        acc = acc + old[3] * factor
        acc_tangent = acc_tangent + old[4] * factor
    return new_max, total, slope, acc, acc_tangent


def three_parts(value):
    high = value.astype(jnp.bfloat16).astype(jnp.float32)
    rest = value - high
    middle = rest.astype(jnp.bfloat16).astype(jnp.float32)
    return high, middle, rest - middle


def attend_kernel(slices, blocks, first, last, heads, *refs):
    queries = refs[:slices]
    keys = refs[slices : slices + blocks]
    values = refs[slices + blocks : slices + 2 * blocks]
    rest = refs[slices + 2 * blocks :]
    olds = None if first else rest[:3]
    outs = rest if first else rest[3:]
    head = pl.program_id(0)
    lane = lax.broadcasted_iota(jnp.int32, (ROWS, DH), 1)
    for i in range(slices):
        old = None
        if not first:
            stats = olds[2][i]
            old = (stats[:, 0:1], stats[:, 1:2], stats[:, 2:3], olds[0][i], olds[1][i])
        new_max, total, slope, acc, acc_tangent = slice_sums(
            queries[i][0:ROWS], queries[i][ROWS : 2 * ROWS], keys, values, old
        )
        if not last:
            outs[0][i] = acc
            outs[1][i] = acc_tangent
            outs[2][i] = jnp.where(lane == 0, new_max, jnp.where(lane == 1, total, slope))
            continue
        inverse = 1.0 / total
        mean = slope * inverse
        out = acc * inverse
        at = pl.multiple_of(head * 2 * DH, 2 * DH)
        outs[i][:, pl.ds(at, DH)] = out.astype(jnp.bfloat16)
        outs[i][:, pl.ds(at + DH, DH)] = (acc_tangent * inverse - mean * out).astype(jnp.bfloat16)
        parts = three_parts(new_max * LOG2_SCALE + jnp.log2(total)) + three_parts(mean)
        tail = slice(2 * heads * DH, (2 * heads + 1) * DH)

        @pl.when(head == 0)
        def clear(i=i, tail=tail):
            outs[i][:, tail] = jnp.zeros((ROWS, DH), jnp.bfloat16)

        packed = outs[i][:, tail].astype(jnp.float32)
        for k, part in enumerate(parts):
            packed = jnp.where(lane == head * STAT_LANES + k, part, packed)
        outs[i][:, tail] = packed.astype(jnp.bfloat16)


def attend(queries, blocks, state, last):
    heads = queries[0].shape[1] // DH
    slices = len(queries)
    first = state is None
    query_spec = pl.BlockSpec((2 * ROWS, DH), lambda h: (0, h))

    def half(at):
        return pl.BlockSpec((2 * ROWS, DH), lambda h: (at, h))

    state_spec = pl.BlockSpec((slices, ROWS, DH), lambda h: (0, 0, h))
    state_type = jax.ShapeDtypeStruct((slices, ROWS, heads * DH), jnp.float32)
    part_type = jax.ShapeDtypeStruct((ROWS, (2 * heads + 1) * DH), jnp.bfloat16)
    part_spec = pl.BlockSpec(part_type.shape, lambda h: (0, 0))
    keys = [block[0] for block in blocks]
    values = [block[1] for block in blocks]
    return pl.pallas_call(
        functools.partial(attend_kernel, slices, len(blocks), first, last, heads),
        grid=(heads,),
        in_specs=[query_spec] * slices
        + [half(at) for unused, at in keys]
        + [half(at) for unused, at in values]
        + ([] if first else [state_spec] * 3),
        out_specs=[part_spec] * slices if last else [state_spec] * 3,
        out_shape=[part_type] * slices if last else [state_type] * 3,
        compiler_params=pltpu.CompilerParams(vmem_limit_bytes=48 * 2**20),
        cost_estimate=pl.CostEstimate(
            flops=slices * len(blocks) * heads * 8 * ROWS * ROWS * ROWS * 2,
            bytes_accessed=slices * ROWS * heads * DH * 24,
            transcendentals=slices * len(blocks) * heads * ROWS * ROWS,
        ),
    )(*queries, *[k for k, unused in keys], *[v for v, unused in values], *([] if first else state))


def combine_kernel(heads, *refs):
    parts, out_ref = refs[:-1], refs[-1]
    tails = [p[:, 2 * heads * DH :].astype(jnp.float32) for p in parts]
    for h in range(heads):
        logs = []
        means = []
        for tail in tails:
            c = [tail[:, h * STAT_LANES + k : h * STAT_LANES + k + 1] for k in range(6)]
            logs.append(c[0] + c[1] + c[2])
            means.append(c[3] + c[4] + c[5])
        top = functools.reduce(jnp.maximum, logs)
        shares = [jnp.exp2(x - top) for x in logs]
        whole = 1.0 / functools.reduce(jnp.add, shares)
        shares = [s * whole for s in shares]
        mean = functools.reduce(jnp.add, [s * m for s, m in zip(shares, means)])
        out = tangent = 0.0
        for part, share, own in zip(parts, shares, means):
            o = part[:, 2 * h * DH : (2 * h + 1) * DH].astype(jnp.float32)
            t = part[:, (2 * h + 1) * DH : (2 * h + 2) * DH].astype(jnp.float32)
            out = out + share * o
            tangent = tangent + share * (t + (own - mean) * o)
        out_ref[0:ROWS, h * DH : (h + 1) * DH] = out.astype(jnp.bfloat16)
        out_ref[ROWS : 2 * ROWS, h * DH : (h + 1) * DH] = tangent.astype(jnp.bfloat16)


def combine(parts):
    heads = (parts[0].shape[1] // DH - 1) // 2
    return pl.pallas_call(
        functools.partial(combine_kernel, heads),
        out_shape=jax.ShapeDtypeStruct((2 * ROWS, heads * DH), jnp.bfloat16),
        compiler_params=pltpu.CompilerParams(vmem_limit_bytes=32 * 2**20),
        cost_estimate=pl.CostEstimate(
            flops=10 * ROWS * heads * DH, bytes_accessed=10 * ROWS * heads * DH, transcendentals=0
        ),
    )(*parts)


def group_heads(key_value, query, ring, across):
    whole = lambda array: ((array, 0), (array, 1))
    ahead, behind = shift(key_value, ring, 1), shift(key_value, ring, -1)
    queries = [query] + [shift(query, across, by) for by in (1, -1, 2)]
    near = [whole(key_value), whole(other(key_value, "co"))]
    state = attend(queries, near, None, False)
    far_keys = shift(ahead[: 2 * ROWS], ring, 1)
    far_values = shift(behind[2 * ROWS :], ring, -1)
    middle = [whole(a) for a in (ahead, behind, other(ahead, "co"), other(behind, "co"))]
    state = attend(queries, middle, state, False)
    far = [
        ((far_keys, 0), (far_values, 0)),
        ((other(far_keys, "co"), 0), (other(far_values, "co"), 0)),
    ]
    parts = attend(queries, far, state, True)
    back = [parts[0]] + [shift(p, across, -by) for p, by in zip(parts[1:], (1, -1, 2))]
    return combine(back)


def weight_rows(out_weight):
    xl, co = lax.axis_index("xl"), lax.axis_index("co")
    width = out_weight.shape[1] // 4
    middle = out_weight.shape[0] // 2

    def columns(array, at, count):
        return lax.dynamic_slice_in_dim(array, at * width, count * width, axis=1)

    away = columns(out_weight, (1 - xl) * 2, 2)
    from_far = jnp.concatenate(
        [
            other(away[:middle], "xl"),
            lax.ppermute(away[middle:], ("xl", "xh"), DIAGONAL),
        ],
        axis=0,
    )
    from_core = other(columns(out_weight, xl * 2 + 1 - co, 1), "co")
    from_both = other(columns(from_far, 1 - co, 1), "co")
    return jnp.concatenate(
        [columns(out_weight, xl * 2 + co, 1), columns(from_far, co, 1), from_core, from_both], axis=0
    )


def per_device(queries, keys, values, query_tangent, key_tangent, value_tangent, out_weight):
    pieces = [[], [], [], []]
    swapped = []
    for start, count, ring, across in GROUPS:
        own = slice(start * DH, (start + count) * DH)
        pack = lambda arrays: jnp.concatenate([a[:, own] for a in arrays], axis=0)
        key_value = lax.ppermute(
            pack((keys, key_tangent, values, value_tangent)), ("co", "xh"), SWAP
        )
        query = lax.ppermute(pack((queries, query_tangent)), ("co", "xh"), SWAP)
        swapped.append((key_value, query))
    out_weight, swapped = lax.optimization_barrier((out_weight, swapped))
    weight = weight_rows(out_weight)
    for (key_value, query), (start, count, ring, across) in zip(swapped, GROUPS):
        heads = group_heads(key_value, query, ring, across)
        back = lax.ppermute(heads, ("co", "xh"), SWAP)
        cross = lax.ppermute(heads, ("xl", "co", "xh"), CROSS)
        found = (back, cross, other(back, "co"), other(cross, "co"))
        for held, piece in zip(pieces, found):
            held.append(piece)
    heads = jnp.concatenate([piece for held in pieces for piece in held], axis=1)
    out = jnp.dot(heads, weight, preferred_element_type=jnp.float32).astype(jnp.bfloat16)
    return out[:ROWS], out[ROWS:]


def solution(mesh):
    split = Mesh(mesh.devices.reshape(2, 2, 2, NEAR, NEAR), ("xl", "co", "xh", "y", "z"))
    tokens, features = ("xh", "y", "z"), ("xl", "co")
    block = P(tokens, features)
    return jax.shard_map(
        per_device,
        mesh=split,
        in_specs=(block,) * 6 + (P(features, None),),
        out_specs=(block, block),
        check_vma=False,
    )
```

time: 989 us -> 201 us (0.20)
  waiting for transfers between devices: 536 us -> 88.1 us
  matrix products: 256 us -> 4.97 us
  local copies, waits for them, and re-layouts: 169 us -> 10.6 us
  Pallas kernels: 0 us -> 58.7 us
  starting transfers between devices: 0.23 us -> 35.9 us
  between operations: 14.2 us -> 0.82 us
    all_gather x4 -> x0, waiting for transfers between devices: 472 us -> none  [the longest x1 118 us: per_device(): lax.all_gather(values, 'tm', axis=0, tiled=True)]
    dot_general x98 -> x1, matrix products: 256 us -> 4.97 us  [per_device(): jnp.dot(heads, weight, preferred_element_type=jnp.float32)]
    dynamic_slice x96 -> x2, local copies, waits for them, and re-layouts: 157 us -> 2.36 us  [columns(): return lax.dynamic_slice_in_dim(array, at * width, count * width, axis=1)]
    ppermute x0 -> x25, waiting for transfers between devices: none -> 88.1 us  [the longest x10 46.5 us: shift(): lax.ppermute(array, axis, [(i, (i + by) % NEAR) for i in range(NEAR)])]
    reduce_scatter x2 -> x0, waiting for transfers between devices: 60.9 us -> none  [the longest x1 36.3 us: per_device(): lax.psum_scatter(tangent_terms.astype(jnp.bfloat16), 'dp', scatter_dimens...]
    pallas_call x0 -> x4, Pallas kernels: none -> 58.7 us  [the longest x3 56.7 us: attend(): pl.pallas_call(functools.partial(attend_kernel, slices, len(blocks), firs...]
    ppermute x0 -> x25, starting transfers between devices: none -> 35.9 us  [the longest x10 14.8 us: shift(): lax.ppermute(array, axis, [(i, (i + by) % NEAR) for i in range(NEAR)])]
  transfers between devices with their start and end apart: 6 -> 25, of which waited for: 6 -> 10; matrix products, arithmetic and copies ran while one was open for 1% -> 5% of each run, Pallas kernels for 0% -> 29%
where the time goes in v1:
time: 201 us
  waiting for transfers between devices  88.1 us (44%)
  Pallas kernels  58.7 us (29%)
  starting transfers between devices  35.9 us (18%)
  local copies, waits for them, and re-layouts  10.6 us (5%)
  matrix products  4.97 us (2%)
    pallas_call x3, Pallas kernels, attend(): pl.pallas_call(functools.partial(attend_kernel, slices, len(blocks), firs...  56.7 us
    ppermute x10, waiting for transfers between devices, shift(): lax.ppermute(array, axis, [(i, (i + by) % NEAR) for i in range(NEAR)])  46.5 us
    ppermute x1, waiting for transfers between devices, per_device(): query = lax.ppermute(pack((queries, query_tangent)), ('co', 'xh'), SWAP)  20.3 us
    ppermute x10, starting transfers between devices, shift(): lax.ppermute(array, axis, [(i, (i + by) % NEAR) for i in range(NEAR)])  14.8 us
    ppermute x1, waiting for transfers between devices, per_device(): back = lax.ppermute(heads, ('co', 'xh'), SWAP)  13.3 us
    ppermute x1, starting transfers between devices, per_device(): back = lax.ppermute(heads, ('co', 'xh'), SWAP)  6.9 us
    ppermute x1, starting transfers between devices, per_device(): lax.ppermute(pack((keys, key_tangent, values, value_tangent)), ('co', 'xh...  6.04 us
    ppermute x10, starting transfers between devices, other(): return lax.ppermute(array, axis, [(0, 1), (1, 0)])  5.01 us
  transfers between devices with their start and end apart: 25, of which 10 were waited for; matrix products, arithmetic and copies ran while one was open for 5% of the time, Pallas kernels for 29%

profile of v1, /device:TPU:1, one launch (start us, length us, event | category | flops | bytes accessed | tf_op | source)
XLA Modules:
  0.0 200.5 jit_solution(14276850335579848495)
XLA Ops:
  0.7 1.4 pad_maximum_fusion
  2.1 6.0 %collective-permute-start = (bf16[1024,640]{1,0:T(8,128)(2,1)S(1)}, bf16[1024,640]{1,0:T(8,128)(2,1)}, u32[]{:S(2)}, u32[]{:S(2)}) collective-permute-start(bf16[1024,640]{1,0:T(8,128)(2,1)S(1)} %pad_maximum_fusion), channel_id=1, source_target_pairs={{0,0},{16,32},{32,16},{48,48},{1,1},{17,33},{33,17},{49,49},{2,2},... | collective-permute-start | bytes 3932168 | tf_op jit(solution)/shard_map/ppermute | solution.py:247
  8.2 1.9 collective-permute-start.1
  10.2 20.3 %collective-permute-done.1.refs_0_ = bf16[512,640]{1,0:T(8,128)(2,1)S(1)} collective-permute-done((bf16[512,640]{1,0:T(8,128)(2,1)S(1)}, bf16[512,640]{1,0:T(8,128)(2,1)S(1)}, u32[]{:S(2)}, u32[]{:S(2)}) %collective-permute-start.1) | collective-permute-done | bytes 655392 | tf_op jit(solution)/shard_map/ppermute | solution.py:250
  30.5 1.3 collective-permute-start.5
  31.8 1.4 collective-permute-start.8
  33.2 1.6 collective-permute-start.2
  34.8 2.1 %collective-permute-start.3 = (bf16[512,640]{1,0:T(8,128)(2,1)S(1)}, bf16[512,640]{1,0:T(8,128)(2,1)}, u32[]{:S(2)}, u32[]{:S(2)}) collective-permute-start(bf16[512,640]{1,0:T(8,128)(2,1)S(1)} %collective-permute-done.1.refs_0_), channel_id=1, source_target_pairs={{0,3},{1,0},{2,1},{3,2},{4,7},{5,4},{6,5},{7,6},{8,11},{9,8},{10,9... | collective-permute-start | bytes 1966088 | tf_op jit(solution)/shard_map/ppermute | solution.py:30
  37.0 11.8 %collective-permute-done.5.refs_4_.refs_8_ = bf16[1024,640]{1,0:T(8,128)(2,1)S(1)} collective-permute-done((bf16[1024,640]{1,0:T(8,128)(2,1)}, bf16[1024,640]{1,0:T(8,128)(2,1)S(1)}, u32[]{:S(2)}, u32[]{:S(2)}) %collective-permute-start.5) | collective-permute-done | bytes 1310752 | tf_op jit(solution)/shard_map/ppermute | solution.py:30
  48.8 3.2 %collective-permute-start.4 = (bf16[512,640]{1,0:T(8,128)(2,1)S(1)}, bf16[512,640]{1,0:T(8,128)(2,1)}, u32[]{:S(2)}, u32[]{:S(2)}) collective-permute-start(bf16[512,640]{1,0:T(8,128)(2,1)S(1)} %collective-permute-done.1.refs_0_), channel_id=1, source_target_pairs={{0,2},{1,3},{2,0},{3,1},{4,6},{5,7},{6,4},{7,5},{8,10},{9,11},{10,... | collective-permute-start | bytes 1966088 | tf_op jit(solution)/shard_map/ppermute | solution.py:30
  52.0 3.9 %fusion.19 = (bf16[320,2560]{1,0:T(8,128)(2,1)}, bf16[320,2560]{1,0:T(8,128)(2,1)}) fusion(bf16[640,5120]{1,0:T(8,128)(2,1)} %param.13, s32[]{:T(128)S(6)} %add.28, s32[]{:T(128)S(6)} %select_n.16), kind=kLoop, calls=%fused_computation.26 | loop fusion | bytes 6553608 | tf_op jit(solution)/shard_map/slice | solution.py:230
  57.0 2.1 %constant_dynamic-slice_fusion.4 = (bf16[640,1280]{1,0:T(8,128)(2,1)S(1)}, bf16[640,1280]{1,0:T(8,128)(2,1)S(1)}) fusion(bf16[640,5120]{1,0:T(8,128)(2,1)} %param.13, s32[]{:T(128)S(6)} %select_n.15, s32[]{:T(128)S(6)} %select_n.18), kind=kLoop, calls=%fused_computation.24 | loop fusion | bytes 6553608 | tf_op jit(solution)/shard_map/dynamic_slice | solution.py:224
  59.3 1.9 collective-permute-start.9
  61.3 6.2 %collective-permute-done.4.refs_3_ = bf16[512,640]{1,0:T(8,128)(2,1)} collective-permute-done((bf16[512,640]{1,0:T(8,128)(2,1)S(1)}, bf16[512,640]{1,0:T(8,128)(2,1)}, u32[]{:S(2)}, u32[]{:S(2)}) %collective-permute-start.4) | collective-permute-done | bytes 655392 | tf_op jit(solution)/shard_map/ppermute | solution.py:30
  68.0 11.3 %shard_map.86 = (f32[4,256,640]{2,1,0:T(8,128)}, f32[4,256,640]{2,1,0:T(8,128)}, f32[4,256,640]{2,1,0:T(8,128)}) custom-call(bf16[512,640]{1,0:T(8,128)(2,1)S(1)} %collective-permute-done.1.refs_0_, bf16[512,640]{1,0:T(8,128)(2,1)} %collective-permute-done.2.refs_1_, bf16[512,640]{1,0:T(8,128)(2,1)} %collective-permute-done.3.refs_2_, ...), custom_call_target="tpu_custom_call" | custom-call | flops 10737418240 | bytes 15728640 | tf_op jit(solution)/shard_map/pallas_call | solution.py:144
  79.3 2.5 %collective-permute-done.21 = bf16[320,2560]{1,0:T(8,128)(2,1)} collective-permute-done((bf16[320,2560]{1,0:T(8,128)(2,1)}, bf16[320,2560]{1,0:T(8,128)(2,1)}, u32[]{:S(2)}, u32[]{:S(2)}) %collective-permute-start.21) | collective-permute-done | bytes 1638432 | tf_op jit(solution)/shard_map/ppermute | solution.py:34
  81.8 1.2 collective-permute-start.22
  83.0 1.5 constant_dynamic-update-slice_fusion.1
  84.6 1.6 collective-permute-start.23
  86.7 22.1 %shard_map.87 = (f32[4,256,640]{2,1,0:T(8,128)}, f32[4,256,640]{2,1,0:T(8,128)}, f32[4,256,640]{2,1,0:T(8,128)}) custom-call(bf16[512,640]{1,0:T(8,128)(2,1)S(1)} %collective-permute-done.1.refs_0_, bf16[512,640]{1,0:T(8,128)(2,1)} %collective-permute-done.2.refs_1_, bf16[512,640]{1,0:T(8,128)(2,1)} %collective-permute-done.3.refs_2_, ...), custom_call_target="tpu_custom_call" | custom-call | flops 21474836480 | bytes 15728640 | tf_op jit(solution)/shard_map/pallas_call | solution.py:144
  108.8 23.2 %shard_map.88 = (bf16[256,1408]{1,0:T(8,128)(2,1)S(1)}, bf16[256,1408]{1,0:T(8,128)(2,1)}, bf16[256,1408]{1,0:T(8,128)(2,1)}, bf16[256,1408]{1,0:T(8,128)(2,1)}) custom-call(bf16[512,640]{1,0:T(8,128)(2,1)S(1)} %collective-permute-done.1.refs_0_, bf16[512,640]{1,0:T(8,128)(2,1)} %collective-permute-done.2.refs_1_, ...), custom_call_target="tpu_custom_call" | custom-call | flops 10737418240 | bytes 15728640 | tf_op jit(solution)/shard_map/pallas_call | solution.py:144
  133.5 1.7 collective-permute-start.16
  135.2 1.5 constant_dynamic-update-slice_fusion
  138.2 11.6 %collective-permute-done.14.refs_1_ = bf16[256,1408]{1,0:T(8,128)(2,1)S(1)} collective-permute-done((bf16[256,1408]{1,0:T(8,128)(2,1)}, bf16[256,1408]{1,0:T(8,128)(2,1)S(1)}, u32[]{:S(2)}, u32[]{:S(2)}) %collective-permute-start.14) | collective-permute-done | bytes 720928 | tf_op jit(solution)/shard_map/ppermute | solution.py:30
  149.7 2.6 %collective-permute-done.15.refs_2_ = bf16[256,1408]{1,0:T(8,128)(2,1)S(1)} collective-permute-done((bf16[256,1408]{1,0:T(8,128)(2,1)}, bf16[256,1408]{1,0:T(8,128)(2,1)S(1)}, u32[]{:S(2)}, u32[]{:S(2)}) %collective-permute-start.15) | collective-permute-done | bytes 720928 | tf_op jit(solution)/shard_map/ppermute | solution.py:30
  152.3 14.3 %collective-permute-done.16.refs_3_ = bf16[256,1408]{1,0:T(8,128)(2,1)S(1)} collective-permute-done((bf16[256,1408]{1,0:T(8,128)(2,1)}, bf16[256,1408]{1,0:T(8,128)(2,1)S(1)}, u32[]{:S(2)}, u32[]{:S(2)}) %collective-permute-start.16) | collective-permute-done | bytes 720928 | tf_op jit(solution)/shard_map/ppermute | solution.py:30
  166.6 2.0 shard_map.89
  168.6 6.9 %collective-permute-start.17 = (bf16[512,640]{1,0:T(8,128)(2,1)S(1)}, bf16[512,640]{1,0:T(8,128)(2,1)S(1)}, u32[]{:S(2)}, u32[]{:S(2)}) collective-permute-start(bf16[512,640]{1,0:T(8,128)(2,1)S(1)} %shard_map.89), channel_id=1, source_target_pairs={{0,0},{16,32},{32,16},{48,48},{1,1},{17,33},{33,17},{49,49},{2,2},... | collective-permute-start | bytes 1966088 | tf_op jit(solution)/shard_map/ppermute | solution.py:256
  175.6 13.3 %collective-permute-done.17 = bf16[512,640]{1,0:T(8,128)(2,1)S(1)} collective-permute-done((bf16[512,640]{1,0:T(8,128)(2,1)S(1)}, bf16[512,640]{1,0:T(8,128)(2,1)S(1)}, u32[]{:S(2)}, u32[]{:S(2)}) %collective-permute-start.17) | collective-permute-done | bytes 655392 | tf_op jit(solution)/shard_map/ppermute | solution.py:256
  188.9 3.5 %collective-permute-done.18 = bf16[512,640]{1,0:T(8,128)(2,1)S(1)} collective-permute-done((bf16[512,640]{1,0:T(8,128)(2,1)S(1)}, bf16[512,640]{1,0:T(8,128)(2,1)S(1)}, u32[]{:S(2)}, u32[]{:S(2)}) %collective-permute-start.18) | collective-permute-done | bytes 655392 | tf_op jit(solution)/shard_map/ppermute | solution.py:257
  192.3 2.1 %collective-permute-done.20 = bf16[512,640]{1,0:T(8,128)(2,1)S(1)} collective-permute-done((bf16[512,640]{1,0:T(8,128)(2,1)S(1)}, bf16[512,640]{1,0:T(8,128)(2,1)S(1)}, u32[]{:S(2)}, u32[]{:S(2)}) %collective-permute-start.20) | collective-permute-done | bytes 655392 | tf_op jit(solution)/shard_map/ppermute | solution.py:34
  194.4 5.0 %fusion.8 = bf16[512,1280]{1,0:T(8,128)(2,1)S(1)} fusion(bf16[640,1280]{1,0:T(8,128)(2,1)S(1)} %collective-permute-done.24, bf16[640,1280]{1,0:T(8,128)(2,1)} %collective-permute-done.23, bf16[640,1280]{1,0:T(8,128)(2,1)S(1)} %get-tuple-element.32, bf16[640,1280]{1,0:T(8,128)(2,1)S(1)} %get-tuple-element.28, ...), kind=kOutput, calls=%fused_computation.8 | convolution fusion | flops 3392798720 | bytes 10485760 | tf_op jit(solution)/shard_map/dot_general | solution.py:262
  (39 shorter events, 6.5 us)
Async XLA Ops:
  0.6 7.5 %copy-start.1 = (bf16[256,640]{1,0:T(8,128)(2,1)S(1)}, bf16[256,640]{1,0:T(8,128)(2,1)}, u32[]{:S(2)}) copy-start(bf16[256,640]{1,0:T(8,128)(2,1)} %param.10) | copy-start | bytes 983044
  0.6 7.5 %copy-start.2 = (bf16[256,640]{1,0:T(8,128)(2,1)S(1)}, bf16[256,640]{1,0:T(8,128)(2,1)}, u32[]{:S(2)}) copy-start(bf16[256,640]{1,0:T(8,128)(2,1)} %param.7) | copy-start | bytes 983044
  2.1 28.4 %collective-permute-start = (bf16[1024,640]{1,0:T(8,128)(2,1)S(1)}, bf16[1024,640]{1,0:T(8,128)(2,1)}, u32[]{:S(2)}, u32[]{:S(2)}) collective-permute-start(bf16[1024,640]{1,0:T(8,128)(2,1)S(1)} %pad_maximum_fusion), channel_id=1, source_target_pairs={{0,0},{16,32},{32,16},{48,48},{1,1},{17,33},{33,17},{49,49},{2,2},... | collective-permute-start | bytes 3932168 | tf_op jit(solution)/shard_map/ppermute | solution.py:247
  8.2 22.2 %collective-permute-start.1 = (bf16[512,640]{1,0:T(8,128)(2,1)S(1)}, bf16[512,640]{1,0:T(8,128)(2,1)S(1)}, u32[]{:S(2)}, u32[]{:S(2)}) collective-permute-start(bf16[512,640]{1,0:T(8,128)(2,1)S(1)} %pad_maximum_fusion.1), channel_id=1, source_target_pairs={{0,0},{16,32},{32,16},{48,48},{1,1},{17,33},{33,17},{49,49},{2,2},... | collective-permute-start | bytes 1966088 | tf_op jit(solution)/shard_map/ppermute | solution.py:250
  30.5 18.3 %collective-permute-start.5 = (bf16[1024,640]{1,0:T(8,128)(2,1)}, bf16[1024,640]{1,0:T(8,128)(2,1)S(1)}, u32[]{:S(2)}, u32[]{:S(2)}) collective-permute-start(bf16[1024,640]{1,0:T(8,128)(2,1)} %collective-permute-done.refs_4_.refs_6_), channel_id=1, source_target_pairs={{0,4},{4,8},{8,12},{12,0},{1,5},{5,9},{9,13},{13,1},{2,6},{6,10},{... | collective-permute-start | bytes 3932168 | tf_op jit(solution)/shard_map/ppermute | solution.py:30
  31.8 24.1 %collective-permute-start.8 = (bf16[1024,640]{1,0:T(8,128)(2,1)}, bf16[1024,640]{1,0:T(8,128)(2,1)S(1)}, u32[]{:S(2)}, u32[]{:S(2)}) collective-permute-start(bf16[1024,640]{1,0:T(8,128)(2,1)} %collective-permute-done.refs_4_.refs_6_), channel_id=1, source_target_pairs={{0,12},{4,0},{8,4},{12,8},{1,13},{5,1},{9,5},{13,9},{2,14},{6,2},{... | collective-permute-start | bytes 3932168 | tf_op jit(solution)/shard_map/ppermute | solution.py:30
  33.2 34.8 %collective-permute-start.13 = (bf16[1024,640]{1,0:T(8,128)(2,1)}, bf16[1024,640]{1,0:T(8,128)(2,1)}, u32[]{:S(2)}, u32[]{:S(2)}) collective-permute-start(bf16[1024,640]{1,0:T(8,128)(2,1)} %collective-permute-done.refs_4_.refs_6_), channel_id=1, source_target_pairs={{0,32},{32,0},{1,33},{33,1},{2,34},{34,2},{3,35},{35,3},{4,36},{36... | collective-permute-start | bytes 3932168 | tf_op jit(solution)/shard_map/ppermute | solution.py:34
  33.2 26.1 %collective-permute-start.2 = (bf16[512,640]{1,0:T(8,128)(2,1)S(1)}, bf16[512,640]{1,0:T(8,128)(2,1)}, u32[]{:S(2)}, u32[]{:S(2)}) collective-permute-start(bf16[512,640]{1,0:T(8,128)(2,1)S(1)} %collective-permute-done.1.refs_0_), channel_id=1, source_target_pairs={{0,1},{1,2},{2,3},{3,0},{4,5},{5,6},{6,7},{7,4},{8,9},{9,10},{10,1... | collective-permute-start | bytes 1966088 | tf_op jit(solution)/shard_map/ppermute | solution.py:30
  34.8 26.4 %collective-permute-start.3 = (bf16[512,640]{1,0:T(8,128)(2,1)S(1)}, bf16[512,640]{1,0:T(8,128)(2,1)}, u32[]{:S(2)}, u32[]{:S(2)}) collective-permute-start(bf16[512,640]{1,0:T(8,128)(2,1)S(1)} %collective-permute-done.1.refs_0_), channel_id=1, source_target_pairs={{0,3},{1,0},{2,1},{3,2},{4,7},{5,4},{6,5},{7,6},{8,11},{9,8},{10,9... | collective-permute-start | bytes 1966088 | tf_op jit(solution)/shard_map/ppermute | solution.py:30
  48.8 18.7 %collective-permute-start.4 = (bf16[512,640]{1,0:T(8,128)(2,1)S(1)}, bf16[512,640]{1,0:T(8,128)(2,1)}, u32[]{:S(2)}, u32[]{:S(2)}) collective-permute-start(bf16[512,640]{1,0:T(8,128)(2,1)S(1)} %collective-permute-done.1.refs_0_), channel_id=1, source_target_pairs={{0,2},{1,3},{2,0},{3,1},{4,6},{5,7},{6,4},{7,5},{8,10},{9,11},{10,... | collective-permute-start | bytes 1966088 | tf_op jit(solution)/shard_map/ppermute | solution.py:30
  55.9 25.9 %collective-permute-start.21 = (bf16[320,2560]{1,0:T(8,128)(2,1)}, bf16[320,2560]{1,0:T(8,128)(2,1)}, u32[]{:S(2)}, u32[]{:S(2)}) collective-permute-start(bf16[320,2560]{1,0:T(8,128)(2,1)} %get-tuple-element.31), channel_id=1, source_target_pairs={{0,64},{64,0},{1,65},{65,1},{2,66},{66,2},{3,67},{67,3},{4,68},{68... | collective-permute-start | bytes 4915208 | tf_op jit(solution)/shard_map/ppermute | solution.py:34
  59.3 22.5 %copy-start = (bf16[320,2560]{1,0:T(8,128)(2,1)S(1)}, bf16[320,2560]{1,0:T(8,128)(2,1)}, u32[]{:S(2)}) copy-start(bf16[320,2560]{1,0:T(8,128)(2,1)} %get-tuple-element.30) | copy-start | bytes 4915204
  59.3 25.2 %collective-permute-start.9 = (bf16[512,640]{1,0:T(8,128)(2,1)S(1)}, bf16[512,640]{1,0:T(8,128)(2,1)S(1)}, u32[]{:S(2)}, u32[]{:S(2)}) collective-permute-start(bf16[512,640]{1,0:T(8,128)(2,1)S(1)} %slice.25), channel_id=1, source_target_pairs={{0,12},{4,0},{8,4},{12,8},{1,13},{5,1},{9,5},{13,9},{2,14},{6,2},{... | collective-permute-start | bytes 1966088 | tf_op jit(solution)/shard_map/ppermute | solution.py:30
  61.3 24.9 %collective-permute-start.6 = (bf16[512,640]{1,0:T(8,128)(2,1)S(1)}, bf16[512,640]{1,0:T(8,128)(2,1)S(1)}, u32[]{:S(2)}, u32[]{:S(2)}) collective-permute-start(bf16[512,640]{1,0:T(8,128)(2,1)S(1)} %slice.24), channel_id=1, source_target_pairs={{0,4},{4,8},{8,12},{12,0},{1,5},{5,9},{9,13},{13,1},{2,6},{6,10},{... | collective-permute-start | bytes 1966088 | tf_op jit(solution)/shard_map/ppermute | solution.py:30
  67.5 18.9 %collective-permute-start.11 = (bf16[1024,640]{1,0:T(8,128)(2,1)S(1)}, bf16[1024,640]{1,0:T(8,128)(2,1)}, u32[]{:S(2)}, u32[]{:S(2)}) collective-permute-start(bf16[1024,640]{1,0:T(8,128)(2,1)S(1)} %collective-permute-done.5.refs_4_.refs_8_), channel_id=1, source_target_pairs={{0,32},{32,0},{1,33},{33,1},{2,34},{34,2},{3,35},{35,3},{4,36},{36... | collective-permute-start | bytes 3932168 | tf_op jit(solution)/shard_map/ppermute | solution.py:34
  68.0 18.7 %collective-permute-start.12 = (bf16[1024,640]{1,0:T(8,128)(2,1)S(1)}, bf16[1024,640]{1,0:T(8,128)(2,1)}, u32[]{:S(2)}, u32[]{:S(2)}) collective-permute-start(bf16[1024,640]{1,0:T(8,128)(2,1)S(1)} %collective-permute-done.8.refs_5_.refs_9_), channel_id=1, source_target_pairs={{0,32},{32,0},{1,33},{33,1},{2,34},{34,2},{3,35},{35,3},{4,36},{36... | collective-permute-start | bytes 3932168 | tf_op jit(solution)/shard_map/ppermute | solution.py:34
  81.8 53.4 %collective-permute-start.22 = (bf16[320,2560]{1,0:T(8,128)(2,1)S(1)}, bf16[320,2560]{1,0:T(8,128)(2,1)}, u32[]{:S(2)}, u32[]{:S(2)}) collective-permute-start(bf16[320,2560]{1,0:T(8,128)(2,1)S(1)} %copy-done), channel_id=1, source_target_pairs={{0,80},{16,64},{64,16},{80,0},{1,81},{17,65},{65,17},{81,1},{2,82}... | collective-permute-start | bytes 4915208 | tf_op jit(solution)/shard_map/ppermute | solution.py:230
  84.6 107.8 %collective-permute-start.23 = (bf16[640,1280]{1,0:T(8,128)(2,1)S(1)}, bf16[640,1280]{1,0:T(8,128)(2,1)}, u32[]{:S(2)}, u32[]{:S(2)}) collective-permute-start(bf16[640,1280]{1,0:T(8,128)(2,1)S(1)} %get-tuple-element.29), channel_id=1, source_target_pairs={{0,32},{32,0},{1,33},{33,1},{2,34},{34,2},{3,35},{35,3},{4,36},{36... | collective-permute-start | bytes 4915208 | tf_op jit(solution)/shard_map/ppermute | solution.py:34
  86.2 22.6 %collective-permute-start.10 = (bf16[512,640]{1,0:T(8,128)(2,1)S(1)}, bf16[512,640]{1,0:T(8,128)(2,1)S(1)}, u32[]{:S(2)}, u32[]{:S(2)}) collective-permute-start(bf16[512,640]{1,0:T(8,128)(2,1)S(1)} %collective-permute-done.9.refs_6_), channel_id=1, source_target_pairs={{0,32},{32,0},{1,33},{33,1},{2,34},{34,2},{3,35},{35,3},{4,36},{36... | collective-permute-start | bytes 1966088 | tf_op jit(solution)/shard_map/ppermute | solution.py:34
  86.3 22.5 %collective-permute-start.7 = (bf16[512,640]{1,0:T(8,128)(2,1)S(1)}, bf16[512,640]{1,0:T(8,128)(2,1)S(1)}, u32[]{:S(2)}, u32[]{:S(2)}) collective-permute-start(bf16[512,640]{1,0:T(8,128)(2,1)S(1)} %collective-permute-done.6.refs_4_), channel_id=1, source_target_pairs={{0,32},{32,0},{1,33},{33,1},{2,34},{34,2},{3,35},{35,3},{4,36},{36... | collective-permute-start | bytes 1966088 | tf_op jit(solution)/shard_map/ppermute | solution.py:34
  132.1 17.7 %collective-permute-start.14 = (bf16[256,1408]{1,0:T(8,128)(2,1)}, bf16[256,1408]{1,0:T(8,128)(2,1)S(1)}, u32[]{:S(2)}, u32[]{:S(2)}) collective-permute-start(bf16[256,1408]{1,0:T(8,128)(2,1)} %get-tuple-element.24), channel_id=1, source_target_pairs={{0,3},{1,0},{2,1},{3,2},{4,7},{5,4},{6,5},{7,6},{8,11},{9,8},{10,9... | collective-permute-start | bytes 2162696 | tf_op jit(solution)/shard_map/ppermute | solution.py:30
  133.2 19.2 %collective-permute-start.15 = (bf16[256,1408]{1,0:T(8,128)(2,1)}, bf16[256,1408]{1,0:T(8,128)(2,1)S(1)}, u32[]{:S(2)}, u32[]{:S(2)}) collective-permute-start(bf16[256,1408]{1,0:T(8,128)(2,1)} %get-tuple-element.25), channel_id=1, source_target_pairs={{0,1},{1,2},{2,3},{3,0},{4,5},{5,6},{6,7},{7,4},{8,9},{9,10},{10,1... | collective-permute-start | bytes 2162696 | tf_op jit(solution)/shard_map/ppermute | solution.py:30
  133.5 33.1 %collective-permute-start.16 = (bf16[256,1408]{1,0:T(8,128)(2,1)}, bf16[256,1408]{1,0:T(8,128)(2,1)S(1)}, u32[]{:S(2)}, u32[]{:S(2)}) collective-permute-start(bf16[256,1408]{1,0:T(8,128)(2,1)} %get-tuple-element.26), channel_id=1, source_target_pairs={{0,2},{1,3},{2,0},{3,1},{4,6},{5,7},{6,4},{7,5},{8,10},{9,11},{10,... | collective-permute-start | bytes 2162696 | tf_op jit(solution)/shard_map/ppermute | solution.py:30
  137.0 55.4 %collective-permute-start.24 = (bf16[640,1280]{1,0:T(8,128)(2,1)S(1)}, bf16[640,1280]{1,0:T(8,128)(2,1)S(1)}, u32[]{:S(2)}, u32[]{:S(2)}) collective-permute-start(bf16[640,1280]{1,0:T(8,128)(2,1)S(1)} %get-tuple-element.33), channel_id=1, source_target_pairs={{0,32},{32,0},{1,33},{33,1},{2,34},{34,2},{3,35},{35,3},{4,36},{36... | collective-permute-start | bytes 4915208 | tf_op jit(solution)/shard_map/ppermute | solution.py:34
  168.6 20.3 %collective-permute-start.17 = (bf16[512,640]{1,0:T(8,128)(2,1)S(1)}, bf16[512,640]{1,0:T(8,128)(2,1)S(1)}, u32[]{:S(2)}, u32[]{:S(2)}) collective-permute-start(bf16[512,640]{1,0:T(8,128)(2,1)S(1)} %shard_map.89), channel_id=1, source_target_pairs={{0,0},{16,32},{32,16},{48,48},{1,1},{17,33},{33,17},{49,49},{2,2},... | collective-permute-start | bytes 1966088 | tf_op jit(solution)/shard_map/ppermute | solution.py:256
  175.5 16.8 %collective-permute-start.18 = (bf16[512,640]{1,0:T(8,128)(2,1)S(1)}, bf16[512,640]{1,0:T(8,128)(2,1)S(1)}, u32[]{:S(2)}, u32[]{:S(2)}) collective-permute-start(bf16[512,640]{1,0:T(8,128)(2,1)S(1)} %shard_map.89), channel_id=1, source_target_pairs={{0,64},{16,96},{32,80},{48,112},{64,0},{80,32},{96,16},{112,48},{1... | collective-permute-start | bytes 1966088 | tf_op jit(solution)/shard_map/ppermute | solution.py:257
  188.8 3.5 %collective-permute-start.19 = (bf16[512,640]{1,0:T(8,128)(2,1)S(1)}, bf16[512,640]{1,0:T(8,128)(2,1)S(1)}, u32[]{:S(2)}, u32[]{:S(2)}) collective-permute-start(bf16[512,640]{1,0:T(8,128)(2,1)S(1)} %collective-permute-done.17), channel_id=1, source_target_pairs={{0,32},{32,0},{1,33},{33,1},{2,34},{34,2},{3,35},{35,3},{4,36},{36... | collective-permute-start | bytes 1966088 | tf_op jit(solution)/shard_map/ppermute | solution.py:34
  192.3 2.1 %collective-permute-start.20 = (bf16[512,640]{1,0:T(8,128)(2,1)S(1)}, bf16[512,640]{1,0:T(8,128)(2,1)S(1)}, u32[]{:S(2)}, u32[]{:S(2)}) collective-permute-start(bf16[512,640]{1,0:T(8,128)(2,1)S(1)} %collective-permute-done.18), channel_id=1, source_target_pairs={{0,32},{32,0},{1,33},{33,1},{2,34},{34,2},{3,35},{35,3},{4,36},{36... | collective-permute-start | bytes 1966088 | tf_op jit(solution)/shard_map/ppermute | solution.py:34

commit v2 on v0

v2 whole, which is shorter than its diff:
```python
import functools
import math

import jax
import jax.numpy as jnp
from jax import lax
from jax.experimental import pallas as pl
from jax.experimental.pallas import tpu as pltpu
from jax.sharding import Mesh, PartitionSpec as P

DH = 128
ROWS = 256
SCALE = 1.0 / DH**0.5
LOG2_SCALE = SCALE * math.log2(math.e)
NEAR = 4
STAT_LANES = 32
VMEM = 60 * 2**20
SHORT = pl.CostEstimate(flops=1, bytes_accessed=1, transcendentals=0)
DIAGONAL = ((0, 3), (1, 2), (2, 1), (3, 0))
PAIR = 2 * DH
HELD = 3


def shift(array, axis, by):
    return lax.ppermute(array, axis, [(i, (i + by) % NEAR) for i in range(NEAR)])


def other(array, axis):
    return lax.ppermute(array, axis, [(0, 1), (1, 0)])


def after(value, *others):
    return lax.optimization_barrier((value, others))[0]


def dot_t(a, b):
    return lax.dot_general(a, b, (((1,), (1,)), ((), ())), preferred_element_type=jnp.float32)


def slice_scores(queries, keys):
    query, dquery = queries[0:ROWS], queries[ROWS : 2 * ROWS]
    return dot_t(query, keys[:, :DH]), dot_t(jnp.concatenate([dquery, query], axis=1), keys)


def slice_weights(scores, slope_scores):
    new_max = jnp.max(scores, axis=1, keepdims=True)
    expo = jnp.exp2(scores * LOG2_SCALE - new_max * LOG2_SCALE)
    weighted = expo * slope_scores
    total = jnp.sum(expo, axis=1, keepdims=True)
    return new_max, total, expo.astype(jnp.bfloat16), weighted.astype(jnp.bfloat16)


def slice_sums(weights, values, values_one):
    new_max, total, expo, weighted = weights
    primal = jnp.dot(expo, values, preferred_element_type=jnp.float32)
    tangent = jnp.dot(weighted, values_one, preferred_element_type=jnp.float32) * SCALE
    return new_max, total, tangent[:, DH : DH + 1], primal[:, :DH], primal[:, DH:] + tangent[:, :DH]


def three_parts(value):
    high = value.astype(jnp.bfloat16).astype(jnp.float32)
    rest = value - high
    middle = rest.astype(jnp.bfloat16).astype(jnp.float32)
    low = rest - middle
    return high + pltpu.roll(middle, STAT_LANES, 1) + pltpu.roll(low, 2 * STAT_LANES, 1)


def from_three(parts):
    return (
        parts
        + pltpu.roll(parts, DH - STAT_LANES, 1)
        + pltpu.roll(parts, DH - 2 * STAT_LANES, 1)
    )


def attend_kernel(slices, blocks, heads, above, *refs):
    queries = refs[:slices]
    key_refs = refs[slices : slices + blocks]
    value_refs = refs[slices + blocks : slices + 2 * blocks]
    outs = refs[-slices:]
    head = pl.program_id(0)
    if above:
        for out, earlier in zip(outs, refs[slices + 2 * blocks : -slices]):
            out[0:above, :] = earlier[...]
    lane = lax.broadcasted_iota(jnp.int32, (ROWS, DH), 1)

    def pairs(parts):
        return jnp.concatenate([jnp.concatenate(p, axis=1) for p in parts], axis=0)

    keys = pairs([(k[0:ROWS], k[ROWS : 2 * ROWS]) for k in key_refs])
    values = pairs([(v[0:ROWS], v[ROWS : 2 * ROWS]) for v in value_refs])
    ones = jnp.ones((ROWS, DH), jnp.bfloat16)
    values_one = pairs([(v[0:ROWS], ones) for v in value_refs])

    def finish(i, weights):
        new_max, total, slope, acc, acc_tangent = slice_sums(weights, values, values_one)
        inverse = 1.0 / total
        mean = slope * inverse
        out = acc * inverse
        at = pl.multiple_of(above + head * 2 * ROWS, ROWS)
        outs[i][pl.ds(at, ROWS), :] = out.astype(jnp.bfloat16)
        outs[i][pl.ds(at + ROWS, ROWS), :] = (acc_tangent * inverse - mean * out).astype(jnp.bfloat16)
        tail = slice(above + 2 * heads * ROWS, above + (2 * heads + 1) * ROWS)
        stats = jnp.where(lane == 2 * head, new_max * LOG2_SCALE + jnp.log2(total), 0.0)
        stats = three_parts(jnp.where(lane == 2 * head + 1, mean, stats))
        before = jnp.where(head == 0, 0.0, outs[i][tail, :].astype(jnp.float32))
        outs[i][tail, :] = (before + stats).astype(jnp.bfloat16)

    scores = slice_scores(queries[0][...], keys)
    held = None
    for i in range(slices):
        following = slice_scores(queries[i + 1][...], keys) if i + 1 < slices else None
        weights = slice_weights(*scores)
        if i > 0:
            finish(i - 1, held)
        held, scores = weights, following
    finish(slices - 1, held)


def attend(queries, blocks, first, heads, earlier=()):
    slices = len(queries)
    query_spec = pl.BlockSpec((2 * ROWS, DH), lambda h: (first + h, 0))
    halved = [isinstance(b, tuple) for b in blocks]
    key_spec = pl.BlockSpec((2 * ROWS, DH), lambda h: (first + h, 0))
    value_specs = [pl.BlockSpec((2 * ROWS, DH), lambda h, w=w: (first + h if w else HELD + first + h, 0)) for w in halved]
    keys = [b[0] if w else b for b, w in zip(blocks, halved)]
    values = [b[1] if w else b for b, w in zip(blocks, halved)]
    above = earlier[0].shape[0] if earlier else 0
    part_type = jax.ShapeDtypeStruct((above + (2 * heads + 1) * ROWS, DH), jnp.bfloat16)
    part_spec = pl.BlockSpec(part_type.shape, lambda h: (0, 0))
    earlier_specs = [pl.BlockSpec(e.shape, lambda h: (0, 0)) for e in earlier]
    return pl.pallas_call(
        functools.partial(attend_kernel, slices, len(blocks), heads, above),
        grid=(heads,),
        in_specs=[query_spec] * slices + [key_spec] * len(blocks) + value_specs + earlier_specs,
        out_specs=[part_spec] * slices,
        out_shape=[part_type] * slices,
        compiler_params=pltpu.CompilerParams(vmem_limit_bytes=VMEM),
        cost_estimate=pl.CostEstimate(
            flops=slices * len(blocks) * heads * 16 * ROWS**3,
            bytes_accessed=(len(blocks) * 4 + slices * 6) * heads * ROWS * DH * 2,
            transcendentals=slices * len(blocks) * heads * ROWS**2,
        ),
    )(*queries, *keys, *values, *earlier)


def combine_kernel(heads, *refs):
    row = column = 0
    for count in heads:
        rows = (2 * count + 1) * ROWS
        combine_group(count, [r.at[row : row + rows] for r in refs[:-1]], refs[-1], column)
        row, column = row + rows, column + count


def combine_group(heads, parts, out_ref, base):
    stats = [from_three(p[2 * heads * ROWS :, :].astype(jnp.float32)) for p in parts]
    top = functools.reduce(jnp.maximum, stats)
    shares = [jnp.exp2(x - top) for x in stats]
    whole = 1.0 / functools.reduce(jnp.add, shares)
    shares = [s * whole for s in shares]
    means = [pltpu.roll(x, DH - 1, 1) for x in stats]
    mean = functools.reduce(jnp.add, [s * m for s, m in zip(shares, means)])
    shifts = [s * (m - mean) for s, m in zip(shares, means)]
    for h in range(heads):
        out = tangent = 0.0
        for part, share, shift_by in zip(parts, shares, shifts):
            o = part[2 * h * ROWS : (2 * h + 1) * ROWS, :].astype(jnp.float32)
            t = part[(2 * h + 1) * ROWS : (2 * h + 2) * ROWS, :].astype(jnp.float32)
            own = share[:, 2 * h : 2 * h + 1]
            out = out + own * o
            tangent = tangent + own * t + shift_by[:, 2 * h : 2 * h + 1] * o
        columns = slice((base + h) * DH, (base + h + 1) * DH)
        out_ref[0:ROWS, columns] = out.astype(jnp.bfloat16)
        out_ref[ROWS : 2 * ROWS, columns] = tangent.astype(jnp.bfloat16)


def combine(parts, heads):
    return pl.pallas_call(
        functools.partial(combine_kernel, heads),
        out_shape=jax.ShapeDtypeStruct((2 * ROWS, sum(heads) * DH), jnp.bfloat16),
        compiler_params=pltpu.CompilerParams(vmem_limit_bytes=VMEM),
        cost_estimate=SHORT,
    )(*parts)


def ring(array, axis):
    ahead, behind = shift(array, axis, 1), shift(array, axis, -1)
    middle = array.shape[0] // 2
    far = shift(ahead[:middle], axis, 1), shift(behind[middle:], axis, -1)
    return [array, ahead, behind, far]


def in_turn(array, axis, beside=()):
    found = [array]
    for by in (1, -1, 2):
        found.append(shift(after(array, found[-1], beside) if by != 1 else array, axis, by))
    return found


def give_back(parts, axis):
    return [parts[0]] + [shift(p, axis, -by) for p, by in zip(parts[1:], (1, -1, 2))]


def project_kernel(terms, pieces, weights, last, at_ref, *refs):
    lhs_refs, weight_refs, rest = refs[:pieces], refs[pieces : pieces + weights], refs[pieces + weights :]
    starts = {
        "kept": (at_ref[0] * PAIR, PAIR),
        "back": ((1 - at_ref[0]) * PAIR, PAIR),
        "fifth": (2 * PAIR, DH),
    }
    lhs, rhs = [], []
    for piece, column, weight, which in terms:
        start, count = starts[which]
        lhs.append(lhs_refs[piece][:, column : column + count])
        rhs.append(weight_refs[weight][pl.ds(pl.multiple_of(start, DH), count), :])
    both = jnp.dot(
        jnp.concatenate(lhs, axis=1),
        jnp.concatenate(rhs, axis=0),
        preferred_element_type=jnp.float32,
    )
    if not last:
        rest[0][...] = both
        return
    both = (both + rest[0][...]).astype(jnp.bfloat16)
    rest[1][...] = both[:ROWS]
    rest[2][...] = both[ROWS:]


def project(terms, pieces, weights, places, sums=None):
    tile = 2 * DH
    columns = min(w.shape[1] for w in weights)
    full = lambda a: pl.BlockSpec(a.shape, lambda j, at: (0, 0))

    def weight_spec(w):
        wide = w.shape[1] > columns
        return pl.BlockSpec((w.shape[0], tile), lambda j, at: (0, at[1] + j if wide else j))

    sum_spec = pl.BlockSpec((2 * ROWS, tile), lambda j, at: (0, j))
    out_spec = pl.BlockSpec((ROWS, tile), lambda j, at: (0, j))
    last = sums is not None
    out_type = jax.ShapeDtypeStruct((ROWS, columns), jnp.bfloat16)
    sum_type = jax.ShapeDtypeStruct((2 * ROWS, columns), jnp.float32)
    return pl.pallas_call(
        functools.partial(project_kernel, terms, len(pieces), len(weights), last),
        grid_spec=pltpu.PrefetchScalarGridSpec(
            num_scalar_prefetch=1,
            grid=(columns // tile,),
            in_specs=[full(a) for a in pieces]
            + [weight_spec(w) for w in weights]
            + ([sum_spec] if last else []),
            out_specs=[out_spec] * 2 if last else sum_spec,
        ),
        out_shape=[out_type] * 2 if last else sum_type,
        compiler_params=pltpu.CompilerParams(vmem_limit_bytes=VMEM),
        cost_estimate=SHORT,
    )(places, *pieces, *weights, *([sums] if last else []))


def weight_slices(out_weight):
    xl, co = lax.axis_index("xl"), lax.axis_index("co")
    width = out_weight.shape[1] // 4
    return [
        lax.dynamic_slice_in_dim(out_weight, at * width, width, axis=1)
        for at in ((1 - xl) * 2 + co, (1 - xl) * 2 + 1 - co, xl * 2 + 1 - co)
    ]


def pack_kernel(at_ref, *refs):
    keys, key_tangent, values, value_tangent, queries, query_tangent = refs[:6]
    for start, key_out, query_out in (
        ((1 - at_ref[0]) * PAIR, refs[6], refs[7]),
        (at_ref[0] * PAIR, refs[8], refs[9]),
    ):
        for h in range(HELD):
            at = 2 * PAIR if h == 2 else pl.multiple_of(start + h * DH, DH)
            for k, array in enumerate((keys, key_tangent, values, value_tangent)):
                row = (k // 2 * 2 * HELD + h * 2 + k % 2) * ROWS
                key_out[row : row + ROWS, :] = array[:, pl.ds(at, DH)]
            for k, array in enumerate((queries, query_tangent)):
                row = (h * 2 + k) * ROWS
                if row < query_out.shape[0]:
                    query_out[row : row + ROWS, :] = array[:, pl.ds(at, DH)]


def pack(arrays, at):
    full = lambda rows, columns: pl.BlockSpec((rows, columns), lambda i, at: (0, 0))
    shapes = [(4 * HELD * ROWS, DH), (4 * ROWS, DH), (4 * HELD * ROWS, DH), (2 * HELD * ROWS, DH)]
    return pl.pallas_call(
        pack_kernel,
        grid_spec=pltpu.PrefetchScalarGridSpec(
            num_scalar_prefetch=1,
            grid=(1,),
            in_specs=[full(*a.shape) for a in arrays],
            out_specs=[full(*shape) for shape in shapes],
        ),
        out_shape=[jax.ShapeDtypeStruct(shape, jnp.bfloat16) for shape in shapes],
        compiler_params=pltpu.CompilerParams(vmem_limit_bytes=VMEM),
        cost_estimate=SHORT,
    )(at, *arrays)


def per_device(queries, keys, values, query_tangent, key_tangent, value_tangent, out_weight):
    xl, co, xh = lax.axis_index("xl"), lax.axis_index("co"), lax.axis_index("xh")
    arrays = (keys, key_tangent, values, value_tangent, queries, query_tangent)
    keys_away, query_away, keys_own, query_own = pack(arrays, xh.reshape(1))
    query_in = other(query_away, "xh")
    keys_in = other(after(keys_away, query_in), "xh")
    keys_own = ring(keys_own, "y")
    mine, theirs, beside = weight_slices(out_weight)
    query_own = in_turn(query_own, "z", (mine, theirs, beside, query_in))
    mine, theirs = after((mine, theirs), keys_in)
    keys_in = ring(after(keys_in, keys_own), "y")
    query_in = after(query_in, query_own)
    query_in = [query_in, shift(query_in, "z", 1), shift(query_in, "z", -1)]
    query_in.append(shift(after(query_in[0], query_in), "z", 2))
    mine, theirs = other(mine, "xl"), lax.ppermute(theirs, ("xl", "xh"), DIAGONAL)

    blocks = keys_own + keys_in
    in_parts = attend(query_in, blocks, 0, 2)
    pair_parts = attend(after(query_own, in_parts), blocks, 0, 2)
    in_back = give_back(in_parts, "z")
    own_parts = attend(after(query_own, pair_parts, in_back), blocks, 2, 1, pair_parts)
    own_back = give_back(own_parts, "z")
    weights = [out_weight, mine]
    weights += [other(a, "co") for a in after((beside, theirs), own_parts)]
    heads_in = combine(after(in_back, weights), (2,))
    heads_own = combine(own_back, (2, 1))
    returned = other(heads_in, "xh")
    returned_far = lax.ppermute(heads_in, ("xl", "xh"), DIAGONAL)
    early = other(jnp.concatenate([returned, returned_far], axis=1), "co")
    beside_own = other(heads_own, "co")
    own_far = other(heads_own, "xl")
    far_beside = lax.ppermute(heads_own, ("xl", "co"), DIAGONAL)
    tiles = out_weight.shape[1] // (8 * DH)
    places = jnp.stack([xh, (xl * 2 + co) * tiles]).astype(jnp.int32)
    sums = project(
        (
            (0, 0, 0, "kept"),
            (1, 0, 0, "back"),
            (0, PAIR, 0, "fifth"),
            (2, 0, 1, "back"),
            (4, 0, 2, "kept"),
            (3, 0, 2, "back"),
            (4, PAIR, 2, "fifth"),
            (3, PAIR, 3, "back"),
        ),
        (heads_own, returned, returned_far, early, beside_own),
        weights,
        places,
    )
    return project(
        ((0, 0, 0, "kept"), (0, PAIR, 0, "fifth"), (1, 0, 1, "kept"), (1, PAIR, 1, "fifth")),
        (own_far, far_beside),
        (weights[1], weights[3]),
        places,
        sums,
    )


def solution(mesh):
    split = Mesh(mesh.devices.reshape(2, 2, 2, NEAR, NEAR), ("xl", "co", "xh", "y", "z"))
    tokens, features = ("xh", "y", "z"), ("xl", "co")
    block = P(tokens, features)
    return jax.shard_map(
        per_device,
        mesh=split,
        in_specs=(block,) * 6 + (P(features, None),),
        out_specs=(block, block),
        check_vma=False,
    )
```

time: 989 us -> 180 us (0.18)
  waiting for transfers between devices: 536 us -> 52.5 us
  matrix products: 256 us -> 0 us
  local copies, waits for them, and re-layouts: 169 us -> 7.65 us
  Pallas kernels: 0 us -> 61.2 us
  starting transfers between devices: 0.23 us -> 55.9 us
  between operations: 14.2 us -> 0.87 us
    all_gather x4 -> x0, waiting for transfers between devices: 472 us -> none  [the longest x1 118 us: per_device(): lax.all_gather(values, 'tm', axis=0, tiled=True)]
    dot_general x98 -> x0, matrix products: 256 us -> none  [the longest x16 62.5 us: block_sums(): jnp.einsum('qhd,khd->hqk', query_heads, dkey_heads, preferred_element_typ...]
    dynamic_slice x96 -> x1, local copies, waits for them, and re-layouts: 157 us -> 4.46 us  [weight_slices(): lax.dynamic_slice_in_dim(out_weight, at * width, width, axis=1)]
    pallas_call x0 -> x8, Pallas kernels: none -> 61.2 us  [the longest x3 35.8 us: attend(): pl.pallas_call(functools.partial(attend_kernel, slices, len(blocks), head...]
    reduce_scatter x2 -> x0, waiting for transfers between devices: 60.9 us -> none  [the longest x1 36.3 us: per_device(): lax.psum_scatter(tangent_terms.astype(jnp.bfloat16), 'dp', scatter_dimens...]
    ppermute x0 -> x32, starting transfers between devices: none -> 55.9 us  [the longest x20 30.2 us: shift(): lax.ppermute(array, axis, [(i, (i + by) % NEAR) for i in range(NEAR)])]
    ppermute x0 -> x32, waiting for transfers between devices: none -> 52.5 us  [the longest x20 26 us: shift(): lax.ppermute(array, axis, [(i, (i + by) % NEAR) for i in range(NEAR)])]
  transfers between devices with their start and end apart: 6 -> 32, of which waited for: 6 -> 13; matrix products, arithmetic and copies ran while one was open for 1% -> 3% of each run, Pallas kernels for 0% -> 28%
where the time goes in v2:
time: 180 us
  Pallas kernels  61.2 us (34%)
  starting transfers between devices  55.9 us (31%)
  waiting for transfers between devices  52.5 us (29%)
  local copies, waits for them, and re-layouts  7.65 us (4%)
    pallas_call x3, Pallas kernels, attend(): pl.pallas_call(functools.partial(attend_kernel, slices, len(blocks), head...  35.8 us
    ppermute x20, starting transfers between devices, shift(): lax.ppermute(array, axis, [(i, (i + by) % NEAR) for i in range(NEAR)])  30.2 us
    ppermute x20, waiting for transfers between devices, shift(): lax.ppermute(array, axis, [(i, (i + by) % NEAR) for i in range(NEAR)])  26 us
    ppermute x9, starting transfers between devices, other(): return lax.ppermute(array, axis, [(0, 1), (1, 0)])  20.1 us
    pallas_call x2, Pallas kernels, project(): pl.pallas_call(functools.partial(project_kernel, terms, len(pieces), len(...  15.3 us
    ppermute x9, waiting for transfers between devices, other(): return lax.ppermute(array, axis, [(0, 1), (1, 0)])  14.4 us
    ppermute x1, waiting for transfers between devices, per_device(): returned_far = lax.ppermute(heads_in, ('xl', 'xh'), DIAGONAL)  11.1 us
    pallas_call x2, Pallas kernels, combine(): pl.pallas_call(functools.partial(combine_kernel, heads), out_shape=jax.Sh...  6.88 us
  transfers between devices with their start and end apart: 32, of which 13 were waited for; matrix products, arithmetic and copies ran while one was open for 3% of the time, Pallas kernels for 28%

profile of v2, /device:TPU:1, one launch (start us, length us, event | category | flops | bytes accessed | tf_op | source)
XLA Modules:
  0.0 179.6 jit_solution(9091581263464849846)
XLA Ops:
  0.6 3.2 %shard_map.86 = (bf16[3072,128]{1,0:T(8,128)(2,1)}, bf16[1024,128]{1,0:T(8,128)(2,1)}, bf16[3072,128]{1,0:T(8,128)(2,1)}, bf16[1536,128]{1,0:T(8,128)(2,1)}) custom-call(s32[1]{0:T(128)} %bitcast.at_ref, bf16[256,640]{1,0:T(8,128)(2,1)} %refs_0_.1, bf16[256,640]{1,0:T(8,128)(2,1)} %refs_1_.1, bf16[256,640]{1,0:T(8,128)(2,1)} %refs_2_.1, ...), custom_call_target="tpu_custom_call" | custom-call | flops 1 | bytes 1 | tf_op jit(solution)/shard_map/pallas_call | solution.py:288
  3.8 3.6 %collective-permute-start.8 = (bf16[3072,128]{1,0:T(8,128)(2,1)}, bf16[3072,128]{1,0:T(8,128)(2,1)S(1)}, u32[]{:S(2)}, u32[]{:S(2)}) collective-permute-start(bf16[3072,128]{1,0:T(8,128)(2,1)} %get-tuple-element.46.refs_4_.refs_12_), channel_id=1, source_target_pairs={{0,12},{4,0},{8,4},{12,8},{1,13},{5,1},{9,5},{13,9},{2,14},{6,2},{... | collective-permute-start | bytes 2359304 | tf_op jit(solution)/shard_map/ppermute | solution.py:25
  7.4 2.7 %collective-permute-start.1 = (bf16[1024,128]{1,0:T(8,128)(2,1)}, bf16[1024,128]{1,0:T(8,128)(2,1)S(1)}, u32[]{:S(2)}, u32[]{:S(2)}) collective-permute-start(bf16[1024,128]{1,0:T(8,128)(2,1)} %get-tuple-element.41), channel_id=1, source_target_pairs={{0,16},{16,0},{1,17},{17,1},{2,18},{18,2},{3,19},{19,3},{4,20},{20... | collective-permute-start | bytes 786440 | tf_op jit(solution)/shard_map/ppermute | solution.py:29
  10.1 5.8 %collective-permute-done.1.refs_0_ = bf16[1024,128]{1,0:T(8,128)(2,1)S(1)} collective-permute-done((bf16[1024,128]{1,0:T(8,128)(2,1)}, bf16[1024,128]{1,0:T(8,128)(2,1)S(1)}, u32[]{:S(2)}, u32[]{:S(2)}) %collective-permute-start.1) | collective-permute-done | bytes 262176 | tf_op jit(solution)/shard_map/ppermute | solution.py:29
  16.0 2.7 %collective-permute-start.10 = (bf16[3072,128]{1,0:T(8,128)(2,1)}, bf16[3072,128]{1,0:T(8,128)(2,1)S(1)}, u32[]{:S(2)}, u32[]{:S(2)}) collective-permute-start(bf16[3072,128]{1,0:T(8,128)(2,1)} %get-tuple-element.48), channel_id=1, source_target_pairs={{0,16},{16,0},{1,17},{17,1},{2,18},{18,2},{3,19},{19,3},{4,20},{20... | collective-permute-start | bytes 2359304 | tf_op jit(solution)/shard_map/ppermute | solution.py:29
  20.4 3.6 %collective-permute-done.8.refs_6_.refs_14_ = bf16[3072,128]{1,0:T(8,128)(2,1)S(1)} collective-permute-done((bf16[3072,128]{1,0:T(8,128)(2,1)}, bf16[3072,128]{1,0:T(8,128)(2,1)S(1)}, u32[]{:S(2)}, u32[]{:S(2)}) %collective-permute-start.8) | collective-permute-done | bytes 786464 | tf_op jit(solution)/shard_map/ppermute | solution.py:25
  24.0 3.4 %collective-permute-start.11 = (bf16[1536,128]{1,0:T(8,128)(2,1)S(1)}, bf16[1536,128]{1,0:T(8,128)(2,1)S(1)}, u32[]{:S(2)}, u32[]{:S(2)}) collective-permute-start(bf16[1536,128]{1,0:T(8,128)(2,1)S(1)} %slice.17), channel_id=1, source_target_pairs={{0,12},{4,0},{8,4},{12,8},{1,13},{5,1},{9,5},{13,9},{2,14},{6,2},{... | collective-permute-start | bytes 1179656 | tf_op jit(solution)/shard_map/ppermute | solution.py:25
  28.2 4.5 %constant_dynamic-slice_fusion = (bf16[640,1280]{1,0:T(8,128)(2,1)}, bf16[640,1280]{1,0:T(8,128)(2,1)S(1)}, bf16[640,1280]{1,0:T(8,128)(2,1)}) fusion(bf16[640,5120]{1,0:T(8,128)(2,1)} %refs_5_.3, s32[]{:T(128)S(6)} %select_n.11, s32[]{:T(128)S(6)} %select_n.10, s32[]{:T(128)S(6)} %select_n.9), kind=kLoop, calls=%fused_computation.1 | loop fusion | bytes 9830412 | tf_op jit(solution)/shard_map/dynamic_slice | solution.py:263
  32.7 3.8 %collective-permute-start.2 = (bf16[1536,128]{1,0:T(8,128)(2,1)S(1)}, bf16[1536,128]{1,0:T(8,128)(2,1)S(1)}, u32[]{:S(2)}, u32[]{:S(2)}) collective-permute-start(bf16[1536,128]{1,0:T(8,128)(2,1)S(1)} %copy-done.13), channel_id=1, source_target_pairs={{0,3},{1,0},{2,1},{3,2},{4,7},{5,4},{6,5},{7,6},{8,11},{9,8},{10,9... | collective-permute-start | bytes 1179656 | tf_op jit(solution)/shard_map/ppermute | solution.py:25
  40.0 3.1 %collective-permute-done.2.refs_2_ = bf16[1536,128]{1,0:T(8,128)(2,1)S(1)} collective-permute-done((bf16[1536,128]{1,0:T(8,128)(2,1)S(1)}, bf16[1536,128]{1,0:T(8,128)(2,1)S(1)}, u32[]{:S(2)}, u32[]{:S(2)}) %collective-permute-start.2) | collective-permute-done | bytes 393248 | tf_op jit(solution)/shard_map/ppermute | solution.py:25
  43.1 2.0 %collective-permute-start.3 = (bf16[1536,128]{1,0:T(8,128)(2,1)S(1)}, bf16[1536,128]{1,0:T(8,128)(2,1)S(1)}, u32[]{:S(2)}, u32[]{:S(2)}) collective-permute-start(bf16[1536,128]{1,0:T(8,128)(2,1)S(1)} %copy-done.13), channel_id=1, source_target_pairs={{0,2},{1,3},{2,0},{3,1},{4,6},{5,7},{6,4},{7,5},{8,10},{9,11},{10,... | collective-permute-start | bytes 1179656 | tf_op jit(solution)/shard_map/ppermute | solution.py:25
  45.2 7.3 %collective-permute-done.3.refs_3_ = bf16[1536,128]{1,0:T(8,128)(2,1)S(1)} collective-permute-done((bf16[1536,128]{1,0:T(8,128)(2,1)S(1)}, bf16[1536,128]{1,0:T(8,128)(2,1)S(1)}, u32[]{:S(2)}, u32[]{:S(2)}) %collective-permute-start.3) | collective-permute-done | bytes 393248 | tf_op jit(solution)/shard_map/ppermute | solution.py:25
  52.5 3.4 %collective-permute-start.5 = (bf16[1024,128]{1,0:T(8,128)(2,1)S(1)}, bf16[1024,128]{1,0:T(8,128)(2,1)S(1)}, u32[]{:S(2)}, u32[]{:S(2)}) collective-permute-start(bf16[1024,128]{1,0:T(8,128)(2,1)S(1)} %copy-done.21), channel_id=1, source_target_pairs={{0,3},{1,0},{2,1},{3,2},{4,7},{5,4},{6,5},{7,6},{8,11},{9,8},{10,9... | collective-permute-start | bytes 786440 | tf_op jit(solution)/shard_map/ppermute | solution.py:25
  56.0 2.2 %collective-permute-start.15 = (bf16[1536,128]{1,0:T(8,128)(2,1)S(1)}, bf16[1536,128]{1,0:T(8,128)(2,1)S(1)}, u32[]{:S(2)}, u32[]{:S(2)}) collective-permute-start(bf16[1536,128]{1,0:T(8,128)(2,1)S(1)} %slice.19), channel_id=1, source_target_pairs={{0,12},{4,0},{8,4},{12,8},{1,13},{5,1},{9,5},{13,9},{2,14},{6,2},{... | collective-permute-start | bytes 1179656 | tf_op jit(solution)/shard_map/ppermute | solution.py:25
  59.8 2.6 %collective-permute-done.4.refs_1_ = bf16[1024,128]{1,0:T(8,128)(2,1)S(1)} collective-permute-done((bf16[1024,128]{1,0:T(8,128)(2,1)S(1)}, bf16[1024,128]{1,0:T(8,128)(2,1)S(1)}, u32[]{:S(2)}, u32[]{:S(2)}) %collective-permute-start.4) | collective-permute-done | bytes 262176 | tf_op jit(solution)/shard_map/ppermute | solution.py:25
  65.6 3.9 %collective-permute-done.6.refs_3_ = bf16[1024,128]{1,0:T(8,128)(2,1)S(1)} collective-permute-done((bf16[1024,128]{1,0:T(8,128)(2,1)S(1)}, bf16[1024,128]{1,0:T(8,128)(2,1)S(1)}, u32[]{:S(2)}, u32[]{:S(2)}) %collective-permute-start.6) | collective-permute-done | bytes 262176 | tf_op jit(solution)/shard_map/ppermute | solution.py:25
  70.9 13.4 %shard_map.87 = (bf16[1280,128]{1,0:T(8,128)(2,1)}, bf16[1280,128]{1,0:T(8,128)(2,1)}, bf16[1280,128]{1,0:T(8,128)(2,1)}, bf16[1280,128]{1,0:T(8,128)(2,1)}) custom-call(bf16[1024,128]{1,0:T(8,128)(2,1)} %copy-done.20, bf16[1024,128]{1,0:T(8,128)(2,1)} %copy-done.23, bf16[1024,128]{1,0:T(8,128)(2,1)} %copy-done.22, bf16[1024,128]{1,0:T(8,128)(2,1)} %copy-done.24, ...), custom_call_target="tpu_custom_call" | custom-call | flops 17179869184 | bytes 7340032 | tf_op jit(solution)/shard_map/pallas_call | solution.py:132
  85.9 2.0 %collective-permute-start.18 = (bf16[1280,128]{1,0:T(8,128)(2,1)}, bf16[1280,128]{1,0:T(8,128)(2,1)}, u32[]{:S(2)}, u32[]{:S(2)}) collective-permute-start(bf16[1280,128]{1,0:T(8,128)(2,1)} %get-tuple-element.53), channel_id=1, source_target_pairs={{0,2},{1,3},{2,0},{3,1},{4,6},{5,7},{6,4},{7,5},{8,10},{9,11},{10,... | collective-permute-start | bytes 983048 | tf_op jit(solution)/shard_map/ppermute | solution.py:25
  87.9 13.4 %shard_map.88 = (bf16[1280,128]{1,0:T(8,128)(2,1)}, bf16[1280,128]{1,0:T(8,128)(2,1)}, bf16[1280,128]{1,0:T(8,128)(2,1)}, bf16[1280,128]{1,0:T(8,128)(2,1)}) custom-call(bf16[1536,128]{1,0:T(8,128)(2,1)} %get-tuple-element.62.refs_0_, bf16[1536,128]{1,0:T(8,128)(2,1)} %copy-done.14, bf16[1536,128]{1,0:T(8,128)(2,1)} %copy-done.17, ...), custom_call_target="tpu_custom_call" | custom-call | flops 17179869184 | bytes 7340032 | tf_op jit(solution)/shard_map/pallas_call | solution.py:132
  101.3 9.0 %shard_map.89 = (bf16[2048,128]{1,0:T(8,128)(2,1)}, bf16[2048,128]{1,0:T(8,128)(2,1)}, bf16[2048,128]{1,0:T(8,128)(2,1)}, bf16[2048,128]{1,0:T(8,128)(2,1)}) custom-call(bf16[1536,128]{1,0:T(8,128)(2,1)} %get-tuple-element.62.refs_0_, bf16[1536,128]{1,0:T(8,128)(2,1)} %copy-done.14, bf16[1536,128]{1,0:T(8,128)(2,1)} %copy-done.17, ...), custom_call_target="tpu_custom_call" | custom-call | flops 8589934592 | bytes 3670016 | tf_op jit(solution)/shard_map/pallas_call | solution.py:132
  110.4 8.9 %collective-permute-start.26 = (bf16[640,1280]{1,0:T(8,128)(2,1)}, bf16[640,1280]{1,0:T(8,128)(2,1)S(1)}, u32[]{:S(2)}, u32[]{:S(2)}) collective-permute-start(bf16[640,1280]{1,0:T(8,128)(2,1)} %collective-permute-done.25), channel_id=1, source_target_pairs={{0,32},{32,0},{1,33},{33,1},{2,34},{34,2},{3,35},{35,3},{4,36},{36... | collective-permute-start | bytes 4915208 | tf_op jit(solution)/shard_map/ppermute | solution.py:29
  119.3 2.4 %collective-permute-start.19 = (bf16[2048,128]{1,0:T(8,128)(2,1)}, bf16[2048,128]{1,0:T(8,128)(2,1)}, u32[]{:S(2)}, u32[]{:S(2)}) collective-permute-start(bf16[2048,128]{1,0:T(8,128)(2,1)} %get-tuple-element.67), channel_id=1, source_target_pairs={{0,3},{1,0},{2,1},{3,2},{4,7},{5,4},{6,5},{7,6},{8,11},{9,8},{10,9... | collective-permute-start | bytes 1572872 | tf_op jit(solution)/shard_map/ppermute | solution.py:25
  121.8 2.3 %collective-permute-start.21 = (bf16[2048,128]{1,0:T(8,128)(2,1)}, bf16[2048,128]{1,0:T(8,128)(2,1)}, u32[]{:S(2)}, u32[]{:S(2)}) collective-permute-start(bf16[2048,128]{1,0:T(8,128)(2,1)} %get-tuple-element.69), channel_id=1, source_target_pairs={{0,2},{1,3},{2,0},{3,1},{4,6},{5,7},{6,4},{7,5},{8,10},{9,11},{10,... | collective-permute-start | bytes 1572872 | tf_op jit(solution)/shard_map/ppermute | solution.py:25
  125.1 3.0 %shard_map.91 = bf16[512,256]{1,0:T(8,128)(2,1)} custom-call(bf16[1280,128]{1,0:T(8,128)(2,1)} %get-tuple-element.74.refs_0_, bf16[1280,128]{1,0:T(8,128)(2,1)} %copy-done.6, bf16[1280,128]{1,0:T(8,128)(2,1)} %copy-done.7, bf16[1280,128]{1,0:T(8,128)(2,1)} %collective-permute-done.18.refs_3_), custom_call_target="tpu_custom_call" | custom-call | flops 1 | bytes 1 | tf_op jit(solution)/shard_map/pallas_call | solution.py:178
  128.0 2.5 %collective-permute-start.29 = (bf16[512,256]{1,0:T(8,128)(2,1)}, bf16[512,256]{1,0:T(8,128)(2,1)S(1)}, u32[]{:S(2)}, u32[]{:S(2)}) collective-permute-start(bf16[512,256]{1,0:T(8,128)(2,1)} %shard_map.91), channel_id=1, source_target_pairs={{0,80},{16,64},{64,16},{80,0},{1,81},{17,65},{65,17},{81,1},{2,82}... | collective-permute-start | bytes 786440 | tf_op jit(solution)/shard_map/ppermute | solution.py:329
  131.0 11.1 %collective-permute-done.29.refs_2_ = bf16[512,256]{1,0:T(8,128)(2,1)S(1)} collective-permute-done((bf16[512,256]{1,0:T(8,128)(2,1)}, bf16[512,256]{1,0:T(8,128)(2,1)S(1)}, u32[]{:S(2)}, u32[]{:S(2)}) %collective-permute-start.29) | collective-permute-done | bytes 262176 | tf_op jit(solution)/shard_map/ppermute | solution.py:329
  144.7 2.3 %collective-permute-done.21.refs_3_ = bf16[2048,128]{1,0:T(8,128)(2,1)} collective-permute-done((bf16[2048,128]{1,0:T(8,128)(2,1)}, bf16[2048,128]{1,0:T(8,128)(2,1)}, u32[]{:S(2)}, u32[]{:S(2)}) %collective-permute-start.21) | collective-permute-done | bytes 524320 | tf_op jit(solution)/shard_map/ppermute | solution.py:25
  147.0 3.9 %shard_map.90.refs_0_ = bf16[512,384]{1,0:T(8,128)(2,1)} custom-call(bf16[2048,128]{1,0:T(8,128)(2,1)} %get-tuple-element.66.refs_0_, bf16[2048,128]{1,0:T(8,128)(2,1)} %collective-permute-done.19.refs_1_, bf16[2048,128]{1,0:T(8,128)(2,1)} %collective-permute-done.20.refs_2_, bf16[2048,128]{1,0:T(8,128)(2,1)} %collective-permute-done.21.refs_3_), custom_call_target="tpu_custom_call" | custom-call | flops 1 | bytes 1 | tf_op jit(solution)/shard_map/pallas_call | solution.py:178
  150.9 2.0 %collective-permute-start.31 = (bf16[512,384]{1,0:T(8,128)(2,1)}, bf16[512,384]{1,0:T(8,128)(2,1)}, u32[]{:S(2)}, u32[]{:S(2)}) collective-permute-start(bf16[512,384]{1,0:T(8,128)(2,1)} %shard_map.90.refs_0_), channel_id=1, source_target_pairs={{0,32},{32,0},{1,33},{33,1},{2,34},{34,2},{3,35},{35,3},{4,36},{36... | collective-permute-start | bytes 1179656 | tf_op jit(solution)/shard_map/ppermute | solution.py:29
  155.0 8.5 %shard_map.92.refs_4_ = f32[512,1280]{1,0:T(8,128)} custom-call(s32[2]{0:T(128)} %pad_add_fusion.at_ref, bf16[512,384]{1,0:T(8,128)(2,1)} %shard_map.90.refs_0_, bf16[512,256]{1,0:T(8,128)(2,1)} %copy-done.3, bf16[512,256]{1,0:T(8,128)(2,1)} %copy-done.2, bf16[512,512]{1,0:T(8,128)(2,1)} %collective-permute-done.30.refs_3_, ...), custom_call_target="tpu_custom_call" | custom-call | flops 1 | bytes 1 | tf_op jit(solution)/shard_map/pallas_call | solution.py:243
  164.5 7.6 %collective-permute-done.22.refs_0_ = bf16[512,384]{1,0:T(8,128)(2,1)S(1)} collective-permute-done((bf16[512,384]{1,0:T(8,128)(2,1)}, bf16[512,384]{1,0:T(8,128)(2,1)S(1)}, u32[]{:S(2)}, u32[]{:S(2)}) %collective-permute-start.22) | collective-permute-done | bytes 393248 | tf_op jit(solution)/shard_map/ppermute | solution.py:29
  172.8 6.8 %shard_map.93 = (bf16[256,1280]{1,0:T(8,128)(2,1)}, bf16[256,1280]{1,0:T(8,128)(2,1)}) custom-call(s32[2]{0:T(128)} %pad_add_fusion.at_ref, bf16[512,384]{1,0:T(8,128)(2,1)} %copy-done.5, bf16[512,384]{1,0:T(8,128)(2,1)} %copy-done.4, bf16[640,1280]{1,0:T(8,128)(2,1)} %copy-done, bf16[640,1280]{1,0:T(8,128)(2,1)} %copy-done.1, f32[512,1280]{1,0:T(8,128)} %shard_map.92.refs_4_), custom_call_target="tpu_custom_call" | custom-call | flops 1 | bytes 1 | tf_op jit(solution)/shard_map/pallas_call | solution.py:243
  (97 shorter events, 21.9 us)
Async XLA Ops:
  3.8 20.1 %collective-permute-start.8 = (bf16[3072,128]{1,0:T(8,128)(2,1)}, bf16[3072,128]{1,0:T(8,128)(2,1)S(1)}, u32[]{:S(2)}, u32[]{:S(2)}) collective-permute-start(bf16[3072,128]{1,0:T(8,128)(2,1)} %get-tuple-element.46.refs_4_.refs_12_), channel_id=1, source_target_pairs={{0,12},{4,0},{8,4},{12,8},{1,13},{5,1},{9,5},{13,9},{2,14},{6,2},{... | collective-permute-start | bytes 2359304 | tf_op jit(solution)/shard_map/ppermute | solution.py:25
  7.4 19.9 %collective-permute-start.7 = (bf16[3072,128]{1,0:T(8,128)(2,1)}, bf16[3072,128]{1,0:T(8,128)(2,1)S(1)}, u32[]{:S(2)}, u32[]{:S(2)}) collective-permute-start(bf16[3072,128]{1,0:T(8,128)(2,1)} %get-tuple-element.46.refs_4_.refs_12_), channel_id=1, source_target_pairs={{0,4},{4,8},{8,12},{12,0},{1,5},{5,9},{9,13},{13,1},{2,6},{6,10},{... | collective-permute-start | bytes 2359304 | tf_op jit(solution)/shard_map/ppermute | solution.py:25
  7.4 8.6 %collective-permute-start.1 = (bf16[1024,128]{1,0:T(8,128)(2,1)}, bf16[1024,128]{1,0:T(8,128)(2,1)S(1)}, u32[]{:S(2)}, u32[]{:S(2)}) collective-permute-start(bf16[1024,128]{1,0:T(8,128)(2,1)} %get-tuple-element.41), channel_id=1, source_target_pairs={{0,16},{16,0},{1,17},{17,1},{2,18},{18,2},{3,19},{19,3},{4,20},{20... | collective-permute-start | bytes 786440 | tf_op jit(solution)/shard_map/ppermute | solution.py:29
  16.0 20.6 %collective-permute-start.10 = (bf16[3072,128]{1,0:T(8,128)(2,1)}, bf16[3072,128]{1,0:T(8,128)(2,1)S(1)}, u32[]{:S(2)}, u32[]{:S(2)}) collective-permute-start(bf16[3072,128]{1,0:T(8,128)(2,1)} %get-tuple-element.48), channel_id=1, source_target_pairs={{0,16},{16,0},{1,17},{17,1},{2,18},{18,2},{3,19},{19,3},{4,20},{20... | collective-permute-start | bytes 2359304 | tf_op jit(solution)/shard_map/ppermute | solution.py:29
  18.7 14.0 %collective-permute-start = (bf16[1536,128]{1,0:T(8,128)(2,1)}, bf16[1536,128]{1,0:T(8,128)(2,1)S(1)}, u32[]{:S(2)}, u32[]{:S(2)}) collective-permute-start(bf16[1536,128]{1,0:T(8,128)(2,1)} %get-tuple-element.62.refs_0_), channel_id=1, source_target_pairs={{0,1},{1,2},{2,3},{3,0},{4,5},{5,6},{6,7},{7,4},{8,9},{9,10},{10,1... | collective-permute-start | bytes 1179656 | tf_op jit(solution)/shard_map/ppermute | solution.py:25
  24.0 12.6 %collective-permute-start.11 = (bf16[1536,128]{1,0:T(8,128)(2,1)S(1)}, bf16[1536,128]{1,0:T(8,128)(2,1)S(1)}, u32[]{:S(2)}, u32[]{:S(2)}) collective-permute-start(bf16[1536,128]{1,0:T(8,128)(2,1)S(1)} %slice.17), channel_id=1, source_target_pairs={{0,12},{4,0},{8,4},{12,8},{1,13},{5,1},{9,5},{13,9},{2,14},{6,2},{... | collective-permute-start | bytes 1179656 | tf_op jit(solution)/shard_map/ppermute | solution.py:25
  28.2 10.0 %collective-permute-start.9 = (bf16[1536,128]{1,0:T(8,128)(2,1)S(1)}, bf16[1536,128]{1,0:T(8,128)(2,1)S(1)}, u32[]{:S(2)}, u32[]{:S(2)}) collective-permute-start(bf16[1536,128]{1,0:T(8,128)(2,1)S(1)} %slice.16), channel_id=1, source_target_pairs={{0,4},{4,8},{8,12},{12,0},{1,5},{5,9},{9,13},{13,1},{2,6},{6,10},{... | collective-permute-start | bytes 1179656 | tf_op jit(solution)/shard_map/ppermute | solution.py:25
  32.7 10.4 %collective-permute-start.2 = (bf16[1536,128]{1,0:T(8,128)(2,1)S(1)}, bf16[1536,128]{1,0:T(8,128)(2,1)S(1)}, u32[]{:S(2)}, u32[]{:S(2)}) collective-permute-start(bf16[1536,128]{1,0:T(8,128)(2,1)S(1)} %copy-done.13), channel_id=1, source_target_pairs={{0,3},{1,0},{2,1},{3,2},{4,7},{5,4},{6,5},{7,6},{8,11},{9,8},{10,9... | collective-permute-start | bytes 1179656 | tf_op jit(solution)/shard_map/ppermute | solution.py:25
  38.2 17.7 %collective-permute-start.13 = (bf16[3072,128]{1,0:T(8,128)(2,1)S(1)}, bf16[3072,128]{1,0:T(8,128)(2,1)S(1)}, u32[]{:S(2)}, u32[]{:S(2)}) collective-permute-start(bf16[3072,128]{1,0:T(8,128)(2,1)S(1)} %collective-permute-done.10.refs_8_.refs_16_), channel_id=1, source_target_pairs={{0,12},{4,0},{8,4},{12,8},{1,13},{5,1},{9,5},{13,9},{2,14},{6,2},{... | collective-permute-start | bytes 2359304 | tf_op jit(solution)/shard_map/ppermute | solution.py:25
  40.0 18.1 %collective-permute-start.12 = (bf16[3072,128]{1,0:T(8,128)(2,1)S(1)}, bf16[3072,128]{1,0:T(8,128)(2,1)S(1)}, u32[]{:S(2)}, u32[]{:S(2)}) collective-permute-start(bf16[3072,128]{1,0:T(8,128)(2,1)S(1)} %collective-permute-done.10.refs_8_.refs_16_), channel_id=1, source_target_pairs={{0,4},{4,8},{8,12},{12,0},{1,5},{5,9},{9,13},{13,1},{2,6},{6,10},{... | collective-permute-start | bytes 2359304 | tf_op jit(solution)/shard_map/ppermute | solution.py:25
  43.1 9.4 %collective-permute-start.3 = (bf16[1536,128]{1,0:T(8,128)(2,1)S(1)}, bf16[1536,128]{1,0:T(8,128)(2,1)S(1)}, u32[]{:S(2)}, u32[]{:S(2)}) collective-permute-start(bf16[1536,128]{1,0:T(8,128)(2,1)S(1)} %copy-done.13), channel_id=1, source_target_pairs={{0,2},{1,3},{2,0},{3,1},{4,6},{5,7},{6,4},{7,5},{8,10},{9,11},{10,... | collective-permute-start | bytes 1179656 | tf_op jit(solution)/shard_map/ppermute | solution.py:25
  52.5 7.2 %collective-permute-start.5 = (bf16[1024,128]{1,0:T(8,128)(2,1)S(1)}, bf16[1024,128]{1,0:T(8,128)(2,1)S(1)}, u32[]{:S(2)}, u32[]{:S(2)}) collective-permute-start(bf16[1024,128]{1,0:T(8,128)(2,1)S(1)} %copy-done.21), channel_id=1, source_target_pairs={{0,3},{1,0},{2,1},{3,2},{4,7},{5,4},{6,5},{7,6},{8,11},{9,8},{10,9... | collective-permute-start | bytes 786440 | tf_op jit(solution)/shard_map/ppermute | solution.py:25
  55.9 6.4 %collective-permute-start.4 = (bf16[1024,128]{1,0:T(8,128)(2,1)S(1)}, bf16[1024,128]{1,0:T(8,128)(2,1)S(1)}, u32[]{:S(2)}, u32[]{:S(2)}) collective-permute-start(bf16[1024,128]{1,0:T(8,128)(2,1)S(1)} %copy-done.21), channel_id=1, source_target_pairs={{0,1},{1,2},{2,3},{3,0},{4,5},{5,6},{6,7},{7,4},{8,9},{9,10},{10,1... | collective-permute-start | bytes 786440 | tf_op jit(solution)/shard_map/ppermute | solution.py:25
  56.0 13.5 %collective-permute-start.15 = (bf16[1536,128]{1,0:T(8,128)(2,1)S(1)}, bf16[1536,128]{1,0:T(8,128)(2,1)S(1)}, u32[]{:S(2)}, u32[]{:S(2)}) collective-permute-start(bf16[1536,128]{1,0:T(8,128)(2,1)S(1)} %slice.19), channel_id=1, source_target_pairs={{0,12},{4,0},{8,4},{12,8},{1,13},{5,1},{9,5},{13,9},{2,14},{6,2},{... | collective-permute-start | bytes 1179656 | tf_op jit(solution)/shard_map/ppermute | solution.py:25
  58.2 12.8 %collective-permute-start.14 = (bf16[1536,128]{1,0:T(8,128)(2,1)S(1)}, bf16[1536,128]{1,0:T(8,128)(2,1)}, u32[]{:S(2)}, u32[]{:S(2)}) collective-permute-start(bf16[1536,128]{1,0:T(8,128)(2,1)S(1)} %slice.18), channel_id=1, source_target_pairs={{0,4},{4,8},{8,12},{12,0},{1,5},{5,9},{9,13},{13,1},{2,6},{6,10},{... | collective-permute-start | bytes 1179656 | tf_op jit(solution)/shard_map/ppermute | solution.py:25
  62.4 7.1 %collective-permute-start.6 = (bf16[1024,128]{1,0:T(8,128)(2,1)S(1)}, bf16[1024,128]{1,0:T(8,128)(2,1)S(1)}, u32[]{:S(2)}, u32[]{:S(2)}) collective-permute-start(bf16[1024,128]{1,0:T(8,128)(2,1)S(1)} %copy-done.21), channel_id=1, source_target_pairs={{0,2},{1,3},{2,0},{3,1},{4,6},{5,7},{6,4},{7,5},{8,10},{9,11},{10,... | collective-permute-start | bytes 786440 | tf_op jit(solution)/shard_map/ppermute | solution.py:25
  62.5 59.3 %collective-permute-start.24 = (bf16[640,1280]{1,0:T(8,128)(2,1)}, bf16[640,1280]{1,0:T(8,128)(2,1)S(1)}, u32[]{:S(2)}, u32[]{:S(2)}) collective-permute-start(bf16[640,1280]{1,0:T(8,128)(2,1)} %get-tuple-element.70), channel_id=1, source_target_pairs={{0,64},{64,0},{1,65},{65,1},{2,66},{66,2},{3,67},{67,3},{4,68},{68... | collective-permute-start | bytes 4915208 | tf_op jit(solution)/shard_map/ppermute | solution.py:29
  63.7 46.6 %collective-permute-start.25 = (bf16[640,1280]{1,0:T(8,128)(2,1)S(1)}, bf16[640,1280]{1,0:T(8,128)(2,1)}, u32[]{:S(2)}, u32[]{:S(2)}) collective-permute-start(bf16[640,1280]{1,0:T(8,128)(2,1)S(1)} %get-tuple-element.71), channel_id=1, source_target_pairs={{0,80},{16,64},{64,16},{80,0},{1,81},{17,65},{65,17},{81,1},{2,82}... | collective-permute-start | bytes 4915208 | tf_op jit(solution)/shard_map/ppermute | solution.py:316
  84.3 17.0 %collective-permute-start.16 = (bf16[1280,128]{1,0:T(8,128)(2,1)}, bf16[1280,128]{1,0:T(8,128)(2,1)S(1)}, u32[]{:S(2)}, u32[]{:S(2)}) collective-permute-start(bf16[1280,128]{1,0:T(8,128)(2,1)} %get-tuple-element.51), channel_id=1, source_target_pairs={{0,3},{1,0},{2,1},{3,2},{4,7},{5,4},{6,5},{7,6},{8,11},{9,8},{10,9... | collective-permute-start | bytes 983048 | tf_op jit(solution)/shard_map/ppermute | solution.py:25
  84.8 16.5 %collective-permute-start.17 = (bf16[1280,128]{1,0:T(8,128)(2,1)}, bf16[1280,128]{1,0:T(8,128)(2,1)S(1)}, u32[]{:S(2)}, u32[]{:S(2)}) collective-permute-start(bf16[1280,128]{1,0:T(8,128)(2,1)} %get-tuple-element.52), channel_id=1, source_target_pairs={{0,1},{1,2},{2,3},{3,0},{4,5},{5,6},{6,7},{7,4},{8,9},{9,10},{10,1... | collective-permute-start | bytes 983048 | tf_op jit(solution)/shard_map/ppermute | solution.py:25
  85.9 15.5 %collective-permute-start.18 = (bf16[1280,128]{1,0:T(8,128)(2,1)}, bf16[1280,128]{1,0:T(8,128)(2,1)}, u32[]{:S(2)}, u32[]{:S(2)}) collective-permute-start(bf16[1280,128]{1,0:T(8,128)(2,1)} %get-tuple-element.53), channel_id=1, source_target_pairs={{0,2},{1,3},{2,0},{3,1},{4,6},{5,7},{6,4},{7,5},{8,10},{9,11},{10,... | collective-permute-start | bytes 983048 | tf_op jit(solution)/shard_map/ppermute | solution.py:25
  110.4 13.7 %collective-permute-start.26 = (bf16[640,1280]{1,0:T(8,128)(2,1)}, bf16[640,1280]{1,0:T(8,128)(2,1)S(1)}, u32[]{:S(2)}, u32[]{:S(2)}) collective-permute-start(bf16[640,1280]{1,0:T(8,128)(2,1)} %collective-permute-done.25), channel_id=1, source_target_pairs={{0,32},{32,0},{1,33},{33,1},{2,34},{34,2},{3,35},{35,3},{4,36},{36... | collective-permute-start | bytes 4915208 | tf_op jit(solution)/shard_map/ppermute | solution.py:29
  119.3 5.8 %collective-permute-start.27 = (bf16[640,1280]{1,0:T(8,128)(2,1)}, bf16[640,1280]{1,0:T(8,128)(2,1)}, u32[]{:S(2)}, u32[]{:S(2)}) collective-permute-start(bf16[640,1280]{1,0:T(8,128)(2,1)} %get-tuple-element.73), channel_id=1, source_target_pairs={{0,32},{32,0},{1,33},{33,1},{2,34},{34,2},{3,35},{35,3},{4,36},{36... | collective-permute-start | bytes 4915208 | tf_op jit(solution)/shard_map/ppermute | solution.py:29
  119.3 25.4 %collective-permute-start.19 = (bf16[2048,128]{1,0:T(8,128)(2,1)}, bf16[2048,128]{1,0:T(8,128)(2,1)}, u32[]{:S(2)}, u32[]{:S(2)}) collective-permute-start(bf16[2048,128]{1,0:T(8,128)(2,1)} %get-tuple-element.67), channel_id=1, source_target_pairs={{0,3},{1,0},{2,1},{3,2},{4,7},{5,4},{6,5},{7,6},{8,11},{9,8},{10,9... | collective-permute-start | bytes 1572872 | tf_op jit(solution)/shard_map/ppermute | solution.py:25
  121.7 23.0 %collective-permute-start.20 = (bf16[2048,128]{1,0:T(8,128)(2,1)}, bf16[2048,128]{1,0:T(8,128)(2,1)}, u32[]{:S(2)}, u32[]{:S(2)}) collective-permute-start(bf16[2048,128]{1,0:T(8,128)(2,1)} %get-tuple-element.68), channel_id=1, source_target_pairs={{0,1},{1,2},{2,3},{3,0},{4,5},{5,6},{6,7},{7,4},{8,9},{9,10},{10,1... | collective-permute-start | bytes 1572872 | tf_op jit(solution)/shard_map/ppermute | solution.py:25
  121.8 25.2 %collective-permute-start.21 = (bf16[2048,128]{1,0:T(8,128)(2,1)}, bf16[2048,128]{1,0:T(8,128)(2,1)}, u32[]{:S(2)}, u32[]{:S(2)}) collective-permute-start(bf16[2048,128]{1,0:T(8,128)(2,1)} %get-tuple-element.69), channel_id=1, source_target_pairs={{0,2},{1,3},{2,0},{3,1},{4,6},{5,7},{6,4},{7,5},{8,10},{9,11},{10,... | collective-permute-start | bytes 1572872 | tf_op jit(solution)/shard_map/ppermute | solution.py:25
  128.0 14.1 %collective-permute-start.29 = (bf16[512,256]{1,0:T(8,128)(2,1)}, bf16[512,256]{1,0:T(8,128)(2,1)S(1)}, u32[]{:S(2)}, u32[]{:S(2)}) collective-permute-start(bf16[512,256]{1,0:T(8,128)(2,1)} %shard_map.91), channel_id=1, source_target_pairs={{0,80},{16,64},{64,16},{80,0},{1,81},{17,65},{65,17},{81,1},{2,82}... | collective-permute-start | bytes 786440 | tf_op jit(solution)/shard_map/ppermute | solution.py:329
  130.5 11.6 %collective-permute-start.28 = (bf16[512,256]{1,0:T(8,128)(2,1)}, bf16[512,256]{1,0:T(8,128)(2,1)S(1)}, u32[]{:S(2)}, u32[]{:S(2)}) collective-permute-start(bf16[512,256]{1,0:T(8,128)(2,1)} %shard_map.91), channel_id=1, source_target_pairs={{0,16},{16,0},{1,17},{17,1},{2,18},{18,2},{3,19},{19,3},{4,20},{20... | collective-permute-start | bytes 786440 | tf_op jit(solution)/shard_map/ppermute | solution.py:29
  143.0 11.9 %collective-permute-start.30 = (bf16[512,512]{1,0:T(8,128)(2,1)}, bf16[512,512]{1,0:T(8,128)(2,1)}, u32[]{:S(2)}, u32[]{:S(2)}) collective-permute-start(bf16[512,512]{1,0:T(8,128)(2,1)} %pad_maximum_fusion), channel_id=1, source_target_pairs={{0,32},{32,0},{1,33},{33,1},{2,34},{34,2},{3,35},{35,3},{4,36},{36... | collective-permute-start | bytes 1572872 | tf_op jit(solution)/shard_map/ppermute | solution.py:29
  150.9 4.1 %collective-permute-start.31 = (bf16[512,384]{1,0:T(8,128)(2,1)}, bf16[512,384]{1,0:T(8,128)(2,1)}, u32[]{:S(2)}, u32[]{:S(2)}) collective-permute-start(bf16[512,384]{1,0:T(8,128)(2,1)} %shard_map.90.refs_0_), channel_id=1, source_target_pairs={{0,32},{32,0},{1,33},{33,1},{2,34},{34,2},{3,35},{35,3},{4,36},{36... | collective-permute-start | bytes 1179656 | tf_op jit(solution)/shard_map/ppermute | solution.py:29
  152.9 11.6 %collective-permute-start.23 = (bf16[512,384]{1,0:T(8,128)(2,1)}, bf16[512,384]{1,0:T(8,128)(2,1)S(1)}, u32[]{:S(2)}, u32[]{:S(2)}) collective-permute-start(bf16[512,384]{1,0:T(8,128)(2,1)} %shard_map.90.refs_0_), channel_id=1, source_target_pairs={{0,96},{32,64},{64,32},{96,0},{1,97},{33,65},{65,33},{97,1},{2,98}... | collective-permute-start | bytes 1179656 | tf_op jit(solution)/shard_map/ppermute | solution.py:333
  154.1 18.0 %collective-permute-start.22 = (bf16[512,384]{1,0:T(8,128)(2,1)}, bf16[512,384]{1,0:T(8,128)(2,1)S(1)}, u32[]{:S(2)}, u32[]{:S(2)}) collective-permute-start(bf16[512,384]{1,0:T(8,128)(2,1)} %shard_map.90.refs_0_), channel_id=1, source_target_pairs={{0,64},{64,0},{1,65},{65,1},{2,66},{66,2},{3,67},{67,3},{4,68},{68... | collective-permute-start | bytes 1179656 | tf_op jit(solution)/shard_map/ppermute | solution.py:29
  (25 other events, 295.0 us)

commit v3 on v2

--- a/solution.py
+++ b/solution.py
@@ -73,15 +73,13 @@
     )
 
 
-def attend_kernel(slices, blocks, heads, above, *refs):
+def attend_kernel(slices, blocks, heads, partial, *refs):
     queries = refs[:slices]
     key_refs = refs[slices : slices + blocks]
     value_refs = refs[slices + blocks : slices + 2 * blocks]
     outs = refs[-slices:]
+    partials = refs[slices + 2 * blocks : -slices]
     head = pl.program_id(0)
-    if above:
-        for out, earlier in zip(outs, refs[slices + 2 * blocks : -slices]):
-            out[0:above, :] = earlier[...]
     lane = lax.broadcasted_iota(jnp.int32, (ROWS, DH), 1)
 
     def pairs(parts):
@@ -97,11 +95,33 @@
         inverse = 1.0 / total
         mean = slope * inverse
         out = acc * inverse
-        at = pl.multiple_of(above + head * 2 * ROWS, ROWS)
+        tangent = acc_tangent * inverse - mean * out
+        log_sum = new_max * LOG2_SCALE + jnp.log2(total)
+        if partial:
+            tail = from_three(partials[slices + i][...].astype(jnp.float32))
+            other_log = jnp.sum(jnp.where(lane == 2 * head, tail, 0.0), axis=1, keepdims=True)
+            other_mean = jnp.sum(jnp.where(lane == 2 * head + 1, tail, 0.0), axis=1, keepdims=True)
+            other_out = partials[i][0:ROWS, :].astype(jnp.float32)
+            other_tangent = partials[i][ROWS : 2 * ROWS, :].astype(jnp.float32)
+            top = jnp.maximum(log_sum, other_log)
+            share, other_share = jnp.exp2(log_sum - top), jnp.exp2(other_log - top)
+            both = share + other_share
+            log_sum = top + jnp.log2(both)
+            share, other_share = share / both, other_share / both
+            joint = share * mean + other_share * other_mean
+            tangent = (
+                share * tangent
+                + other_share * other_tangent
+                + (share * (mean - joint)) * out
+                + (other_share * (other_mean - joint)) * other_out
+            )
+            out = share * out + other_share * other_out
+            mean = joint
+        at = pl.multiple_of(head * 2 * ROWS, 2 * ROWS)
         outs[i][pl.ds(at, ROWS), :] = out.astype(jnp.bfloat16)
-        outs[i][pl.ds(at + ROWS, ROWS), :] = (acc_tangent * inverse - mean * out).astype(jnp.bfloat16)
-        tail = slice(above + 2 * heads * ROWS, above + (2 * heads + 1) * ROWS)
-        stats = jnp.where(lane == 2 * head, new_max * LOG2_SCALE + jnp.log2(total), 0.0)
+        outs[i][pl.ds(at + ROWS, ROWS), :] = tangent.astype(jnp.bfloat16)
+        tail = slice(2 * heads * ROWS, (2 * heads + 1) * ROWS)
+        stats = jnp.where(lane == 2 * head, log_sum, 0.0)
         stats = three_parts(jnp.where(lane == 2 * head + 1, mean, stats))
         before = jnp.where(head == 0, 0.0, outs[i][tail, :].astype(jnp.float32))
         outs[i][tail, :] = (before + stats).astype(jnp.bfloat16)
@@ -117,23 +137,26 @@
     finish(slices - 1, held)
 
 
-def attend(queries, blocks, first, heads, earlier=()):
+def attend(queries, blocks, partials=()):
+    heads = queries[0].shape[0] // (2 * ROWS)
     slices = len(queries)
-    query_spec = pl.BlockSpec((2 * ROWS, DH), lambda h: (first + h, 0))
+    head_spec = pl.BlockSpec((2 * ROWS, DH), lambda h: (h, 0))
+    stats_spec = pl.BlockSpec((ROWS, DH), lambda h: (2 * heads, 0))
     halved = [isinstance(b, tuple) for b in blocks]
-    key_spec = pl.BlockSpec((2 * ROWS, DH), lambda h: (first + h, 0))
-    value_specs = [pl.BlockSpec((2 * ROWS, DH), lambda h, w=w: (first + h if w else HELD + first + h, 0)) for w in halved]
+    value_specs = [
+        pl.BlockSpec((2 * ROWS, DH), lambda h, w=w: (h if w else HELD + h, 0)) for w in halved
+    ]
     keys = [b[0] if w else b for b, w in zip(blocks, halved)]
     values = [b[1] if w else b for b, w in zip(blocks, halved)]
-    above = earlier[0].shape[0] if earlier else 0
-    part_type = jax.ShapeDtypeStruct((above + (2 * heads + 1) * ROWS, DH), jnp.bfloat16)
-    part_spec = pl.BlockSpec(part_type.shape, lambda h: (0, 0))
-    earlier_specs = [pl.BlockSpec(e.shape, lambda h: (0, 0)) for e in earlier]
+    part_type = jax.ShapeDtypeStruct(((2 * heads + 1) * ROWS, DH), jnp.bfloat16)
     return pl.pallas_call(
-        functools.partial(attend_kernel, slices, len(blocks), heads, above),
+        functools.partial(attend_kernel, slices, len(blocks), heads, len(partials)),
         grid=(heads,),
-        in_specs=[query_spec] * slices + [key_spec] * len(blocks) + value_specs + earlier_specs,
-        out_specs=[part_spec] * slices,
+        in_specs=[head_spec] * (slices + len(blocks))
+        + value_specs
+        + [head_spec] * len(partials)
+        + [stats_spec] * len(partials),
+        out_specs=[pl.BlockSpec(part_type.shape, lambda h: (0, 0))] * slices,
         out_shape=[part_type] * slices,
         compiler_params=pltpu.CompilerParams(vmem_limit_bytes=VMEM),
         cost_estimate=pl.CostEstimate(
@@ -141,18 +164,11 @@
             bytes_accessed=(len(blocks) * 4 + slices * 6) * heads * ROWS * DH * 2,
             transcendentals=slices * len(blocks) * heads * ROWS**2,
         ),
-    )(*queries, *keys, *values, *earlier)
+    )(*queries, *keys, *values, *partials, *partials)
 
 
 def combine_kernel(heads, *refs):
-    row = column = 0
-    for count in heads:
-        rows = (2 * count + 1) * ROWS
-        combine_group(count, [r.at[row : row + rows] for r in refs[:-1]], refs[-1], column)
-        row, column = row + rows, column + count
-
-
-def combine_group(heads, parts, out_ref, base):
+    parts, out_ref = refs[:-1], refs[-1]
     stats = [from_three(p[2 * heads * ROWS :, :].astype(jnp.float32)) for p in parts]
     top = functools.reduce(jnp.maximum, stats)
     shares = [jnp.exp2(x - top) for x in stats]
@@ -169,32 +185,32 @@
             own = share[:, 2 * h : 2 * h + 1]
             out = out + own * o
             tangent = tangent + own * t + shift_by[:, 2 * h : 2 * h + 1] * o
-        columns = slice((base + h) * DH, (base + h + 1) * DH)
+        columns = slice(h * DH, (h + 1) * DH)
         out_ref[0:ROWS, columns] = out.astype(jnp.bfloat16)
         out_ref[ROWS : 2 * ROWS, columns] = tangent.astype(jnp.bfloat16)
 
 
-def combine(parts, heads):
+def combine(parts):
+    heads = (parts[0].shape[0] // ROWS - 1) // 2
     return pl.pallas_call(
         functools.partial(combine_kernel, heads),
-        out_shape=jax.ShapeDtypeStruct((2 * ROWS, sum(heads) * DH), jnp.bfloat16),
+        out_shape=jax.ShapeDtypeStruct((2 * ROWS, heads * DH), jnp.bfloat16),
         compiler_params=pltpu.CompilerParams(vmem_limit_bytes=VMEM),
         cost_estimate=SHORT,
     )(*parts)
 
 
-def ring(array, axis):
+def ring(array, axis, beside=()):
     ahead, behind = shift(array, axis, 1), shift(array, axis, -1)
     middle = array.shape[0] // 2
-    far = shift(ahead[:middle], axis, 1), shift(behind[middle:], axis, -1)
+    parts = after((ahead[:middle], behind[middle:]), beside)
+    far = shift(parts[0], axis, 1), shift(parts[1], axis, -1)
     return [array, ahead, behind, far]
 
 
-def in_turn(array, axis, beside=()):
-    found = [array]
-    for by in (1, -1, 2):
-        found.append(shift(after(array, found[-1], beside) if by != 1 else array, axis, by))
-    return found
+def gather(array, axis, beside=()):
+    near = [array, shift(array, axis, 1), shift(array, axis, -1)]
+    return near + [shift(after(array, near, beside), axis, 2)]
 
 
 def give_back(parts, axis):
@@ -226,9 +242,9 @@
     rest[2][...] = both[ROWS:]
 
 
-def project(terms, pieces, weights, places, sums=None):
-    tile = 2 * DH
+def project(terms, pieces, weights, places, tiles, sums=None):
     columns = min(w.shape[1] for w in weights)
+    tile = columns // tiles
     full = lambda a: pl.BlockSpec(a.shape, lambda j, at: (0, 0))
 
     def weight_spec(w):
@@ -307,31 +323,27 @@
     keys_in = other(after(keys_away, query_in), "xh")
     keys_own = ring(keys_own, "y")
     mine, theirs, beside = weight_slices(out_weight)
-    query_own = in_turn(query_own, "z", (mine, theirs, beside, query_in))
+    query_own = gather(query_own, "z", (mine, theirs, beside, query_in))
     mine, theirs = after((mine, theirs), keys_in)
-    keys_in = ring(after(keys_in, keys_own), "y")
-    query_in = after(query_in, query_own)
-    query_in = [query_in, shift(query_in, "z", 1), shift(query_in, "z", -1)]
-    query_in.append(shift(after(query_in[0], query_in), "z", 2))
+    early_own = attend(query_own, keys_own)
+    keys_in = ring(after(keys_in, keys_own), "y", early_own)
+    query_in = gather(after(query_in, query_own), "z")
     mine, theirs = other(mine, "xl"), lax.ppermute(theirs, ("xl", "xh"), DIAGONAL)
 
-    blocks = keys_own + keys_in
-    in_parts = attend(query_in, blocks, 0, 2)
-    pair_parts = attend(after(query_own, in_parts), blocks, 0, 2)
+    in_parts = attend(query_in, keys_in, attend(query_in, keys_own))
+    own_parts = attend(after(query_own, in_parts), keys_in, early_own)
     in_back = give_back(in_parts, "z")
-    own_parts = attend(after(query_own, pair_parts, in_back), blocks, 2, 1, pair_parts)
-    own_back = give_back(own_parts, "z")
-    weights = [out_weight, mine]
-    weights += [other(a, "co") for a in after((beside, theirs), own_parts)]
-    heads_in = combine(after(in_back, weights), (2,))
-    heads_own = combine(own_back, (2, 1))
+    crossed = [other(a, "co") for a in after((beside, theirs), in_parts, mine)]
+    own_back = give_back(after(own_parts, in_back, crossed), "z")
+    weights = [out_weight, mine, *crossed]
+    heads_in = combine(after(in_back, own_parts))
+    heads_own = combine(own_back)
     returned = other(heads_in, "xh")
     returned_far = lax.ppermute(heads_in, ("xl", "xh"), DIAGONAL)
     early = other(jnp.concatenate([returned, returned_far], axis=1), "co")
     beside_own = other(heads_own, "co")
     own_far = other(heads_own, "xl")
-    far_beside = lax.ppermute(heads_own, ("xl", "co"), DIAGONAL)
-    tiles = out_weight.shape[1] // (8 * DH)
+    tiles = 2
     places = jnp.stack([xh, (xl * 2 + co) * tiles]).astype(jnp.int32)
     sums = project(
         (
@@ -347,12 +359,15 @@
         (heads_own, returned, returned_far, early, beside_own),
         weights,
         places,
-    )
+        tiles,
+    )
+    far_beside = other(after(own_far, sums), "co")
     return project(
         ((0, 0, 0, "kept"), (0, PAIR, 0, "fifth"), (1, 0, 1, "kept"), (1, PAIR, 1, "fifth")),
         (own_far, far_beside),
         (weights[1], weights[3]),
         places,
+        1,
         sums,
     )
 

time: 180 us -> 161 us (0.89)
  waiting for transfers between devices: 52.5 us -> 35.6 us
  starting transfers between devices: 55.9 us -> 51.7 us
  Pallas kernels: 61.2 us -> 64.1 us
    ppermute x9 -> x10, waiting for transfers between devices: 14.4 us -> 4.93 us  [other(): return lax.ppermute(array, axis, [(0, 1), (1, 0)])]
    pallas_call x3 -> x4, Pallas kernels: 35.8 us -> 40.9 us  [attend(): pl.pallas_call(functools.partial(attend_kernel, slices, len(blocks), head...]
    ppermute x20, waiting for transfers between devices: 26 us -> 22.5 us  [shift(): lax.ppermute(array, axis, [(i, (i + by) % NEAR) for i in range(NEAR)])]
    ppermute x1, waiting for transfers between devices: 11.1 us -> 8.13 us  [per_device(): returned_far = lax.ppermute(heads_in, ('xl', 'xh'), DIAGONAL)]
    slice x4, local copies, waits for them, and re-layouts: 0.11 us -> 2.84 us  [ring(): parts = after((ahead[:middle], behind[middle:]), beside)]
    unnamed x50 -> x34, local copies, waits for them, and re-layouts: 3.08 us -> 0.82 us
    ppermute x1, starting transfers between devices: 2.48 us -> 0.65 us  [per_device(): returned_far = lax.ppermute(heads_in, ('xl', 'xh'), DIAGONAL)]
    ppermute x9 -> x10, starting transfers between devices: 20.1 us -> 21.2 us  [other(): return lax.ppermute(array, axis, [(0, 1), (1, 0)])]
  transfers between devices with their start and end apart: 32 -> 32, of which waited for: 13 -> 13; matrix products, arithmetic and copies ran while one was open for 3% -> 5% of each run, Pallas kernels for 28% -> 34%
where the time goes in v3:
time: 161 us
  Pallas kernels  64.1 us (40%)
  starting transfers between devices  51.7 us (32%)
  waiting for transfers between devices  35.6 us (22%)
  local copies, waits for them, and re-layouts  8.14 us (5%)
    pallas_call x4, Pallas kernels, attend(): pl.pallas_call(functools.partial(attend_kernel, slices, len(blocks), head...  40.9 us
    ppermute x20, starting transfers between devices, shift(): lax.ppermute(array, axis, [(i, (i + by) % NEAR) for i in range(NEAR)])  28.8 us
    ppermute x20, waiting for transfers between devices, shift(): lax.ppermute(array, axis, [(i, (i + by) % NEAR) for i in range(NEAR)])  22.5 us
    ppermute x10, starting transfers between devices, other(): return lax.ppermute(array, axis, [(0, 1), (1, 0)])  21.2 us
    pallas_call x2, Pallas kernels, project(): pl.pallas_call(functools.partial(project_kernel, terms, len(pieces), len(...  13.5 us
    ppermute x1, waiting for transfers between devices, per_device(): returned_far = lax.ppermute(heads_in, ('xl', 'xh'), DIAGONAL)  8.13 us
    pallas_call x2, Pallas kernels, combine(): pl.pallas_call(functools.partial(combine_kernel, heads), out_shape=jax.Sh...  6.44 us
    ppermute x10, waiting for transfers between devices, other(): return lax.ppermute(array, axis, [(0, 1), (1, 0)])  4.93 us
  transfers between devices with their start and end apart: 32, of which 13 were waited for; matrix products, arithmetic and copies ran while one was open for 5% of the time, Pallas kernels for 34%

profile of v3, /device:TPU:1, one launch (start us, length us, event | category | flops | bytes accessed | tf_op | source)
XLA Modules:
  0.0 161.1 jit_solution(11287863713138890186)
XLA Ops:
  0.6 3.2 %shard_map.86 = (bf16[3072,128]{1,0:T(8,128)(2,1)}, bf16[1024,128]{1,0:T(8,128)(2,1)}, bf16[3072,128]{1,0:T(8,128)(2,1)}, bf16[1536,128]{1,0:T(8,128)(2,1)}) custom-call(s32[1]{0:T(128)} %bitcast.at_ref, bf16[256,640]{1,0:T(8,128)(2,1)} %refs_0_.1, bf16[256,640]{1,0:T(8,128)(2,1)} %refs_1_.1, bf16[256,640]{1,0:T(8,128)(2,1)} %refs_2_.1, ...), custom_call_target="tpu_custom_call" | custom-call | flops 1 | bytes 1 | tf_op jit(solution)/shard_map/pallas_call | solution.py:304
  3.9 3.6 %collective-permute-start.2 = (bf16[1024,128]{1,0:T(8,128)(2,1)}, bf16[1024,128]{1,0:T(8,128)(2,1)S(1)}, u32[]{:S(2)}, u32[]{:S(2)}) collective-permute-start(bf16[1024,128]{1,0:T(8,128)(2,1)} %get-tuple-element.49), channel_id=1, source_target_pairs={{0,16},{16,0},{1,17},{17,1},{2,18},{18,2},{3,19},{19,3},{4,20},{20... | collective-permute-start | bytes 786440 | tf_op jit(solution)/shard_map/ppermute | solution.py:29
  11.8 2.1 %collective-permute-start.1 = (bf16[1536,128]{1,0:T(8,128)(2,1)}, bf16[1536,128]{1,0:T(8,128)(2,1)}, u32[]{:S(2)}, u32[]{:S(2)}) collective-permute-start(bf16[1536,128]{1,0:T(8,128)(2,1)} %get-tuple-element.73.refs_0_), channel_id=1, source_target_pairs={{0,3},{1,0},{2,1},{3,2},{4,7},{5,4},{6,5},{7,6},{8,11},{9,8},{10,9... | collective-permute-start | bytes 1179656 | tf_op jit(solution)/shard_map/ppermute | solution.py:25
  13.9 2.4 %collective-permute-start.7 = (bf16[3072,128]{1,0:T(8,128)(2,1)}, bf16[3072,128]{1,0:T(8,128)(2,1)}, u32[]{:S(2)}, u32[]{:S(2)}) collective-permute-start(bf16[3072,128]{1,0:T(8,128)(2,1)} %get-tuple-element.54), channel_id=1, source_target_pairs={{0,16},{16,0},{1,17},{17,1},{2,18},{18,2},{3,19},{19,3},{4,20},{20... | collective-permute-start | bytes 2359304 | tf_op jit(solution)/shard_map/ppermute | solution.py:29
  16.3 4.5 %constant_dynamic-slice_fusion = (bf16[640,1280]{1,0:T(8,128)(2,1)}, bf16[640,1280]{1,0:T(8,128)(2,1)}, bf16[640,1280]{1,0:T(8,128)(2,1)S(1)}) fusion(bf16[640,5120]{1,0:T(8,128)(2,1)} %refs_5_.3, s32[]{:T(128)S(6)} %select_n.11, s32[]{:T(128)S(6)} %select_n.10, s32[]{:T(128)S(6)} %select_n.9), kind=kLoop, calls=%fused_computation.1 | loop fusion | bytes 9830412 | tf_op jit(solution)/shard_map/dynamic_slice | solution.py:279
  22.2 2.3 %collective-permute-start.3 = (bf16[1536,128]{1,0:T(8,128)(2,1)S(1)}, bf16[1536,128]{1,0:T(8,128)(2,1)S(1)}, u32[]{:S(2)}, u32[]{:S(2)}) collective-permute-start(bf16[1536,128]{1,0:T(8,128)(2,1)S(1)} %copy-done.10), channel_id=1, source_target_pairs={{0,2},{1,3},{2,0},{3,1},{4,6},{5,7},{6,4},{7,5},{8,10},{9,11},{10,... | collective-permute-start | bytes 1179656 | tf_op jit(solution)/shard_map/ppermute | solution.py:25
  24.5 2.7 %collective-permute-done.8.refs_5_.refs_9_ = bf16[3072,128]{1,0:T(8,128)(2,1)S(1)} collective-permute-done((bf16[3072,128]{1,0:T(8,128)(2,1)}, bf16[3072,128]{1,0:T(8,128)(2,1)S(1)}, u32[]{:S(2)}, u32[]{:S(2)}) %collective-permute-start.8) | collective-permute-done | bytes 786464 | tf_op jit(solution)/shard_map/ppermute | solution.py:25
  28.2 1.8 %collective-permute-start.11 = (bf16[1536,128]{1,0:T(8,128)(2,1)S(1)}, bf16[1536,128]{1,0:T(8,128)(2,1)S(1)}, u32[]{:S(2)}, u32[]{:S(2)}) collective-permute-start(bf16[1536,128]{1,0:T(8,128)(2,1)S(1)} %slice.17), channel_id=1, source_target_pairs={{0,12},{4,0},{8,4},{12,8},{1,13},{5,1},{9,5},{13,9},{2,14},{6,2},{... | collective-permute-start | bytes 1179656 | tf_op jit(solution)/shard_map/ppermute | solution.py:25
  30.0 2.3 %collective-permute-done.3.refs_3_ = bf16[1536,128]{1,0:T(8,128)(2,1)S(1)} collective-permute-done((bf16[1536,128]{1,0:T(8,128)(2,1)S(1)}, bf16[1536,128]{1,0:T(8,128)(2,1)S(1)}, u32[]{:S(2)}, u32[]{:S(2)}) %collective-permute-start.3) | collective-permute-done | bytes 393248 | tf_op jit(solution)/shard_map/ppermute | solution.py:25
  32.3 2.7 %collective-permute-start.5 = (bf16[1024,128]{1,0:T(8,128)(2,1)S(1)}, bf16[1024,128]{1,0:T(8,128)(2,1)S(1)}, u32[]{:S(2)}, u32[]{:S(2)}) collective-permute-start(bf16[1024,128]{1,0:T(8,128)(2,1)S(1)} %collective-permute-done.2.refs_0_), channel_id=1, source_target_pairs={{0,3},{1,0},{2,1},{3,2},{4,7},{5,4},{6,5},{7,6},{8,11},{9,8},{10,9... | collective-permute-start | bytes 786440 | tf_op jit(solution)/shard_map/ppermute | solution.py:25
  35.0 4.1 %collective-permute-done.4.refs_1_ = bf16[1024,128]{1,0:T(8,128)(2,1)S(1)} collective-permute-done((bf16[1024,128]{1,0:T(8,128)(2,1)S(1)}, bf16[1024,128]{1,0:T(8,128)(2,1)S(1)}, u32[]{:S(2)}, u32[]{:S(2)}) %collective-permute-start.4) | collective-permute-done | bytes 262176 | tf_op jit(solution)/shard_map/ppermute | solution.py:25
  39.1 2.1 %collective-permute-start.6 = (bf16[1024,128]{1,0:T(8,128)(2,1)S(1)}, bf16[1024,128]{1,0:T(8,128)(2,1)}, u32[]{:S(2)}, u32[]{:S(2)}) collective-permute-start(bf16[1024,128]{1,0:T(8,128)(2,1)S(1)} %collective-permute-done.2.refs_0_), channel_id=1, source_target_pairs={{0,2},{1,3},{2,0},{3,1},{4,6},{5,7},{6,4},{7,5},{8,10},{9,11},{10,... | collective-permute-start | bytes 786440 | tf_op jit(solution)/shard_map/ppermute | solution.py:25
  42.2 1.9 %collective-permute-start.12 = (bf16[3072,128]{1,0:T(8,128)(2,1)}, bf16[3072,128]{1,0:T(8,128)(2,1)}, u32[]{:S(2)}, u32[]{:S(2)}) collective-permute-start(bf16[3072,128]{1,0:T(8,128)(2,1)} %collective-permute-done.7.refs_4_.refs_8_), channel_id=1, source_target_pairs={{0,4},{4,8},{8,12},{12,0},{1,5},{5,9},{9,13},{13,1},{2,6},{6,10},{... | collective-permute-start | bytes 2359304 | tf_op jit(solution)/shard_map/ppermute | solution.py:25
  44.1 2.2 %collective-permute-start.13 = (bf16[3072,128]{1,0:T(8,128)(2,1)}, bf16[3072,128]{1,0:T(8,128)(2,1)}, u32[]{:S(2)}, u32[]{:S(2)}) collective-permute-start(bf16[3072,128]{1,0:T(8,128)(2,1)} %collective-permute-done.7.refs_4_.refs_8_), channel_id=1, source_target_pairs={{0,12},{4,0},{8,4},{12,8},{1,13},{5,1},{9,5},{13,9},{2,14},{6,2},{... | collective-permute-start | bytes 2359304 | tf_op jit(solution)/shard_map/ppermute | solution.py:25
  46.3 11.0 %shard_map.87 = (bf16[1792,128]{1,0:T(8,128)(2,1)}, bf16[1792,128]{1,0:T(8,128)(2,1)}, bf16[1792,128]{1,0:T(8,128)(2,1)}, bf16[1792,128]{1,0:T(8,128)(2,1)}) custom-call(bf16[1536,128]{1,0:T(8,128)(2,1)} %get-tuple-element.73.refs_0_, bf16[1536,128]{1,0:T(8,128)(2,1)} %collective-permute-done.refs_1_, bf16[1536,128]{1,0:T(8,128)(2,1)} %collective-permute-done.1.refs_2_, ...), custom_call_target="tpu_custom_call" | custom-call | flops 12884901888 | bytes 7864320 | tf_op jit(solution)/shard_map/pallas_call | solution.py:152
  59.4 1.8 %slice.19 = bf16[1536,128]{1,0:T(8,128)(2,1)} slice(bf16[3072,128]{1,0:T(8,128)(2,1)} %collective-permute-done.13.refs_6_.refs_10_), slice={[1536:3072], [0:128]} | slice | bytes 786432 | tf_op jit(solution)/shard_map/slice | solution.py:206
  61.8 2.2 %collective-permute-start.15 = (bf16[1536,128]{1,0:T(8,128)(2,1)}, bf16[1536,128]{1,0:T(8,128)(2,1)}, u32[]{:S(2)}, u32[]{:S(2)}) collective-permute-start(bf16[1536,128]{1,0:T(8,128)(2,1)} %slice.19), channel_id=1, source_target_pairs={{0,12},{4,0},{8,4},{12,8},{1,13},{5,1},{9,5},{13,9},{2,14},{6,2},{... | collective-permute-start | bytes 1179656 | tf_op jit(solution)/shard_map/ppermute | solution.py:25
  64.0 8.0 %shard_map.88 = (bf16[1280,128]{1,0:T(8,128)(2,1)}, bf16[1280,128]{1,0:T(8,128)(2,1)}, bf16[1280,128]{1,0:T(8,128)(2,1)}, bf16[1280,128]{1,0:T(8,128)(2,1)}) custom-call(bf16[1024,128]{1,0:T(8,128)(2,1)} %copy-done.14, bf16[1024,128]{1,0:T(8,128)(2,1)} %copy-done.15, bf16[1024,128]{1,0:T(8,128)(2,1)} %copy-done.16, ...), custom_call_target="tpu_custom_call" | custom-call | flops 8589934592 | bytes 5242880 | tf_op jit(solution)/shard_map/pallas_call | solution.py:152
  72.0 9.2 %shard_map.89 = (bf16[1280,128]{1,0:T(8,128)(2,1)}, bf16[1280,128]{1,0:T(8,128)(2,1)}, bf16[1280,128]{1,0:T(8,128)(2,1)}, bf16[1280,128]{1,0:T(8,128)(2,1)}) custom-call(bf16[1024,128]{1,0:T(8,128)(2,1)} %copy-done.14, bf16[1024,128]{1,0:T(8,128)(2,1)} %copy-done.15, bf16[1024,128]{1,0:T(8,128)(2,1)} %copy-done.16, ...), custom_call_target="tpu_custom_call" | custom-call | flops 8589934592 | bytes 5242880 | tf_op jit(solution)/shard_map/pallas_call | solution.py:152
  81.3 6.5 %collective-permute-start.21 = (bf16[640,1280]{1,0:T(8,128)(2,1)}, bf16[640,1280]{1,0:T(8,128)(2,1)}, u32[]{:S(2)}, u32[]{:S(2)}) collective-permute-start(bf16[640,1280]{1,0:T(8,128)(2,1)} %get-tuple-element.83), channel_id=1, source_target_pairs={{0,32},{32,0},{1,33},{33,1},{2,34},{34,2},{3,35},{35,3},{4,36},{36... | collective-permute-start | bytes 4915208 | tf_op jit(solution)/shard_map/ppermute | solution.py:29
  90.2 12.7 %shard_map.90 = (bf16[1792,128]{1,0:T(8,128)(2,1)}, bf16[1792,128]{1,0:T(8,128)(2,1)}, bf16[1792,128]{1,0:T(8,128)(2,1)}, bf16[1792,128]{1,0:T(8,128)(2,1)}) custom-call(bf16[1536,128]{1,0:T(8,128)(2,1)} %get-tuple-element.73.refs_0_, bf16[1536,128]{1,0:T(8,128)(2,1)} %collective-permute-done.refs_1_, bf16[1536,128]{1,0:T(8,128)(2,1)} %collective-permute-done.1.refs_2_, ...), custom_call_target="tpu_custom_call" | custom-call | flops 12884901888 | bytes 7864320 | tf_op jit(solution)/shard_map/pallas_call | solution.py:152
  103.0 2.0 %collective-permute-done.18.refs_3_ = bf16[1280,128]{1,0:T(8,128)(2,1)} collective-permute-done((bf16[1280,128]{1,0:T(8,128)(2,1)}, bf16[1280,128]{1,0:T(8,128)(2,1)}, u32[]{:S(2)}, u32[]{:S(2)}) %collective-permute-start.18) | collective-permute-done | bytes 327712 | tf_op jit(solution)/shard_map/ppermute | solution.py:25
  105.0 3.0 %shard_map.92 = bf16[512,256]{1,0:T(8,128)(2,1)} custom-call(bf16[1280,128]{1,0:T(8,128)(2,1)} %get-tuple-element.89.refs_0_, bf16[1280,128]{1,0:T(8,128)(2,1)} %copy-done.7, bf16[1280,128]{1,0:T(8,128)(2,1)} %collective-permute-done.17.refs_2_, bf16[1280,128]{1,0:T(8,128)(2,1)} %collective-permute-done.18.refs_3_), custom_call_target="tpu_custom_call" | custom-call | flops 1 | bytes 1 | tf_op jit(solution)/shard_map/pallas_call | solution.py:195
  108.0 3.2 %collective-permute-start.27 = (bf16[512,256]{1,0:T(8,128)(2,1)}, bf16[512,256]{1,0:T(8,128)(2,1)S(1)}, u32[]{:S(2)}, u32[]{:S(2)}) collective-permute-start(bf16[512,256]{1,0:T(8,128)(2,1)} %shard_map.92), channel_id=1, source_target_pairs={{0,16},{16,0},{1,17},{17,1},{2,18},{18,2},{3,19},{19,3},{4,20},{20... | collective-permute-start | bytes 786440 | tf_op jit(solution)/shard_map/ppermute | solution.py:29
  113.4 1.7 %collective-permute-start.25 = (bf16[1792,128]{1,0:T(8,128)(2,1)}, bf16[1792,128]{1,0:T(8,128)(2,1)}, u32[]{:S(2)}, u32[]{:S(2)}) collective-permute-start(bf16[1792,128]{1,0:T(8,128)(2,1)} %get-tuple-element.88), channel_id=1, source_target_pairs={{0,2},{1,3},{2,0},{3,1},{4,6},{5,7},{6,4},{7,5},{8,10},{9,11},{10,... | collective-permute-start | bytes 1376264 | tf_op jit(solution)/shard_map/ppermute | solution.py:25
  115.7 8.1 %collective-permute-done.28.refs_2_ = bf16[512,256]{1,0:T(8,128)(2,1)S(1)} collective-permute-done((bf16[512,256]{1,0:T(8,128)(2,1)}, bf16[512,256]{1,0:T(8,128)(2,1)S(1)}, u32[]{:S(2)}, u32[]{:S(2)}) %collective-permute-start.28) | collective-permute-done | bytes 262176 | tf_op jit(solution)/shard_map/ppermute | solution.py:342
  126.0 7.3 %collective-permute-done.25.refs_3_ = bf16[1792,128]{1,0:T(8,128)(2,1)} collective-permute-done((bf16[1792,128]{1,0:T(8,128)(2,1)}, bf16[1792,128]{1,0:T(8,128)(2,1)}, u32[]{:S(2)}, u32[]{:S(2)}) %collective-permute-start.25) | collective-permute-done | bytes 458784 | tf_op jit(solution)/shard_map/ppermute | solution.py:25
  133.4 3.5 %shard_map.91.refs_0_ = bf16[512,384]{1,0:T(8,128)(2,1)} custom-call(bf16[1792,128]{1,0:T(8,128)(2,1)} %get-tuple-element.85.refs_0_, bf16[1792,128]{1,0:T(8,128)(2,1)} %copy-done.5, bf16[1792,128]{1,0:T(8,128)(2,1)} %collective-permute-done.24.refs_2_, bf16[1792,128]{1,0:T(8,128)(2,1)} %collective-permute-done.25.refs_3_), custom_call_target="tpu_custom_call" | custom-call | flops 1 | bytes 1 | tf_op jit(solution)/shard_map/pallas_call | solution.py:195
  136.8 4.3 %collective-permute-start.30 = (bf16[512,384]{1,0:T(8,128)(2,1)}, bf16[512,384]{1,0:T(8,128)(2,1)}, u32[]{:S(2)}, u32[]{:S(2)}) collective-permute-start(bf16[512,384]{1,0:T(8,128)(2,1)} %shard_map.91.refs_0_), channel_id=1, source_target_pairs={{0,32},{32,0},{1,33},{33,1},{2,34},{34,2},{3,35},{35,3},{4,36},{36... | collective-permute-start | bytes 1179656 | tf_op jit(solution)/shard_map/ppermute | solution.py:29
  142.8 7.7 %shard_map.93.refs_4_ = f32[512,1280]{1,0:T(8,128)} custom-call(s32[2]{0:T(128)} %pad_add_fusion.at_ref, bf16[512,384]{1,0:T(8,128)(2,1)} %shard_map.91.refs_0_, bf16[512,256]{1,0:T(8,128)(2,1)} %copy-done.2, bf16[512,256]{1,0:T(8,128)(2,1)} %copy-done.3, bf16[512,512]{1,0:T(8,128)(2,1)} %copy-done.4, bf16[512,384]{1,0:T(8,128)(2,1)} %collective-permute-done.30.refs_4_, ...), custom_call_target="tpu_custom_call" | custom-call | flops 1 | bytes 1 | tf_op jit(solution)/shard_map/pallas_call | solution.py:259
  150.5 1.6 %collective-permute-done.26.refs_0_ = bf16[512,384]{1,0:T(8,128)(2,1)} collective-permute-done((bf16[512,384]{1,0:T(8,128)(2,1)}, bf16[512,384]{1,0:T(8,128)(2,1)}, u32[]{:S(2)}, u32[]{:S(2)}) %collective-permute-start.26) | collective-permute-done | bytes 393248 | tf_op jit(solution)/shard_map/ppermute | solution.py:29
  155.3 5.8 %shard_map.94 = (bf16[256,1280]{1,0:T(8,128)(2,1)}, bf16[256,1280]{1,0:T(8,128)(2,1)}) custom-call(s32[2]{0:T(128)} %pad_add_fusion.at_ref, bf16[512,384]{1,0:T(8,128)(2,1)} %collective-permute-done.26.refs_0_, bf16[512,384]{1,0:T(8,128)(2,1)} %copy-done.6, bf16[640,1280]{1,0:T(8,128)(2,1)} %copy-done, bf16[640,1280]{1,0:T(8,128)(2,1)} %copy-done.1, ...), custom_call_target="tpu_custom_call" | custom-call | flops 1 | bytes 1 | tf_op jit(solution)/shard_map/pallas_call | solution.py:259
  (82 shorter events, 22.9 us)
Async XLA Ops:
  3.9 10.1 %collective-permute-start.2 = (bf16[1024,128]{1,0:T(8,128)(2,1)}, bf16[1024,128]{1,0:T(8,128)(2,1)S(1)}, u32[]{:S(2)}, u32[]{:S(2)}) collective-permute-start(bf16[1024,128]{1,0:T(8,128)(2,1)} %get-tuple-element.49), channel_id=1, source_target_pairs={{0,16},{16,0},{1,17},{17,1},{2,18},{18,2},{3,19},{19,3},{4,20},{20... | collective-permute-start | bytes 786440 | tf_op jit(solution)/shard_map/ppermute | solution.py:29
  7.4 19.7 %collective-permute-start.8 = (bf16[3072,128]{1,0:T(8,128)(2,1)}, bf16[3072,128]{1,0:T(8,128)(2,1)S(1)}, u32[]{:S(2)}, u32[]{:S(2)}) collective-permute-start(bf16[3072,128]{1,0:T(8,128)(2,1)} %get-tuple-element.55.refs_4_.refs_8_), channel_id=1, source_target_pairs={{0,4},{4,8},{8,12},{12,0},{1,5},{5,9},{9,13},{13,1},{2,6},{6,10},{... | collective-permute-start | bytes 2359304 | tf_op jit(solution)/shard_map/ppermute | solution.py:25
  8.7 18.5 %collective-permute-start.9 = (bf16[3072,128]{1,0:T(8,128)(2,1)}, bf16[3072,128]{1,0:T(8,128)(2,1)S(1)}, u32[]{:S(2)}, u32[]{:S(2)}) collective-permute-start(bf16[3072,128]{1,0:T(8,128)(2,1)} %get-tuple-element.55.refs_4_.refs_8_), channel_id=1, source_target_pairs={{0,12},{4,0},{8,4},{12,8},{1,13},{5,1},{9,5},{13,9},{2,14},{6,2},{... | collective-permute-start | bytes 2359304 | tf_op jit(solution)/shard_map/ppermute | solution.py:25
  10.2 12.0 %collective-permute-start = (bf16[1536,128]{1,0:T(8,128)(2,1)}, bf16[1536,128]{1,0:T(8,128)(2,1)}, u32[]{:S(2)}, u32[]{:S(2)}) collective-permute-start(bf16[1536,128]{1,0:T(8,128)(2,1)} %get-tuple-element.73.refs_0_), channel_id=1, source_target_pairs={{0,1},{1,2},{2,3},{3,0},{4,5},{5,6},{6,7},{7,4},{8,9},{9,10},{10,1... | collective-permute-start | bytes 1179656 | tf_op jit(solution)/shard_map/ppermute | solution.py:25
  11.8 10.4 %collective-permute-start.1 = (bf16[1536,128]{1,0:T(8,128)(2,1)}, bf16[1536,128]{1,0:T(8,128)(2,1)}, u32[]{:S(2)}, u32[]{:S(2)}) collective-permute-start(bf16[1536,128]{1,0:T(8,128)(2,1)} %get-tuple-element.73.refs_0_), channel_id=1, source_target_pairs={{0,3},{1,0},{2,1},{3,2},{4,7},{5,4},{6,5},{7,6},{8,11},{9,8},{10,9... | collective-permute-start | bytes 1179656 | tf_op jit(solution)/shard_map/ppermute | solution.py:25
  13.9 27.3 %collective-permute-start.7 = (bf16[3072,128]{1,0:T(8,128)(2,1)}, bf16[3072,128]{1,0:T(8,128)(2,1)}, u32[]{:S(2)}, u32[]{:S(2)}) collective-permute-start(bf16[3072,128]{1,0:T(8,128)(2,1)} %get-tuple-element.54), channel_id=1, source_target_pairs={{0,16},{16,0},{1,17},{17,1},{2,18},{18,2},{3,19},{19,3},{4,20},{20... | collective-permute-start | bytes 2359304 | tf_op jit(solution)/shard_map/ppermute | solution.py:29
  22.2 10.1 %collective-permute-start.3 = (bf16[1536,128]{1,0:T(8,128)(2,1)S(1)}, bf16[1536,128]{1,0:T(8,128)(2,1)S(1)}, u32[]{:S(2)}, u32[]{:S(2)}) collective-permute-start(bf16[1536,128]{1,0:T(8,128)(2,1)S(1)} %copy-done.10), channel_id=1, source_target_pairs={{0,2},{1,3},{2,0},{3,1},{4,6},{5,7},{6,4},{7,5},{8,10},{9,11},{10,... | collective-permute-start | bytes 1179656 | tf_op jit(solution)/shard_map/ppermute | solution.py:25
  27.3 14.9 %collective-permute-start.10 = (bf16[1536,128]{1,0:T(8,128)(2,1)S(1)}, bf16[1536,128]{1,0:T(8,128)(2,1)S(1)}, u32[]{:S(2)}, u32[]{:S(2)}) collective-permute-start(bf16[1536,128]{1,0:T(8,128)(2,1)S(1)} %slice.16), channel_id=1, source_target_pairs={{0,4},{4,8},{8,12},{12,0},{1,5},{5,9},{9,13},{13,1},{2,6},{6,10},{... | collective-permute-start | bytes 1179656 | tf_op jit(solution)/shard_map/ppermute | solution.py:25
  28.2 14.0 %collective-permute-start.11 = (bf16[1536,128]{1,0:T(8,128)(2,1)S(1)}, bf16[1536,128]{1,0:T(8,128)(2,1)S(1)}, u32[]{:S(2)}, u32[]{:S(2)}) collective-permute-start(bf16[1536,128]{1,0:T(8,128)(2,1)S(1)} %slice.17), channel_id=1, source_target_pairs={{0,12},{4,0},{8,4},{12,8},{1,13},{5,1},{9,5},{13,9},{2,14},{6,2},{... | collective-permute-start | bytes 1179656 | tf_op jit(solution)/shard_map/ppermute | solution.py:25
  32.3 6.7 %collective-permute-start.4 = (bf16[1024,128]{1,0:T(8,128)(2,1)S(1)}, bf16[1024,128]{1,0:T(8,128)(2,1)S(1)}, u32[]{:S(2)}, u32[]{:S(2)}) collective-permute-start(bf16[1024,128]{1,0:T(8,128)(2,1)S(1)} %collective-permute-done.2.refs_0_), channel_id=1, source_target_pairs={{0,1},{1,2},{2,3},{3,0},{4,5},{5,6},{6,7},{7,4},{8,9},{9,10},{10,1... | collective-permute-start | bytes 786440 | tf_op jit(solution)/shard_map/ppermute | solution.py:25
  32.3 6.7 %collective-permute-start.5 = (bf16[1024,128]{1,0:T(8,128)(2,1)S(1)}, bf16[1024,128]{1,0:T(8,128)(2,1)S(1)}, u32[]{:S(2)}, u32[]{:S(2)}) collective-permute-start(bf16[1024,128]{1,0:T(8,128)(2,1)S(1)} %collective-permute-done.2.refs_0_), channel_id=1, source_target_pairs={{0,3},{1,0},{2,1},{3,2},{4,7},{5,4},{6,5},{7,6},{8,11},{9,8},{10,9... | collective-permute-start | bytes 786440 | tf_op jit(solution)/shard_map/ppermute | solution.py:25
  39.1 24.9 %collective-permute-start.6 = (bf16[1024,128]{1,0:T(8,128)(2,1)S(1)}, bf16[1024,128]{1,0:T(8,128)(2,1)}, u32[]{:S(2)}, u32[]{:S(2)}) collective-permute-start(bf16[1024,128]{1,0:T(8,128)(2,1)S(1)} %collective-permute-done.2.refs_0_), channel_id=1, source_target_pairs={{0,2},{1,3},{2,0},{3,1},{4,6},{5,7},{6,4},{7,5},{8,10},{9,11},{10,... | collective-permute-start | bytes 786440 | tf_op jit(solution)/shard_map/ppermute | solution.py:25
  41.3 40.0 %collective-permute-start.19 = (bf16[640,1280]{1,0:T(8,128)(2,1)}, bf16[640,1280]{1,0:T(8,128)(2,1)}, u32[]{:S(2)}, u32[]{:S(2)}) collective-permute-start(bf16[640,1280]{1,0:T(8,128)(2,1)} %get-tuple-element.81), channel_id=1, source_target_pairs={{0,80},{16,64},{64,16},{80,0},{1,81},{17,65},{65,17},{81,1},{2,82}... | collective-permute-start | bytes 4915208 | tf_op jit(solution)/shard_map/ppermute | solution.py:331
  42.2 39.1 %collective-permute-start.20 = (bf16[640,1280]{1,0:T(8,128)(2,1)S(1)}, bf16[640,1280]{1,0:T(8,128)(2,1)S(1)}, u32[]{:S(2)}, u32[]{:S(2)}) collective-permute-start(bf16[640,1280]{1,0:T(8,128)(2,1)S(1)} %get-tuple-element.82), channel_id=1, source_target_pairs={{0,64},{64,0},{1,65},{65,1},{2,66},{66,2},{3,67},{67,3},{4,68},{68... | collective-permute-start | bytes 4915208 | tf_op jit(solution)/shard_map/ppermute | solution.py:29
  42.2 16.1 %collective-permute-start.12 = (bf16[3072,128]{1,0:T(8,128)(2,1)}, bf16[3072,128]{1,0:T(8,128)(2,1)}, u32[]{:S(2)}, u32[]{:S(2)}) collective-permute-start(bf16[3072,128]{1,0:T(8,128)(2,1)} %collective-permute-done.7.refs_4_.refs_8_), channel_id=1, source_target_pairs={{0,4},{4,8},{8,12},{12,0},{1,5},{5,9},{9,13},{13,1},{2,6},{6,10},{... | collective-permute-start | bytes 2359304 | tf_op jit(solution)/shard_map/ppermute | solution.py:25
  44.1 15.3 %collective-permute-start.13 = (bf16[3072,128]{1,0:T(8,128)(2,1)}, bf16[3072,128]{1,0:T(8,128)(2,1)}, u32[]{:S(2)}, u32[]{:S(2)}) collective-permute-start(bf16[3072,128]{1,0:T(8,128)(2,1)} %collective-permute-done.7.refs_4_.refs_8_), channel_id=1, source_target_pairs={{0,12},{4,0},{8,4},{12,8},{1,13},{5,1},{9,5},{13,9},{2,14},{6,2},{... | collective-permute-start | bytes 2359304 | tf_op jit(solution)/shard_map/ppermute | solution.py:25
  61.2 10.8 %collective-permute-start.14 = (bf16[1536,128]{1,0:T(8,128)(2,1)S(1)}, bf16[1536,128]{1,0:T(8,128)(2,1)}, u32[]{:S(2)}, u32[]{:S(2)}) collective-permute-start(bf16[1536,128]{1,0:T(8,128)(2,1)S(1)} %slice.18), channel_id=1, source_target_pairs={{0,4},{4,8},{8,12},{12,0},{1,5},{5,9},{9,13},{13,1},{2,6},{6,10},{... | collective-permute-start | bytes 1179656 | tf_op jit(solution)/shard_map/ppermute | solution.py:25
  61.8 10.2 %collective-permute-start.15 = (bf16[1536,128]{1,0:T(8,128)(2,1)}, bf16[1536,128]{1,0:T(8,128)(2,1)}, u32[]{:S(2)}, u32[]{:S(2)}) collective-permute-start(bf16[1536,128]{1,0:T(8,128)(2,1)} %slice.19), channel_id=1, source_target_pairs={{0,12},{4,0},{8,4},{12,8},{1,13},{5,1},{9,5},{13,9},{2,14},{6,2},{... | collective-permute-start | bytes 1179656 | tf_op jit(solution)/shard_map/ppermute | solution.py:25
  81.3 30.6 %collective-permute-start.21 = (bf16[640,1280]{1,0:T(8,128)(2,1)}, bf16[640,1280]{1,0:T(8,128)(2,1)}, u32[]{:S(2)}, u32[]{:S(2)}) collective-permute-start(bf16[640,1280]{1,0:T(8,128)(2,1)} %get-tuple-element.83), channel_id=1, source_target_pairs={{0,32},{32,0},{1,33},{33,1},{2,34},{34,2},{3,35},{35,3},{4,36},{36... | collective-permute-start | bytes 4915208 | tf_op jit(solution)/shard_map/ppermute | solution.py:29
  87.7 24.1 %collective-permute-start.22 = (bf16[640,1280]{1,0:T(8,128)(2,1)}, bf16[640,1280]{1,0:T(8,128)(2,1)S(1)}, u32[]{:S(2)}, u32[]{:S(2)}) collective-permute-start(bf16[640,1280]{1,0:T(8,128)(2,1)} %collective-permute-done.19), channel_id=1, source_target_pairs={{0,32},{32,0},{1,33},{33,1},{2,34},{34,2},{3,35},{35,3},{4,36},{36... | collective-permute-start | bytes 4915208 | tf_op jit(solution)/shard_map/ppermute | solution.py:29
  87.8 15.1 %collective-permute-start.16 = (bf16[1280,128]{1,0:T(8,128)(2,1)}, bf16[1280,128]{1,0:T(8,128)(2,1)S(1)}, u32[]{:S(2)}, u32[]{:S(2)}) collective-permute-start(bf16[1280,128]{1,0:T(8,128)(2,1)} %get-tuple-element.70), channel_id=1, source_target_pairs={{0,3},{1,0},{2,1},{3,2},{4,7},{5,4},{6,5},{7,6},{8,11},{9,8},{10,9... | collective-permute-start | bytes 983048 | tf_op jit(solution)/shard_map/ppermute | solution.py:25
  88.6 14.4 %collective-permute-start.17 = (bf16[1280,128]{1,0:T(8,128)(2,1)}, bf16[1280,128]{1,0:T(8,128)(2,1)}, u32[]{:S(2)}, u32[]{:S(2)}) collective-permute-start(bf16[1280,128]{1,0:T(8,128)(2,1)} %get-tuple-element.71), channel_id=1, source_target_pairs={{0,1},{1,2},{2,3},{3,0},{4,5},{5,6},{6,7},{7,4},{8,9},{9,10},{10,1... | collective-permute-start | bytes 983048 | tf_op jit(solution)/shard_map/ppermute | solution.py:25
  89.3 15.7 %collective-permute-start.18 = (bf16[1280,128]{1,0:T(8,128)(2,1)}, bf16[1280,128]{1,0:T(8,128)(2,1)}, u32[]{:S(2)}, u32[]{:S(2)}) collective-permute-start(bf16[1280,128]{1,0:T(8,128)(2,1)} %get-tuple-element.72), channel_id=1, source_target_pairs={{0,2},{1,3},{2,0},{3,1},{4,6},{5,7},{6,4},{7,5},{8,10},{9,11},{10,... | collective-permute-start | bytes 983048 | tf_op jit(solution)/shard_map/ppermute | solution.py:25
  108.0 7.8 %collective-permute-start.27 = (bf16[512,256]{1,0:T(8,128)(2,1)}, bf16[512,256]{1,0:T(8,128)(2,1)S(1)}, u32[]{:S(2)}, u32[]{:S(2)}) collective-permute-start(bf16[512,256]{1,0:T(8,128)(2,1)} %shard_map.92), channel_id=1, source_target_pairs={{0,16},{16,0},{1,17},{17,1},{2,18},{18,2},{3,19},{19,3},{4,20},{20... | collective-permute-start | bytes 786440 | tf_op jit(solution)/shard_map/ppermute | solution.py:29
  111.2 12.7 %collective-permute-start.28 = (bf16[512,256]{1,0:T(8,128)(2,1)}, bf16[512,256]{1,0:T(8,128)(2,1)S(1)}, u32[]{:S(2)}, u32[]{:S(2)}) collective-permute-start(bf16[512,256]{1,0:T(8,128)(2,1)} %shard_map.92), channel_id=1, source_target_pairs={{0,80},{16,64},{64,16},{80,0},{1,81},{17,65},{65,17},{81,1},{2,82}... | collective-permute-start | bytes 786440 | tf_op jit(solution)/shard_map/ppermute | solution.py:342
  111.9 12.5 %collective-permute-start.23 = (bf16[1792,128]{1,0:T(8,128)(2,1)}, bf16[1792,128]{1,0:T(8,128)(2,1)S(1)}, u32[]{:S(2)}, u32[]{:S(2)}) collective-permute-start(bf16[1792,128]{1,0:T(8,128)(2,1)} %get-tuple-element.86), channel_id=1, source_target_pairs={{0,3},{1,0},{2,1},{3,2},{4,7},{5,4},{6,5},{7,6},{8,11},{9,8},{10,9... | collective-permute-start | bytes 1376264 | tf_op jit(solution)/shard_map/ppermute | solution.py:25
  113.3 12.7 %collective-permute-start.24 = (bf16[1792,128]{1,0:T(8,128)(2,1)}, bf16[1792,128]{1,0:T(8,128)(2,1)}, u32[]{:S(2)}, u32[]{:S(2)}) collective-permute-start(bf16[1792,128]{1,0:T(8,128)(2,1)} %get-tuple-element.87), channel_id=1, source_target_pairs={{0,1},{1,2},{2,3},{3,0},{4,5},{5,6},{6,7},{7,4},{8,9},{9,10},{10,1... | collective-permute-start | bytes 1376264 | tf_op jit(solution)/shard_map/ppermute | solution.py:25
  113.4 20.0 %collective-permute-start.25 = (bf16[1792,128]{1,0:T(8,128)(2,1)}, bf16[1792,128]{1,0:T(8,128)(2,1)}, u32[]{:S(2)}, u32[]{:S(2)}) collective-permute-start(bf16[1792,128]{1,0:T(8,128)(2,1)} %get-tuple-element.88), channel_id=1, source_target_pairs={{0,2},{1,3},{2,0},{3,1},{4,6},{5,7},{6,4},{7,5},{8,10},{9,11},{10,... | collective-permute-start | bytes 1376264 | tf_op jit(solution)/shard_map/ppermute | solution.py:25
  123.9 17.9 %collective-permute-start.29 = (bf16[512,512]{1,0:T(8,128)(2,1)S(1)}, bf16[512,512]{1,0:T(8,128)(2,1)S(1)}, u32[]{:S(2)}, u32[]{:S(2)}) collective-permute-start(bf16[512,512]{1,0:T(8,128)(2,1)S(1)} %pad_maximum_fusion), channel_id=1, source_target_pairs={{0,32},{32,0},{1,33},{33,1},{2,34},{34,2},{3,35},{35,3},{4,36},{36... | collective-permute-start | bytes 1572872 | tf_op jit(solution)/shard_map/ppermute | solution.py:29
  136.8 5.9 %collective-permute-start.30 = (bf16[512,384]{1,0:T(8,128)(2,1)}, bf16[512,384]{1,0:T(8,128)(2,1)}, u32[]{:S(2)}, u32[]{:S(2)}) collective-permute-start(bf16[512,384]{1,0:T(8,128)(2,1)} %shard_map.91.refs_0_), channel_id=1, source_target_pairs={{0,32},{32,0},{1,33},{33,1},{2,34},{34,2},{3,35},{35,3},{4,36},{36... | collective-permute-start | bytes 1179656 | tf_op jit(solution)/shard_map/ppermute | solution.py:29
  141.1 11.1 %collective-permute-start.26 = (bf16[512,384]{1,0:T(8,128)(2,1)}, bf16[512,384]{1,0:T(8,128)(2,1)}, u32[]{:S(2)}, u32[]{:S(2)}) collective-permute-start(bf16[512,384]{1,0:T(8,128)(2,1)} %shard_map.91.refs_0_), channel_id=1, source_target_pairs={{0,64},{64,0},{1,65},{65,1},{2,66},{66,2},{3,67},{67,3},{4,68},{68... | collective-permute-start | bytes 1179656 | tf_op jit(solution)/shard_map/ppermute | solution.py:29
  152.2 2.3 %collective-permute-start.31 = (bf16[512,384]{1,0:T(8,128)(2,1)}, bf16[512,384]{1,0:T(8,128)(2,1)S(1)}, u32[]{:S(2)}, u32[]{:S(2)}) collective-permute-start(bf16[512,384]{1,0:T(8,128)(2,1)} %collective-permute-done.26.refs_0_), channel_id=1, source_target_pairs={{0,32},{32,0},{1,33},{33,1},{2,34},{34,2},{3,35},{35,3},{4,36},{36... | collective-permute-start | bytes 1179656 | tf_op jit(solution)/shard_map/ppermute | solution.py:29
  (17 other events, 191.7 us)

commit v4 on v3

--- a/solution.py
+++ b/solution.py
@@ -14,7 +14,8 @@
 LOG2_SCALE = SCALE * math.log2(math.e)
 NEAR = 4
 STAT_LANES = 32
-VMEM = 60 * 2**20
+VMEM = 28 * 2**20
+VMEM_FIRST = 60 * 2**20
 SHORT = pl.CostEstimate(flops=1, bytes_accessed=1, transcendentals=0)
 DIAGONAL = ((0, 3), (1, 2), (2, 1), (3, 0))
 PAIR = 2 * DH
@@ -277,7 +278,7 @@
     width = out_weight.shape[1] // 4
     return [
         lax.dynamic_slice_in_dim(out_weight, at * width, width, axis=1)
-        for at in ((1 - xl) * 2 + co, (1 - xl) * 2 + 1 - co, xl * 2 + 1 - co)
+        for at in (xl * 2 + co, (1 - xl) * 2 + co, (1 - xl) * 2 + 1 - co, xl * 2 + 1 - co)
     ]
 
 
@@ -310,7 +311,7 @@
             out_specs=[full(*shape) for shape in shapes],
         ),
         out_shape=[jax.ShapeDtypeStruct(shape, jnp.bfloat16) for shape in shapes],
-        compiler_params=pltpu.CompilerParams(vmem_limit_bytes=VMEM),
+        compiler_params=pltpu.CompilerParams(vmem_limit_bytes=VMEM_FIRST),
         cost_estimate=SHORT,
     )(at, *arrays)
 
@@ -322,8 +323,8 @@
     query_in = other(query_away, "xh")
     keys_in = other(after(keys_away, query_in), "xh")
     keys_own = ring(keys_own, "y")
-    mine, theirs, beside = weight_slices(out_weight)
-    query_own = gather(query_own, "z", (mine, theirs, beside, query_in))
+    kept, mine, theirs, beside = weight_slices(out_weight)
+    query_own = gather(query_own, "z", (kept, mine, theirs, beside, query_in))
     mine, theirs = after((mine, theirs), keys_in)
     early_own = attend(query_own, keys_own)
     keys_in = ring(after(keys_in, keys_own), "y", early_own)
@@ -335,12 +336,12 @@
     in_back = give_back(in_parts, "z")
     crossed = [other(a, "co") for a in after((beside, theirs), in_parts, mine)]
     own_back = give_back(after(own_parts, in_back, crossed), "z")
-    weights = [out_weight, mine, *crossed]
+    weights = [kept, mine, *crossed]
     heads_in = combine(after(in_back, own_parts))
     heads_own = combine(own_back)
     returned = other(heads_in, "xh")
     returned_far = lax.ppermute(heads_in, ("xl", "xh"), DIAGONAL)
-    early = other(jnp.concatenate([returned, returned_far], axis=1), "co")
+    returned_beside, returned_far_beside = other(returned, "co"), other(returned_far, "co")
     beside_own = other(heads_own, "co")
     own_far = other(heads_own, "xl")
     tiles = 2
@@ -351,12 +352,12 @@
             (1, 0, 0, "back"),
             (0, PAIR, 0, "fifth"),
             (2, 0, 1, "back"),
-            (4, 0, 2, "kept"),
+            (5, 0, 2, "kept"),
             (3, 0, 2, "back"),
-            (4, PAIR, 2, "fifth"),
-            (3, PAIR, 3, "back"),
+            (5, PAIR, 2, "fifth"),
+            (4, 0, 3, "back"),
         ),
-        (heads_own, returned, returned_far, early, beside_own),
+        (heads_own, returned, returned_far, returned_beside, returned_far_beside, beside_own),
         weights,
         places,
         tiles,

time: 161 us -> 145 us (0.901)
  Pallas kernels: 64.1 us -> 46.7 us
    pallas_call x4, Pallas kernels: 40.9 us -> 31.1 us  [attend(): pl.pallas_call(functools.partial(attend_kernel, slices, len(blocks), head...]
    ppermute x20, waiting for transfers between devices: 22.5 us -> 32.2 us  [shift(): lax.ppermute(array, axis, [(i, (i + by) % NEAR) for i in range(NEAR)])]
    ppermute x1, waiting for transfers between devices: 8.13 us -> 0.01 us  [per_device(): returned_far = lax.ppermute(heads_in, ('xl', 'xh'), DIAGONAL)]
    pallas_call x2, Pallas kernels: 13.5 us -> 9.33 us  [project(): pl.pallas_call(functools.partial(project_kernel, terms, len(pieces), len(...]
    unnamed x34 -> x18, local copies, waits for them, and re-layouts: 0.82 us -> 4.87 us
    pallas_call x2, Pallas kernels: 6.44 us -> 3.07 us  [combine(): pl.pallas_call(functools.partial(combine_kernel, heads), out_shape=jax.Sh...]
    slice x4, local copies, waits for them, and re-layouts: 2.84 us -> 0.11 us  [ring(): parts = after((ahead[:middle], behind[middle:]), beside)]
    ppermute x10 -> x11, waiting for transfers between devices: 4.93 us -> 3.33 us  [other(): return lax.ppermute(array, axis, [(0, 1), (1, 0)])]
  transfers between devices with their start and end apart: 32 -> 33, of which waited for: 13 -> 15; matrix products, arithmetic and copies ran while one was open for 5% -> 3% of each run, Pallas kernels for 34% -> 27%
where the time goes in v4:
time: 145 us
  starting transfers between devices  51.7 us (36%)
  Pallas kernels  46.7 us (32%)
  waiting for transfers between devices  35.8 us (25%)
  local copies, waits for them, and re-layouts  9.52 us (7%)
    ppermute x20, waiting for transfers between devices, shift(): lax.ppermute(array, axis, [(i, (i + by) % NEAR) for i in range(NEAR)])  32.2 us
    pallas_call x4, Pallas kernels, attend(): pl.pallas_call(functools.partial(attend_kernel, slices, len(blocks), head...  31.1 us
    ppermute x20, starting transfers between devices, shift(): lax.ppermute(array, axis, [(i, (i + by) % NEAR) for i in range(NEAR)])  27.3 us
    ppermute x11, starting transfers between devices, other(): return lax.ppermute(array, axis, [(0, 1), (1, 0)])  22.7 us
    pallas_call x2, Pallas kernels, project(): pl.pallas_call(functools.partial(project_kernel, terms, len(pieces), len(...  9.33 us
    unnamed x18, local copies, waits for them, and re-layouts  4.87 us
    dynamic_slice x1, local copies, waits for them, and re-layouts, weight_slices(): lax.dynamic_slice_in_dim(out_weight, at * width, width, axis=1)  4.54 us
    ppermute x11, waiting for transfers between devices, other(): return lax.ppermute(array, axis, [(0, 1), (1, 0)])  3.33 us
  transfers between devices with their start and end apart: 33, of which 15 were waited for; matrix products, arithmetic and copies ran while one was open for 3% of the time, Pallas kernels for 27%

profile of v4, /device:TPU:1, one launch (start us, length us, event | category | flops | bytes accessed | tf_op | source)
XLA Modules:
  0.0 144.6 jit_solution(9840503500606438629)
XLA Ops:
  0.6 3.2 %shard_map.86 = (bf16[3072,128]{1,0:T(8,128)(2,1)}, bf16[1024,128]{1,0:T(8,128)(2,1)}, bf16[3072,128]{1,0:T(8,128)(2,1)}, bf16[1536,128]{1,0:T(8,128)(2,1)}) custom-call(s32[1]{0:T(128)} %bitcast.at_ref, bf16[256,640]{1,0:T(8,128)(2,1)} %refs_0_.1, bf16[256,640]{1,0:T(8,128)(2,1)} %refs_1_.1, bf16[256,640]{1,0:T(8,128)(2,1)} %refs_2_.1, ...), custom_call_target="tpu_custom_call" | custom-call | flops 1 | bytes 1 | tf_op jit(solution)/shard_map/pallas_call | solution.py:305
  3.8 3.6 %collective-permute-start.2 = (bf16[1024,128]{1,0:T(8,128)(2,1)}, bf16[1024,128]{1,0:T(8,128)(2,1)S(1)}, u32[]{:S(2)}, u32[]{:S(2)}) collective-permute-start(bf16[1024,128]{1,0:T(8,128)(2,1)} %get-tuple-element.49), channel_id=1, source_target_pairs={{0,16},{16,0},{1,17},{17,1},{2,18},{18,2},{3,19},{19,3},{4,20},{20... | collective-permute-start | bytes 786440 | tf_op jit(solution)/shard_map/ppermute | solution.py:30
  10.2 1.6 %collective-permute-start = (bf16[1536,128]{1,0:T(8,128)(2,1)}, bf16[1536,128]{1,0:T(8,128)(2,1)S(1)}, u32[]{:S(2)}, u32[]{:S(2)}) collective-permute-start(bf16[1536,128]{1,0:T(8,128)(2,1)} %get-tuple-element.73.refs_0_), channel_id=1, source_target_pairs={{0,1},{1,2},{2,3},{3,0},{4,5},{5,6},{6,7},{7,4},{8,9},{9,10},{10,1... | collective-permute-start | bytes 1179656 | tf_op jit(solution)/shard_map/ppermute | solution.py:26
  11.8 2.1 %collective-permute-start.1 = (bf16[1536,128]{1,0:T(8,128)(2,1)}, bf16[1536,128]{1,0:T(8,128)(2,1)S(1)}, u32[]{:S(2)}, u32[]{:S(2)}) collective-permute-start(bf16[1536,128]{1,0:T(8,128)(2,1)} %get-tuple-element.73.refs_0_), channel_id=1, source_target_pairs={{0,3},{1,0},{2,1},{3,2},{4,7},{5,4},{6,5},{7,6},{8,11},{9,8},{10,9... | collective-permute-start | bytes 1179656 | tf_op jit(solution)/shard_map/ppermute | solution.py:26
  13.9 2.4 %collective-permute-start.7 = (bf16[3072,128]{1,0:T(8,128)(2,1)}, bf16[3072,128]{1,0:T(8,128)(2,1)S(1)}, u32[]{:S(2)}, u32[]{:S(2)}) collective-permute-start(bf16[3072,128]{1,0:T(8,128)(2,1)} %get-tuple-element.54), channel_id=1, source_target_pairs={{0,16},{16,0},{1,17},{17,1},{2,18},{18,2},{3,19},{19,3},{4,20},{20... | collective-permute-start | bytes 2359304 | tf_op jit(solution)/shard_map/ppermute | solution.py:30
  16.3 4.5 %constant_dynamic-slice_fusion = (bf16[640,1280]{1,0:T(8,128)(2,1)S(1)}, bf16[640,1280]{1,0:T(8,128)(2,1)S(1)}, bf16[640,1280]{1,0:T(8,128)(2,1)}, bf16[640,1280]{1,0:T(8,128)(2,1)S(1)}) fusion(bf16[640,5120]{1,0:T(8,128)(2,1)} %param.13, s32[]{:T(128)S(6)} %select_n.15, s32[]{:T(128)S(6)} %select_n.13, s32[]{:T(128)S(6)} %select_n.12, s32[]{:T(128)S(6)} %select_n.14), kind=kLoop, calls=%fused_computation | loop fusion | bytes 13107216 | tf_op jit(solution)/shard_map/dynamic_slice | solution.py:280
  22.1 2.5 %collective-permute-start.3 = (bf16[1536,128]{1,0:T(8,128)(2,1)S(1)}, bf16[1536,128]{1,0:T(8,128)(2,1)S(1)}, u32[]{:S(2)}, u32[]{:S(2)}) collective-permute-start(bf16[1536,128]{1,0:T(8,128)(2,1)S(1)} %copy-done.4), channel_id=1, source_target_pairs={{0,2},{1,3},{2,0},{3,1},{4,6},{5,7},{6,4},{7,5},{8,10},{9,11},{10,... | collective-permute-start | bytes 1179656 | tf_op jit(solution)/shard_map/ppermute | solution.py:26
  24.6 2.5 %collective-permute-done.8.refs_5_.refs_9_ = bf16[3072,128]{1,0:T(8,128)(2,1)S(1)} collective-permute-done((bf16[3072,128]{1,0:T(8,128)(2,1)}, bf16[3072,128]{1,0:T(8,128)(2,1)S(1)}, u32[]{:S(2)}, u32[]{:S(2)}) %collective-permute-start.8) | collective-permute-done | bytes 786464 | tf_op jit(solution)/shard_map/ppermute | solution.py:26
  28.1 1.8 %collective-permute-start.11 = (bf16[1536,128]{1,0:T(8,128)(2,1)S(1)}, bf16[1536,128]{1,0:T(8,128)(2,1)S(1)}, u32[]{:S(2)}, u32[]{:S(2)}) collective-permute-start(bf16[1536,128]{1,0:T(8,128)(2,1)S(1)} %slice.17), channel_id=1, source_target_pairs={{0,12},{4,0},{8,4},{12,8},{1,13},{5,1},{9,5},{13,9},{2,14},{6,2},{... | collective-permute-start | bytes 1179656 | tf_op jit(solution)/shard_map/ppermute | solution.py:26
  29.9 2.3 %collective-permute-done.3.refs_3_ = bf16[1536,128]{1,0:T(8,128)(2,1)S(1)} collective-permute-done((bf16[1536,128]{1,0:T(8,128)(2,1)S(1)}, bf16[1536,128]{1,0:T(8,128)(2,1)S(1)}, u32[]{:S(2)}, u32[]{:S(2)}) %collective-permute-start.3) | collective-permute-done | bytes 393248 | tf_op jit(solution)/shard_map/ppermute | solution.py:26
  32.2 2.7 %collective-permute-start.5 = (bf16[1024,128]{1,0:T(8,128)(2,1)S(1)}, bf16[1024,128]{1,0:T(8,128)(2,1)S(1)}, u32[]{:S(2)}, u32[]{:S(2)}) collective-permute-start(bf16[1024,128]{1,0:T(8,128)(2,1)S(1)} %collective-permute-done.2.refs_0_), channel_id=1, source_target_pairs={{0,3},{1,0},{2,1},{3,2},{4,7},{5,4},{6,5},{7,6},{8,11},{9,8},{10,9... | collective-permute-start | bytes 786440 | tf_op jit(solution)/shard_map/ppermute | solution.py:26
  34.9 4.1 %collective-permute-done.4.refs_1_ = bf16[1024,128]{1,0:T(8,128)(2,1)S(1)} collective-permute-done((bf16[1024,128]{1,0:T(8,128)(2,1)S(1)}, bf16[1024,128]{1,0:T(8,128)(2,1)S(1)}, u32[]{:S(2)}, u32[]{:S(2)}) %collective-permute-start.4) | collective-permute-done | bytes 262176 | tf_op jit(solution)/shard_map/ppermute | solution.py:26
  38.9 2.5 %collective-permute-start.6 = (bf16[1024,128]{1,0:T(8,128)(2,1)S(1)}, bf16[1024,128]{1,0:T(8,128)(2,1)S(1)}, u32[]{:S(2)}, u32[]{:S(2)}) collective-permute-start(bf16[1024,128]{1,0:T(8,128)(2,1)S(1)} %collective-permute-done.2.refs_0_), channel_id=1, source_target_pairs={{0,2},{1,3},{2,0},{3,1},{4,6},{5,7},{6,4},{7,5},{8,10},{9,11},{10,... | collective-permute-start | bytes 786440 | tf_op jit(solution)/shard_map/ppermute | solution.py:26
  42.4 1.7 %collective-permute-start.12 = (bf16[3072,128]{1,0:T(8,128)(2,1)S(1)}, bf16[3072,128]{1,0:T(8,128)(2,1)S(1)}, u32[]{:S(2)}, u32[]{:S(2)}) collective-permute-start(bf16[3072,128]{1,0:T(8,128)(2,1)S(1)} %collective-permute-done.7.refs_4_.refs_8_), channel_id=1, source_target_pairs={{0,4},{4,8},{8,12},{12,0},{1,5},{5,9},{9,13},{13,1},{2,6},{6,10},{... | collective-permute-start | bytes 2359304 | tf_op jit(solution)/shard_map/ppermute | solution.py:26
  44.0 1.5 %collective-permute-start.13 = (bf16[3072,128]{1,0:T(8,128)(2,1)S(1)}, bf16[3072,128]{1,0:T(8,128)(2,1)S(1)}, u32[]{:S(2)}, u32[]{:S(2)}) collective-permute-start(bf16[3072,128]{1,0:T(8,128)(2,1)S(1)} %collective-permute-done.7.refs_4_.refs_8_), channel_id=1, source_target_pairs={{0,12},{4,0},{8,4},{12,8},{1,13},{5,1},{9,5},{13,9},{2,14},{6,2},{... | collective-permute-start | bytes 2359304 | tf_op jit(solution)/shard_map/ppermute | solution.py:26
  47.6 8.6 %shard_map.87 = (bf16[1792,128]{1,0:T(8,128)(2,1)S(1)}, bf16[1792,128]{1,0:T(8,128)(2,1)S(1)}, bf16[1792,128]{1,0:T(8,128)(2,1)S(1)}, bf16[1792,128]{1,0:T(8,128)(2,1)S(1)}) custom-call(bf16[1536,128]{1,0:T(8,128)(2,1)S(1)} %copy-done.4, bf16[1536,128]{1,0:T(8,128)(2,1)S(1)} %copy-done.6, bf16[1536,128]{1,0:T(8,128)(2,1)S(1)} %copy-done.8, ...), custom_call_target="tpu_custom_call" | custom-call | flops 12884901888 | bytes 7864320 | tf_op jit(solution)/shard_map/pallas_call | solution.py:153
  56.2 1.8 %collective-permute-done.12.refs_5_.refs_9_ = bf16[3072,128]{1,0:T(8,128)(2,1)S(1)} collective-permute-done((bf16[3072,128]{1,0:T(8,128)(2,1)S(1)}, bf16[3072,128]{1,0:T(8,128)(2,1)S(1)}, u32[]{:S(2)}, u32[]{:S(2)}) %collective-permute-start.12) | collective-permute-done | bytes 786464 | tf_op jit(solution)/shard_map/ppermute | solution.py:26
  60.9 5.7 %shard_map.88 = (bf16[1280,128]{1,0:T(8,128)(2,1)S(1)}, bf16[1280,128]{1,0:T(8,128)(2,1)S(1)}, bf16[1280,128]{1,0:T(8,128)(2,1)S(1)}, bf16[1280,128]{1,0:T(8,128)(2,1)S(1)}) custom-call(bf16[1024,128]{1,0:T(8,128)(2,1)S(1)} %collective-permute-done.2.refs_0_, bf16[1024,128]{1,0:T(8,128)(2,1)S(1)} %collective-permute-done.4.refs_1_, ...), custom_call_target="tpu_custom_call" | custom-call | flops 8589934592 | bytes 5242880 | tf_op jit(solution)/shard_map/pallas_call | solution.py:153
  67.8 6.7 %shard_map.89 = (bf16[1280,128]{1,0:T(8,128)(2,1)S(1)}, bf16[1280,128]{1,0:T(8,128)(2,1)S(1)}, bf16[1280,128]{1,0:T(8,128)(2,1)S(1)}, bf16[1280,128]{1,0:T(8,128)(2,1)S(1)}) custom-call(bf16[1024,128]{1,0:T(8,128)(2,1)S(1)} %collective-permute-done.2.refs_0_, bf16[1024,128]{1,0:T(8,128)(2,1)S(1)} %collective-permute-done.4.refs_1_, ...), custom_call_target="tpu_custom_call" | custom-call | flops 8589934592 | bytes 5242880 | tf_op jit(solution)/shard_map/pallas_call | solution.py:153
  74.8 7.1 %collective-permute-start.21 = (bf16[640,1280]{1,0:T(8,128)(2,1)S(1)}, bf16[640,1280]{1,0:T(8,128)(2,1)S(1)}, u32[]{:S(2)}, u32[]{:S(2)}) collective-permute-start(bf16[640,1280]{1,0:T(8,128)(2,1)S(1)} %get-tuple-element.83), channel_id=1, source_target_pairs={{0,32},{32,0},{1,33},{33,1},{2,34},{34,2},{3,35},{35,3},{4,36},{36... | collective-permute-start | bytes 4915208 | tf_op jit(solution)/shard_map/ppermute | solution.py:30
  83.7 10.0 %shard_map.90 = (bf16[1792,128]{1,0:T(8,128)(2,1)S(1)}, bf16[1792,128]{1,0:T(8,128)(2,1)S(1)}, bf16[1792,128]{1,0:T(8,128)(2,1)S(1)}, bf16[1792,128]{1,0:T(8,128)(2,1)S(1)}) custom-call(bf16[1536,128]{1,0:T(8,128)(2,1)S(1)} %copy-done.4, bf16[1536,128]{1,0:T(8,128)(2,1)S(1)} %copy-done.6, bf16[1536,128]{1,0:T(8,128)(2,1)S(1)} %copy-done.8, ...), custom_call_target="tpu_custom_call" | custom-call | flops 12884901888 | bytes 7864320 | tf_op jit(solution)/shard_map/pallas_call | solution.py:153
  93.7 5.6 %collective-permute-done.17.refs_2_ = bf16[1280,128]{1,0:T(8,128)(2,1)S(1)} collective-permute-done((bf16[1280,128]{1,0:T(8,128)(2,1)S(1)}, bf16[1280,128]{1,0:T(8,128)(2,1)S(1)}, u32[]{:S(2)}, u32[]{:S(2)}) %collective-permute-start.17) | collective-permute-done | bytes 327712 | tf_op jit(solution)/shard_map/ppermute | solution.py:26
  103.1 3.3 %collective-permute-start.27 = (bf16[512,256]{1,0:T(8,128)(2,1)S(1)}, bf16[512,256]{1,0:T(8,128)(2,1)S(1)}, u32[]{:S(2)}, u32[]{:S(2)}) collective-permute-start(bf16[512,256]{1,0:T(8,128)(2,1)S(1)} %shard_map.92), channel_id=1, source_target_pairs={{0,16},{16,0},{1,17},{17,1},{2,18},{18,2},{3,19},{19,3},{4,20},{20... | collective-permute-start | bytes 786440 | tf_op jit(solution)/shard_map/ppermute | solution.py:30
  107.2 2.6 %collective-permute-done.23.refs_1_ = bf16[1792,128]{1,0:T(8,128)(2,1)S(1)} collective-permute-done((bf16[1792,128]{1,0:T(8,128)(2,1)S(1)}, bf16[1792,128]{1,0:T(8,128)(2,1)S(1)}, u32[]{:S(2)}, u32[]{:S(2)}) %collective-permute-start.23) | collective-permute-done | bytes 458784 | tf_op jit(solution)/shard_map/ppermute | solution.py:26
  109.8 3.5 %collective-permute-done.24.refs_2_ = bf16[1792,128]{1,0:T(8,128)(2,1)S(1)} collective-permute-done((bf16[1792,128]{1,0:T(8,128)(2,1)S(1)}, bf16[1792,128]{1,0:T(8,128)(2,1)S(1)}, u32[]{:S(2)}, u32[]{:S(2)}) %collective-permute-start.24) | collective-permute-done | bytes 458784 | tf_op jit(solution)/shard_map/ppermute | solution.py:26
  113.3 7.3 %collective-permute-done.25.refs_3_ = bf16[1792,128]{1,0:T(8,128)(2,1)S(1)} collective-permute-done((bf16[1792,128]{1,0:T(8,128)(2,1)S(1)}, bf16[1792,128]{1,0:T(8,128)(2,1)S(1)}, u32[]{:S(2)}, u32[]{:S(2)}) %collective-permute-start.25) | collective-permute-done | bytes 458784 | tf_op jit(solution)/shard_map/ppermute | solution.py:26
  120.6 2.1 %shard_map.91.refs_0_ = bf16[512,384]{1,0:T(8,128)(2,1)} custom-call(bf16[1792,128]{1,0:T(8,128)(2,1)S(1)} %get-tuple-element.85.refs_0_, bf16[1792,128]{1,0:T(8,128)(2,1)S(1)} %collective-permute-done.23.refs_1_, bf16[1792,128]{1,0:T(8,128)(2,1)S(1)} %collective-permute-done.24.refs_2_, bf16[1792,128]{1,0:T(8,128)(2,1)S(1)} %collective-permute-done.25.refs_3_), custom_call_target="tpu_custom_call" | custom-call | flops 1 | bytes 1 | tf_op jit(solution)/shard_map/pallas_call | solution.py:196
  122.7 3.7 %collective-permute-start.31 = (bf16[512,384]{1,0:T(8,128)(2,1)}, bf16[512,384]{1,0:T(8,128)(2,1)}, u32[]{:S(2)}, u32[]{:S(2)}) collective-permute-start(bf16[512,384]{1,0:T(8,128)(2,1)} %shard_map.91.refs_0_), channel_id=1, source_target_pairs={{0,32},{32,0},{1,33},{33,1},{2,34},{34,2},{3,35},{35,3},{4,36},{36... | collective-permute-start | bytes 1179656 | tf_op jit(solution)/shard_map/ppermute | solution.py:30
  126.4 1.7 %collective-permute-start.26 = (bf16[512,384]{1,0:T(8,128)(2,1)}, bf16[512,384]{1,0:T(8,128)(2,1)}, u32[]{:S(2)}, u32[]{:S(2)}) collective-permute-start(bf16[512,384]{1,0:T(8,128)(2,1)} %shard_map.91.refs_0_), channel_id=1, source_target_pairs={{0,64},{64,0},{1,65},{65,1},{2,66},{66,2},{3,67},{67,3},{4,68},{68... | collective-permute-start | bytes 1179656 | tf_op jit(solution)/shard_map/ppermute | solution.py:30
  133.2 5.6 %shard_map.93.refs_4_ = f32[512,1280]{1,0:T(8,128)S(1)} custom-call(s32[2]{0:T(128)S(1)} %pad_add_fusion.at_ref, bf16[512,384]{1,0:T(8,128)(2,1)} %shard_map.91.refs_0_, bf16[512,256]{1,0:T(8,128)(2,1)S(1)} %collective-permute-done.27.refs_1_, bf16[512,256]{1,0:T(8,128)(2,1)} %collective-permute-done.28.refs_2_, ...), custom_call_target="tpu_custom_call" | custom-call | flops 1 | bytes 1 | tf_op jit(solution)/shard_map/pallas_call | solution.py:260
  139.2 1.6 %collective-permute-done.32.refs_1_ = bf16[512,384]{1,0:T(8,128)(2,1)S(1)} collective-permute-done((bf16[512,384]{1,0:T(8,128)(2,1)}, bf16[512,384]{1,0:T(8,128)(2,1)S(1)}, u32[]{:S(2)}, u32[]{:S(2)}) %collective-permute-start.32) | collective-permute-done | bytes 393248 | tf_op jit(solution)/shard_map/ppermute | solution.py:30
  140.8 3.7 %shard_map.94 = (bf16[256,1280]{1,0:T(8,128)(2,1)}, bf16[256,1280]{1,0:T(8,128)(2,1)}) custom-call(s32[2]{0:T(128)S(1)} %pad_add_fusion.at_ref, bf16[512,384]{1,0:T(8,128)(2,1)} %collective-permute-done.26.refs_0_, bf16[512,384]{1,0:T(8,128)(2,1)S(1)} %collective-permute-done.32.refs_1_, bf16[640,1280]{1,0:T(8,128)(2,1)S(1)} %collective-permute-done.20.refs_7_.refs_2_, ...), custom_call_target="tpu_custom_call" | custom-call | flops 1 | bytes 1 | tf_op jit(solution)/shard_map/pallas_call | solution.py:260
  (67 shorter events, 24.3 us)
Async XLA Ops:
  3.8 10.1 %collective-permute-start.2 = (bf16[1024,128]{1,0:T(8,128)(2,1)}, bf16[1024,128]{1,0:T(8,128)(2,1)S(1)}, u32[]{:S(2)}, u32[]{:S(2)}) collective-permute-start(bf16[1024,128]{1,0:T(8,128)(2,1)} %get-tuple-element.49), channel_id=1, source_target_pairs={{0,16},{16,0},{1,17},{17,1},{2,18},{18,2},{3,19},{19,3},{4,20},{20... | collective-permute-start | bytes 786440 | tf_op jit(solution)/shard_map/ppermute | solution.py:30
  7.4 19.6 %collective-permute-start.8 = (bf16[3072,128]{1,0:T(8,128)(2,1)}, bf16[3072,128]{1,0:T(8,128)(2,1)S(1)}, u32[]{:S(2)}, u32[]{:S(2)}) collective-permute-start(bf16[3072,128]{1,0:T(8,128)(2,1)} %get-tuple-element.55.refs_4_.refs_8_), channel_id=1, source_target_pairs={{0,4},{4,8},{8,12},{12,0},{1,5},{5,9},{9,13},{13,1},{2,6},{6,10},{... | collective-permute-start | bytes 2359304 | tf_op jit(solution)/shard_map/ppermute | solution.py:26
  8.7 18.4 %collective-permute-start.9 = (bf16[3072,128]{1,0:T(8,128)(2,1)}, bf16[3072,128]{1,0:T(8,128)(2,1)S(1)}, u32[]{:S(2)}, u32[]{:S(2)}) collective-permute-start(bf16[3072,128]{1,0:T(8,128)(2,1)} %get-tuple-element.55.refs_4_.refs_8_), channel_id=1, source_target_pairs={{0,12},{4,0},{8,4},{12,8},{1,13},{5,1},{9,5},{13,9},{2,14},{6,2},{... | collective-permute-start | bytes 2359304 | tf_op jit(solution)/shard_map/ppermute | solution.py:26
  10.2 11.9 %collective-permute-start = (bf16[1536,128]{1,0:T(8,128)(2,1)}, bf16[1536,128]{1,0:T(8,128)(2,1)S(1)}, u32[]{:S(2)}, u32[]{:S(2)}) collective-permute-start(bf16[1536,128]{1,0:T(8,128)(2,1)} %get-tuple-element.73.refs_0_), channel_id=1, source_target_pairs={{0,1},{1,2},{2,3},{3,0},{4,5},{5,6},{6,7},{7,4},{8,9},{9,10},{10,1... | collective-permute-start | bytes 1179656 | tf_op jit(solution)/shard_map/ppermute | solution.py:26
  11.8 10.3 %collective-permute-start.1 = (bf16[1536,128]{1,0:T(8,128)(2,1)}, bf16[1536,128]{1,0:T(8,128)(2,1)S(1)}, u32[]{:S(2)}, u32[]{:S(2)}) collective-permute-start(bf16[1536,128]{1,0:T(8,128)(2,1)} %get-tuple-element.73.refs_0_), channel_id=1, source_target_pairs={{0,3},{1,0},{2,1},{3,2},{4,7},{5,4},{6,5},{7,6},{8,11},{9,8},{10,9... | collective-permute-start | bytes 1179656 | tf_op jit(solution)/shard_map/ppermute | solution.py:26
  13.9 27.5 %collective-permute-start.7 = (bf16[3072,128]{1,0:T(8,128)(2,1)}, bf16[3072,128]{1,0:T(8,128)(2,1)S(1)}, u32[]{:S(2)}, u32[]{:S(2)}) collective-permute-start(bf16[3072,128]{1,0:T(8,128)(2,1)} %get-tuple-element.54), channel_id=1, source_target_pairs={{0,16},{16,0},{1,17},{17,1},{2,18},{18,2},{3,19},{19,3},{4,20},{20... | collective-permute-start | bytes 2359304 | tf_op jit(solution)/shard_map/ppermute | solution.py:30
  22.1 10.1 %collective-permute-start.3 = (bf16[1536,128]{1,0:T(8,128)(2,1)S(1)}, bf16[1536,128]{1,0:T(8,128)(2,1)S(1)}, u32[]{:S(2)}, u32[]{:S(2)}) collective-permute-start(bf16[1536,128]{1,0:T(8,128)(2,1)S(1)} %copy-done.4), channel_id=1, source_target_pairs={{0,2},{1,3},{2,0},{3,1},{4,6},{5,7},{6,4},{7,5},{8,10},{9,11},{10,... | collective-permute-start | bytes 1179656 | tf_op jit(solution)/shard_map/ppermute | solution.py:26
  27.1 15.2 %collective-permute-start.10 = (bf16[1536,128]{1,0:T(8,128)(2,1)S(1)}, bf16[1536,128]{1,0:T(8,128)(2,1)S(1)}, u32[]{:S(2)}, u32[]{:S(2)}) collective-permute-start(bf16[1536,128]{1,0:T(8,128)(2,1)S(1)} %slice.16), channel_id=1, source_target_pairs={{0,4},{4,8},{8,12},{12,0},{1,5},{5,9},{9,13},{13,1},{2,6},{6,10},{... | collective-permute-start | bytes 1179656 | tf_op jit(solution)/shard_map/ppermute | solution.py:26
  28.1 14.2 %collective-permute-start.11 = (bf16[1536,128]{1,0:T(8,128)(2,1)S(1)}, bf16[1536,128]{1,0:T(8,128)(2,1)S(1)}, u32[]{:S(2)}, u32[]{:S(2)}) collective-permute-start(bf16[1536,128]{1,0:T(8,128)(2,1)S(1)} %slice.17), channel_id=1, source_target_pairs={{0,12},{4,0},{8,4},{12,8},{1,13},{5,1},{9,5},{13,9},{2,14},{6,2},{... | collective-permute-start | bytes 1179656 | tf_op jit(solution)/shard_map/ppermute | solution.py:26
  32.2 6.7 %collective-permute-start.4 = (bf16[1024,128]{1,0:T(8,128)(2,1)S(1)}, bf16[1024,128]{1,0:T(8,128)(2,1)S(1)}, u32[]{:S(2)}, u32[]{:S(2)}) collective-permute-start(bf16[1024,128]{1,0:T(8,128)(2,1)S(1)} %collective-permute-done.2.refs_0_), channel_id=1, source_target_pairs={{0,1},{1,2},{2,3},{3,0},{4,5},{5,6},{6,7},{7,4},{8,9},{9,10},{10,1... | collective-permute-start | bytes 786440 | tf_op jit(solution)/shard_map/ppermute | solution.py:26
  32.2 6.7 %collective-permute-start.5 = (bf16[1024,128]{1,0:T(8,128)(2,1)S(1)}, bf16[1024,128]{1,0:T(8,128)(2,1)S(1)}, u32[]{:S(2)}, u32[]{:S(2)}) collective-permute-start(bf16[1024,128]{1,0:T(8,128)(2,1)S(1)} %collective-permute-done.2.refs_0_), channel_id=1, source_target_pairs={{0,3},{1,0},{2,1},{3,2},{4,7},{5,4},{6,5},{7,6},{8,11},{9,8},{10,9... | collective-permute-start | bytes 786440 | tf_op jit(solution)/shard_map/ppermute | solution.py:26
  38.9 21.9 %collective-permute-start.6 = (bf16[1024,128]{1,0:T(8,128)(2,1)S(1)}, bf16[1024,128]{1,0:T(8,128)(2,1)S(1)}, u32[]{:S(2)}, u32[]{:S(2)}) collective-permute-start(bf16[1024,128]{1,0:T(8,128)(2,1)S(1)} %collective-permute-done.2.refs_0_), channel_id=1, source_target_pairs={{0,2},{1,3},{2,0},{3,1},{4,6},{5,7},{6,4},{7,5},{8,10},{9,11},{10,... | collective-permute-start | bytes 786440 | tf_op jit(solution)/shard_map/ppermute | solution.py:26
  41.4 33.4 %collective-permute-start.19 = (bf16[640,1280]{1,0:T(8,128)(2,1)S(1)}, bf16[640,1280]{1,0:T(8,128)(2,1)S(1)}, u32[]{:S(2)}, u32[]{:S(2)}) collective-permute-start(bf16[640,1280]{1,0:T(8,128)(2,1)S(1)} %get-tuple-element.81), channel_id=1, source_target_pairs={{0,80},{16,64},{64,16},{80,0},{1,81},{17,65},{65,17},{81,1},{2,82}... | collective-permute-start | bytes 4915208 | tf_op jit(solution)/shard_map/ppermute | solution.py:332
  42.3 32.5 %collective-permute-start.20 = (bf16[640,1280]{1,0:T(8,128)(2,1)S(1)}, bf16[640,1280]{1,0:T(8,128)(2,1)S(1)}, u32[]{:S(2)}, u32[]{:S(2)}) collective-permute-start(bf16[640,1280]{1,0:T(8,128)(2,1)S(1)} %get-tuple-element.82), channel_id=1, source_target_pairs={{0,64},{64,0},{1,65},{65,1},{2,66},{66,2},{3,67},{67,3},{4,68},{68... | collective-permute-start | bytes 4915208 | tf_op jit(solution)/shard_map/ppermute | solution.py:30
  42.4 15.6 %collective-permute-start.12 = (bf16[3072,128]{1,0:T(8,128)(2,1)S(1)}, bf16[3072,128]{1,0:T(8,128)(2,1)S(1)}, u32[]{:S(2)}, u32[]{:S(2)}) collective-permute-start(bf16[3072,128]{1,0:T(8,128)(2,1)S(1)} %collective-permute-done.7.refs_4_.refs_8_), channel_id=1, source_target_pairs={{0,4},{4,8},{8,12},{12,0},{1,5},{5,9},{9,13},{13,1},{2,6},{6,10},{... | collective-permute-start | bytes 2359304 | tf_op jit(solution)/shard_map/ppermute | solution.py:26
  44.0 14.0 %collective-permute-start.13 = (bf16[3072,128]{1,0:T(8,128)(2,1)S(1)}, bf16[3072,128]{1,0:T(8,128)(2,1)S(1)}, u32[]{:S(2)}, u32[]{:S(2)}) collective-permute-start(bf16[3072,128]{1,0:T(8,128)(2,1)S(1)} %collective-permute-done.7.refs_4_.refs_8_), channel_id=1, source_target_pairs={{0,12},{4,0},{8,4},{12,8},{1,13},{5,1},{9,5},{13,9},{2,14},{6,2},{... | collective-permute-start | bytes 2359304 | tf_op jit(solution)/shard_map/ppermute | solution.py:26
  58.1 9.7 %collective-permute-start.14 = (bf16[1536,128]{1,0:T(8,128)(2,1)S(1)}, bf16[1536,128]{1,0:T(8,128)(2,1)S(1)}, u32[]{:S(2)}, u32[]{:S(2)}) collective-permute-start(bf16[1536,128]{1,0:T(8,128)(2,1)S(1)} %slice.18), channel_id=1, source_target_pairs={{0,4},{4,8},{8,12},{12,0},{1,5},{5,9},{9,13},{13,1},{2,6},{6,10},{... | collective-permute-start | bytes 1179656 | tf_op jit(solution)/shard_map/ppermute | solution.py:26
  59.5 8.3 %collective-permute-start.15 = (bf16[1536,128]{1,0:T(8,128)(2,1)S(1)}, bf16[1536,128]{1,0:T(8,128)(2,1)S(1)}, u32[]{:S(2)}, u32[]{:S(2)}) collective-permute-start(bf16[1536,128]{1,0:T(8,128)(2,1)S(1)} %slice.19), channel_id=1, source_target_pairs={{0,12},{4,0},{8,4},{12,8},{1,13},{5,1},{9,5},{13,9},{2,14},{6,2},{... | collective-permute-start | bytes 1179656 | tf_op jit(solution)/shard_map/ppermute | solution.py:26
  74.8 24.5 %collective-permute-start.21 = (bf16[640,1280]{1,0:T(8,128)(2,1)S(1)}, bf16[640,1280]{1,0:T(8,128)(2,1)S(1)}, u32[]{:S(2)}, u32[]{:S(2)}) collective-permute-start(bf16[640,1280]{1,0:T(8,128)(2,1)S(1)} %get-tuple-element.83), channel_id=1, source_target_pairs={{0,32},{32,0},{1,33},{33,1},{2,34},{34,2},{3,35},{35,3},{4,36},{36... | collective-permute-start | bytes 4915208 | tf_op jit(solution)/shard_map/ppermute | solution.py:30
  81.9 17.4 %collective-permute-start.22 = (bf16[640,1280]{1,0:T(8,128)(2,1)S(1)}, bf16[640,1280]{1,0:T(8,128)(2,1)S(1)}, u32[]{:S(2)}, u32[]{:S(2)}) collective-permute-start(bf16[640,1280]{1,0:T(8,128)(2,1)S(1)} %collective-permute-done.19), channel_id=1, source_target_pairs={{0,32},{32,0},{1,33},{33,1},{2,34},{34,2},{3,35},{35,3},{4,36},{36... | collective-permute-start | bytes 4915208 | tf_op jit(solution)/shard_map/ppermute | solution.py:30
  82.0 11.7 %collective-permute-start.16 = (bf16[1280,128]{1,0:T(8,128)(2,1)S(1)}, bf16[1280,128]{1,0:T(8,128)(2,1)S(1)}, u32[]{:S(2)}, u32[]{:S(2)}) collective-permute-start(bf16[1280,128]{1,0:T(8,128)(2,1)S(1)} %get-tuple-element.70), channel_id=1, source_target_pairs={{0,3},{1,0},{2,1},{3,2},{4,7},{5,4},{6,5},{7,6},{8,11},{9,8},{10,9... | collective-permute-start | bytes 983048 | tf_op jit(solution)/shard_map/ppermute | solution.py:26
  82.5 16.8 %collective-permute-start.17 = (bf16[1280,128]{1,0:T(8,128)(2,1)S(1)}, bf16[1280,128]{1,0:T(8,128)(2,1)S(1)}, u32[]{:S(2)}, u32[]{:S(2)}) collective-permute-start(bf16[1280,128]{1,0:T(8,128)(2,1)S(1)} %get-tuple-element.71), channel_id=1, source_target_pairs={{0,1},{1,2},{2,3},{3,0},{4,5},{5,6},{6,7},{7,4},{8,9},{9,10},{10,1... | collective-permute-start | bytes 983048 | tf_op jit(solution)/shard_map/ppermute | solution.py:26
  83.5 15.8 %collective-permute-start.18 = (bf16[1280,128]{1,0:T(8,128)(2,1)S(1)}, bf16[1280,128]{1,0:T(8,128)(2,1)S(1)}, u32[]{:S(2)}, u32[]{:S(2)}) collective-permute-start(bf16[1280,128]{1,0:T(8,128)(2,1)S(1)} %get-tuple-element.72), channel_id=1, source_target_pairs={{0,2},{1,3},{2,0},{3,1},{4,6},{5,7},{6,4},{7,5},{8,10},{9,11},{10,... | collective-permute-start | bytes 983048 | tf_op jit(solution)/shard_map/ppermute | solution.py:26
  99.3 10.5 %collective-permute-start.23 = (bf16[1792,128]{1,0:T(8,128)(2,1)S(1)}, bf16[1792,128]{1,0:T(8,128)(2,1)S(1)}, u32[]{:S(2)}, u32[]{:S(2)}) collective-permute-start(bf16[1792,128]{1,0:T(8,128)(2,1)S(1)} %get-tuple-element.86), channel_id=1, source_target_pairs={{0,3},{1,0},{2,1},{3,2},{4,7},{5,4},{6,5},{7,6},{8,11},{9,8},{10,9... | collective-permute-start | bytes 1376264 | tf_op jit(solution)/shard_map/ppermute | solution.py:26
  100.4 13.0 %collective-permute-start.24 = (bf16[1792,128]{1,0:T(8,128)(2,1)S(1)}, bf16[1792,128]{1,0:T(8,128)(2,1)S(1)}, u32[]{:S(2)}, u32[]{:S(2)}) collective-permute-start(bf16[1792,128]{1,0:T(8,128)(2,1)S(1)} %get-tuple-element.87), channel_id=1, source_target_pairs={{0,1},{1,2},{2,3},{3,0},{4,5},{5,6},{6,7},{7,4},{8,9},{9,10},{10,1... | collective-permute-start | bytes 1376264 | tf_op jit(solution)/shard_map/ppermute | solution.py:26
  100.8 19.8 %collective-permute-start.25 = (bf16[1792,128]{1,0:T(8,128)(2,1)S(1)}, bf16[1792,128]{1,0:T(8,128)(2,1)S(1)}, u32[]{:S(2)}, u32[]{:S(2)}) collective-permute-start(bf16[1792,128]{1,0:T(8,128)(2,1)S(1)} %get-tuple-element.88), channel_id=1, source_target_pairs={{0,2},{1,3},{2,0},{3,1},{4,6},{5,7},{6,4},{7,5},{8,10},{9,11},{10,... | collective-permute-start | bytes 1376264 | tf_op jit(solution)/shard_map/ppermute | solution.py:26
  103.1 25.0 %collective-permute-start.27 = (bf16[512,256]{1,0:T(8,128)(2,1)S(1)}, bf16[512,256]{1,0:T(8,128)(2,1)S(1)}, u32[]{:S(2)}, u32[]{:S(2)}) collective-permute-start(bf16[512,256]{1,0:T(8,128)(2,1)S(1)} %shard_map.92), channel_id=1, source_target_pairs={{0,16},{16,0},{1,17},{17,1},{2,18},{18,2},{3,19},{19,3},{4,20},{20... | collective-permute-start | bytes 786440 | tf_op jit(solution)/shard_map/ppermute | solution.py:30
  106.4 22.0 %collective-permute-start.28 = (bf16[512,256]{1,0:T(8,128)(2,1)S(1)}, bf16[512,256]{1,0:T(8,128)(2,1)}, u32[]{:S(2)}, u32[]{:S(2)}) collective-permute-start(bf16[512,256]{1,0:T(8,128)(2,1)S(1)} %shard_map.92), channel_id=1, source_target_pairs={{0,80},{16,64},{64,16},{80,0},{1,81},{17,65},{65,17},{81,1},{2,82}... | collective-permute-start | bytes 786440 | tf_op jit(solution)/shard_map/ppermute | solution.py:343
  122.7 7.6 %collective-permute-start.31 = (bf16[512,384]{1,0:T(8,128)(2,1)}, bf16[512,384]{1,0:T(8,128)(2,1)}, u32[]{:S(2)}, u32[]{:S(2)}) collective-permute-start(bf16[512,384]{1,0:T(8,128)(2,1)} %shard_map.91.refs_0_), channel_id=1, source_target_pairs={{0,32},{32,0},{1,33},{33,1},{2,34},{34,2},{3,35},{35,3},{4,36},{36... | collective-permute-start | bytes 1179656 | tf_op jit(solution)/shard_map/ppermute | solution.py:30
  126.4 12.4 %collective-permute-start.26 = (bf16[512,384]{1,0:T(8,128)(2,1)}, bf16[512,384]{1,0:T(8,128)(2,1)}, u32[]{:S(2)}, u32[]{:S(2)}) collective-permute-start(bf16[512,384]{1,0:T(8,128)(2,1)} %shard_map.91.refs_0_), channel_id=1, source_target_pairs={{0,64},{64,0},{1,65},{65,1},{2,66},{66,2},{3,67},{67,3},{4,68},{68... | collective-permute-start | bytes 1179656 | tf_op jit(solution)/shard_map/ppermute | solution.py:30
  128.4 2.0 %collective-permute-start.30 = (bf16[512,256]{1,0:T(8,128)(2,1)}, bf16[512,256]{1,0:T(8,128)(2,1)}, u32[]{:S(2)}, u32[]{:S(2)}) collective-permute-start(bf16[512,256]{1,0:T(8,128)(2,1)} %collective-permute-done.28.refs_2_), channel_id=1, source_target_pairs={{0,32},{32,0},{1,33},{33,1},{2,34},{34,2},{3,35},{35,3},{4,36},{36... | collective-permute-start | bytes 786440 | tf_op jit(solution)/shard_map/ppermute | solution.py:30
  138.8 2.0 %collective-permute-start.32 = (bf16[512,384]{1,0:T(8,128)(2,1)}, bf16[512,384]{1,0:T(8,128)(2,1)S(1)}, u32[]{:S(2)}, u32[]{:S(2)}) collective-permute-start(bf16[512,384]{1,0:T(8,128)(2,1)} %collective-permute-done.26.refs_0_), channel_id=1, source_target_pairs={{0,32},{32,0},{1,33},{33,1},{2,34},{34,2},{3,35},{35,3},{4,36},{36... | collective-permute-start | bytes 1179656 | tf_op jit(solution)/shard_map/ppermute | solution.py:30
  (10 other events, 108.4 us)

commit v5 on v4

--- a/solution.py
+++ b/solution.py
@@ -13,7 +13,8 @@
 SCALE = 1.0 / DH**0.5
 LOG2_SCALE = SCALE * math.log2(math.e)
 NEAR = 4
-STAT_LANES = 32
+STAT_LANES = 8
+FOLD = ROWS // 4
 VMEM = 28 * 2**20
 VMEM_FIRST = 60 * 2**20
 SHORT = pl.CostEstimate(flops=1, bytes_accessed=1, transcendentals=0)
@@ -59,18 +60,24 @@
 
 
 def three_parts(value):
-    high = value.astype(jnp.bfloat16).astype(jnp.float32)
-    rest = value - high
+    folded = value[0:FOLD]
+    for g in range(1, 4):
+        folded = folded + pltpu.roll(value[g * FOLD : (g + 1) * FOLD], g * DH // 4, 1)
+    high = folded.astype(jnp.bfloat16).astype(jnp.float32)
+    rest = folded - high
     middle = rest.astype(jnp.bfloat16).astype(jnp.float32)
     low = rest - middle
     return high + pltpu.roll(middle, STAT_LANES, 1) + pltpu.roll(low, 2 * STAT_LANES, 1)
 
 
 def from_three(parts):
-    return (
+    folded = (
         parts
         + pltpu.roll(parts, DH - STAT_LANES, 1)
         + pltpu.roll(parts, DH - 2 * STAT_LANES, 1)
+    )
+    return jnp.concatenate(
+        [folded] + [pltpu.roll(folded, DH - g * DH // 4, 1) for g in range(1, 4)], axis=0
     )
 
 
@@ -121,7 +128,7 @@
         at = pl.multiple_of(head * 2 * ROWS, 2 * ROWS)
         outs[i][pl.ds(at, ROWS), :] = out.astype(jnp.bfloat16)
         outs[i][pl.ds(at + ROWS, ROWS), :] = tangent.astype(jnp.bfloat16)
-        tail = slice(2 * heads * ROWS, (2 * heads + 1) * ROWS)
+        tail = slice(2 * heads * ROWS, 2 * heads * ROWS + FOLD)
         stats = jnp.where(lane == 2 * head, log_sum, 0.0)
         stats = three_parts(jnp.where(lane == 2 * head + 1, mean, stats))
         before = jnp.where(head == 0, 0.0, outs[i][tail, :].astype(jnp.float32))
@@ -142,14 +149,14 @@
     heads = queries[0].shape[0] // (2 * ROWS)
     slices = len(queries)
     head_spec = pl.BlockSpec((2 * ROWS, DH), lambda h: (h, 0))
-    stats_spec = pl.BlockSpec((ROWS, DH), lambda h: (2 * heads, 0))
+    stats_spec = pl.BlockSpec((FOLD, DH), lambda h: (2 * heads * ROWS // FOLD, 0))
     halved = [isinstance(b, tuple) for b in blocks]
     value_specs = [
         pl.BlockSpec((2 * ROWS, DH), lambda h, w=w: (h if w else HELD + h, 0)) for w in halved
     ]
     keys = [b[0] if w else b for b, w in zip(blocks, halved)]
     values = [b[1] if w else b for b, w in zip(blocks, halved)]
-    part_type = jax.ShapeDtypeStruct(((2 * heads + 1) * ROWS, DH), jnp.bfloat16)
+    part_type = jax.ShapeDtypeStruct((2 * heads * ROWS + FOLD, DH), jnp.bfloat16)
     return pl.pallas_call(
         functools.partial(attend_kernel, slices, len(blocks), heads, len(partials)),
         grid=(heads,),
@@ -192,7 +199,7 @@
 
 
 def combine(parts):
-    heads = (parts[0].shape[0] // ROWS - 1) // 2
+    heads = parts[0].shape[0] // (2 * ROWS)
     return pl.pallas_call(
         functools.partial(combine_kernel, heads),
         out_shape=jax.ShapeDtypeStruct((2 * ROWS, heads * DH), jnp.bfloat16),

time: 145 us -> 141 us (0.972)
  waiting for transfers between devices: 35.8 us -> 30.3 us
    ppermute x20, waiting for transfers between devices: 32.2 us -> 26.9 us  [shift(): lax.ppermute(array, axis, [(i, (i + by) % NEAR) for i in range(NEAR)])]
  transfers between devices with their start and end apart: 33 -> 33, of which waited for: 15 -> 14; matrix products, arithmetic and copies ran while one was open for 3% -> 3% of each run, Pallas kernels for 27% -> 29%
where the time goes in v5:
time: 141 us
  starting transfers between devices  52 us (37%)
  Pallas kernels  48.1 us (34%)
  waiting for transfers between devices  30.3 us (21%)
  local copies, waits for them, and re-layouts  9.52 us (7%)
    pallas_call x4, Pallas kernels, attend(): pl.pallas_call(functools.partial(attend_kernel, slices, len(blocks), head...  32.2 us
    ppermute x20, starting transfers between devices, shift(): lax.ppermute(array, axis, [(i, (i + by) % NEAR) for i in range(NEAR)])  27.3 us
    ppermute x20, waiting for transfers between devices, shift(): lax.ppermute(array, axis, [(i, (i + by) % NEAR) for i in range(NEAR)])  26.9 us
    ppermute x11, starting transfers between devices, other(): return lax.ppermute(array, axis, [(0, 1), (1, 0)])  22.9 us
    pallas_call x2, Pallas kernels, project(): pl.pallas_call(functools.partial(project_kernel, terms, len(pieces), len(...  9.33 us
    unnamed x18, local copies, waits for them, and re-layouts  4.87 us
    dynamic_slice x1, local copies, waits for them, and re-layouts, weight_slices(): lax.dynamic_slice_in_dim(out_weight, at * width, width, axis=1)  4.54 us
    pallas_call x2, Pallas kernels, combine(): pl.pallas_call(functools.partial(combine_kernel, heads), out_shape=jax.Sh...  3.41 us
  transfers between devices with their start and end apart: 33, of which 14 were waited for; matrix products, arithmetic and copies ran while one was open for 3% of the time, Pallas kernels for 29%

profile of v5, /device:TPU:1, one launch (start us, length us, event | category | flops | bytes accessed | tf_op | source)
XLA Modules:
  0.0 140.8 jit_solution(6417143552568091117)
XLA Ops:
  0.6 3.2 %shard_map.86 = (bf16[3072,128]{1,0:T(8,128)(2,1)}, bf16[1024,128]{1,0:T(8,128)(2,1)}, bf16[3072,128]{1,0:T(8,128)(2,1)}, bf16[1536,128]{1,0:T(8,128)(2,1)}) custom-call(s32[1]{0:T(128)} %bitcast.at_ref, bf16[256,640]{1,0:T(8,128)(2,1)} %refs_0_.1, bf16[256,640]{1,0:T(8,128)(2,1)} %refs_1_.1, bf16[256,640]{1,0:T(8,128)(2,1)} %refs_2_.1, ...), custom_call_target="tpu_custom_call" | custom-call | flops 1 | bytes 1 | tf_op jit(solution)/shard_map/pallas_call | solution.py:312
  3.8 3.6 %collective-permute-start.2 = (bf16[1024,128]{1,0:T(8,128)(2,1)}, bf16[1024,128]{1,0:T(8,128)(2,1)S(1)}, u32[]{:S(2)}, u32[]{:S(2)}) collective-permute-start(bf16[1024,128]{1,0:T(8,128)(2,1)} %get-tuple-element.49), channel_id=1, source_target_pairs={{0,16},{16,0},{1,17},{17,1},{2,18},{18,2},{3,19},{19,3},{4,20},{20... | collective-permute-start | bytes 786440 | tf_op jit(solution)/shard_map/ppermute | solution.py:31
  8.7 1.4 %collective-permute-start.9 = (bf16[3072,128]{1,0:T(8,128)(2,1)}, bf16[3072,128]{1,0:T(8,128)(2,1)S(1)}, u32[]{:S(2)}, u32[]{:S(2)}) collective-permute-start(bf16[3072,128]{1,0:T(8,128)(2,1)} %get-tuple-element.55.refs_4_.refs_8_), channel_id=1, source_target_pairs={{0,12},{4,0},{8,4},{12,8},{1,13},{5,1},{9,5},{13,9},{2,14},{6,2},{... | collective-permute-start | bytes 2359304 | tf_op jit(solution)/shard_map/ppermute | solution.py:27
  10.2 1.6 %collective-permute-start = (bf16[1536,128]{1,0:T(8,128)(2,1)}, bf16[1536,128]{1,0:T(8,128)(2,1)S(1)}, u32[]{:S(2)}, u32[]{:S(2)}) collective-permute-start(bf16[1536,128]{1,0:T(8,128)(2,1)} %get-tuple-element.73.refs_0_), channel_id=1, source_target_pairs={{0,1},{1,2},{2,3},{3,0},{4,5},{5,6},{6,7},{7,4},{8,9},{9,10},{10,1... | collective-permute-start | bytes 1179656 | tf_op jit(solution)/shard_map/ppermute | solution.py:27
  11.8 2.1 %collective-permute-start.1 = (bf16[1536,128]{1,0:T(8,128)(2,1)}, bf16[1536,128]{1,0:T(8,128)(2,1)S(1)}, u32[]{:S(2)}, u32[]{:S(2)}) collective-permute-start(bf16[1536,128]{1,0:T(8,128)(2,1)} %get-tuple-element.73.refs_0_), channel_id=1, source_target_pairs={{0,3},{1,0},{2,1},{3,2},{4,7},{5,4},{6,5},{7,6},{8,11},{9,8},{10,9... | collective-permute-start | bytes 1179656 | tf_op jit(solution)/shard_map/ppermute | solution.py:27
  13.9 2.4 %collective-permute-start.7 = (bf16[3072,128]{1,0:T(8,128)(2,1)}, bf16[3072,128]{1,0:T(8,128)(2,1)S(1)}, u32[]{:S(2)}, u32[]{:S(2)}) collective-permute-start(bf16[3072,128]{1,0:T(8,128)(2,1)} %get-tuple-element.54), channel_id=1, source_target_pairs={{0,16},{16,0},{1,17},{17,1},{2,18},{18,2},{3,19},{19,3},{4,20},{20... | collective-permute-start | bytes 2359304 | tf_op jit(solution)/shard_map/ppermute | solution.py:31
  16.3 4.5 %constant_dynamic-slice_fusion = (bf16[640,1280]{1,0:T(8,128)(2,1)S(1)}, bf16[640,1280]{1,0:T(8,128)(2,1)S(1)}, bf16[640,1280]{1,0:T(8,128)(2,1)}, bf16[640,1280]{1,0:T(8,128)(2,1)S(1)}) fusion(bf16[640,5120]{1,0:T(8,128)(2,1)} %param.13, s32[]{:T(128)S(6)} %select_n.15, s32[]{:T(128)S(6)} %select_n.13, s32[]{:T(128)S(6)} %select_n.12, s32[]{:T(128)S(6)} %select_n.14), kind=kLoop, calls=%fused_computation | loop fusion | bytes 13107216 | tf_op jit(solution)/shard_map/dynamic_slice | solution.py:287
  22.1 2.5 %collective-permute-start.3 = (bf16[1536,128]{1,0:T(8,128)(2,1)S(1)}, bf16[1536,128]{1,0:T(8,128)(2,1)S(1)}, u32[]{:S(2)}, u32[]{:S(2)}) collective-permute-start(bf16[1536,128]{1,0:T(8,128)(2,1)S(1)} %copy-done.4), channel_id=1, source_target_pairs={{0,2},{1,3},{2,0},{3,1},{4,6},{5,7},{6,4},{7,5},{8,10},{9,11},{10,... | collective-permute-start | bytes 1179656 | tf_op jit(solution)/shard_map/ppermute | solution.py:27
  24.6 2.5 %collective-permute-done.8.refs_5_.refs_9_ = bf16[3072,128]{1,0:T(8,128)(2,1)S(1)} collective-permute-done((bf16[3072,128]{1,0:T(8,128)(2,1)}, bf16[3072,128]{1,0:T(8,128)(2,1)S(1)}, u32[]{:S(2)}, u32[]{:S(2)}) %collective-permute-start.8) | collective-permute-done | bytes 786464 | tf_op jit(solution)/shard_map/ppermute | solution.py:27
  28.1 1.8 %collective-permute-start.11 = (bf16[1536,128]{1,0:T(8,128)(2,1)S(1)}, bf16[1536,128]{1,0:T(8,128)(2,1)S(1)}, u32[]{:S(2)}, u32[]{:S(2)}) collective-permute-start(bf16[1536,128]{1,0:T(8,128)(2,1)S(1)} %slice.17), channel_id=1, source_target_pairs={{0,12},{4,0},{8,4},{12,8},{1,13},{5,1},{9,5},{13,9},{2,14},{6,2},{... | collective-permute-start | bytes 1179656 | tf_op jit(solution)/shard_map/ppermute | solution.py:27
  29.9 2.3 %collective-permute-done.3.refs_3_ = bf16[1536,128]{1,0:T(8,128)(2,1)S(1)} collective-permute-done((bf16[1536,128]{1,0:T(8,128)(2,1)S(1)}, bf16[1536,128]{1,0:T(8,128)(2,1)S(1)}, u32[]{:S(2)}, u32[]{:S(2)}) %collective-permute-start.3) | collective-permute-done | bytes 393248 | tf_op jit(solution)/shard_map/ppermute | solution.py:27
  32.2 2.7 %collective-permute-start.5 = (bf16[1024,128]{1,0:T(8,128)(2,1)S(1)}, bf16[1024,128]{1,0:T(8,128)(2,1)S(1)}, u32[]{:S(2)}, u32[]{:S(2)}) collective-permute-start(bf16[1024,128]{1,0:T(8,128)(2,1)S(1)} %collective-permute-done.2.refs_0_), channel_id=1, source_target_pairs={{0,3},{1,0},{2,1},{3,2},{4,7},{5,4},{6,5},{7,6},{8,11},{9,8},{10,9... | collective-permute-start | bytes 786440 | tf_op jit(solution)/shard_map/ppermute | solution.py:27
  34.9 4.1 %collective-permute-done.4.refs_1_ = bf16[1024,128]{1,0:T(8,128)(2,1)S(1)} collective-permute-done((bf16[1024,128]{1,0:T(8,128)(2,1)S(1)}, bf16[1024,128]{1,0:T(8,128)(2,1)S(1)}, u32[]{:S(2)}, u32[]{:S(2)}) %collective-permute-start.4) | collective-permute-done | bytes 262176 | tf_op jit(solution)/shard_map/ppermute | solution.py:27
  38.9 2.5 %collective-permute-start.6 = (bf16[1024,128]{1,0:T(8,128)(2,1)S(1)}, bf16[1024,128]{1,0:T(8,128)(2,1)S(1)}, u32[]{:S(2)}, u32[]{:S(2)}) collective-permute-start(bf16[1024,128]{1,0:T(8,128)(2,1)S(1)} %collective-permute-done.2.refs_0_), channel_id=1, source_target_pairs={{0,2},{1,3},{2,0},{3,1},{4,6},{5,7},{6,4},{7,5},{8,10},{9,11},{10,... | collective-permute-start | bytes 786440 | tf_op jit(solution)/shard_map/ppermute | solution.py:27
  42.4 1.7 %collective-permute-start.12 = (bf16[3072,128]{1,0:T(8,128)(2,1)S(1)}, bf16[3072,128]{1,0:T(8,128)(2,1)S(1)}, u32[]{:S(2)}, u32[]{:S(2)}) collective-permute-start(bf16[3072,128]{1,0:T(8,128)(2,1)S(1)} %collective-permute-done.7.refs_4_.refs_8_), channel_id=1, source_target_pairs={{0,4},{4,8},{8,12},{12,0},{1,5},{5,9},{9,13},{13,1},{2,6},{6,10},{... | collective-permute-start | bytes 2359304 | tf_op jit(solution)/shard_map/ppermute | solution.py:27
  44.0 1.5 %collective-permute-start.13 = (bf16[3072,128]{1,0:T(8,128)(2,1)S(1)}, bf16[3072,128]{1,0:T(8,128)(2,1)S(1)}, u32[]{:S(2)}, u32[]{:S(2)}) collective-permute-start(bf16[3072,128]{1,0:T(8,128)(2,1)S(1)} %collective-permute-done.7.refs_4_.refs_8_), channel_id=1, source_target_pairs={{0,12},{4,0},{8,4},{12,8},{1,13},{5,1},{9,5},{13,9},{2,14},{6,2},{... | collective-permute-start | bytes 2359304 | tf_op jit(solution)/shard_map/ppermute | solution.py:27
  47.6 8.9 %shard_map.87 = (bf16[1600,128]{1,0:T(8,128)(2,1)S(1)}, bf16[1600,128]{1,0:T(8,128)(2,1)S(1)}, bf16[1600,128]{1,0:T(8,128)(2,1)S(1)}, bf16[1600,128]{1,0:T(8,128)(2,1)S(1)}) custom-call(bf16[1536,128]{1,0:T(8,128)(2,1)S(1)} %copy-done.4, bf16[1536,128]{1,0:T(8,128)(2,1)S(1)} %copy-done.6, bf16[1536,128]{1,0:T(8,128)(2,1)S(1)} %copy-done.8, ...), custom_call_target="tpu_custom_call" | custom-call | flops 12884901888 | bytes 7864320 | tf_op jit(solution)/shard_map/pallas_call | solution.py:160
  56.5 1.5 %collective-permute-done.12.refs_5_.refs_9_ = bf16[3072,128]{1,0:T(8,128)(2,1)S(1)} collective-permute-done((bf16[3072,128]{1,0:T(8,128)(2,1)S(1)}, bf16[3072,128]{1,0:T(8,128)(2,1)S(1)}, u32[]{:S(2)}, u32[]{:S(2)}) %collective-permute-start.12) | collective-permute-done | bytes 786464 | tf_op jit(solution)/shard_map/ppermute | solution.py:27
  60.9 6.0 %shard_map.88 = (bf16[1088,128]{1,0:T(8,128)(2,1)S(1)}, bf16[1088,128]{1,0:T(8,128)(2,1)S(1)}, bf16[1088,128]{1,0:T(8,128)(2,1)S(1)}, bf16[1088,128]{1,0:T(8,128)(2,1)S(1)}) custom-call(bf16[1024,128]{1,0:T(8,128)(2,1)S(1)} %collective-permute-done.2.refs_0_, bf16[1024,128]{1,0:T(8,128)(2,1)S(1)} %collective-permute-done.4.refs_1_, ...), custom_call_target="tpu_custom_call" | custom-call | flops 8589934592 | bytes 5242880 | tf_op jit(solution)/shard_map/pallas_call | solution.py:160
  67.8 6.9 %shard_map.89 = (bf16[1088,128]{1,0:T(8,128)(2,1)S(1)}, bf16[1088,128]{1,0:T(8,128)(2,1)S(1)}, bf16[1088,128]{1,0:T(8,128)(2,1)S(1)}, bf16[1088,128]{1,0:T(8,128)(2,1)S(1)}) custom-call(bf16[1024,128]{1,0:T(8,128)(2,1)S(1)} %collective-permute-done.2.refs_0_, bf16[1024,128]{1,0:T(8,128)(2,1)S(1)} %collective-permute-done.4.refs_1_, ...), custom_call_target="tpu_custom_call" | custom-call | flops 8589934592 | bytes 5242880 | tf_op jit(solution)/shard_map/pallas_call | solution.py:160
  74.8 7.3 %collective-permute-start.21 = (bf16[640,1280]{1,0:T(8,128)(2,1)S(1)}, bf16[640,1280]{1,0:T(8,128)(2,1)S(1)}, u32[]{:S(2)}, u32[]{:S(2)}) collective-permute-start(bf16[640,1280]{1,0:T(8,128)(2,1)S(1)} %get-tuple-element.83), channel_id=1, source_target_pairs={{0,32},{32,0},{1,33},{33,1},{2,34},{34,2},{3,35},{35,3},{4,36},{36... | collective-permute-start | bytes 4915208 | tf_op jit(solution)/shard_map/ppermute | solution.py:31
  83.9 10.4 %shard_map.90 = (bf16[1600,128]{1,0:T(8,128)(2,1)S(1)}, bf16[1600,128]{1,0:T(8,128)(2,1)S(1)}, bf16[1600,128]{1,0:T(8,128)(2,1)S(1)}, bf16[1600,128]{1,0:T(8,128)(2,1)S(1)}) custom-call(bf16[1536,128]{1,0:T(8,128)(2,1)S(1)} %copy-done.4, bf16[1536,128]{1,0:T(8,128)(2,1)S(1)} %copy-done.6, bf16[1536,128]{1,0:T(8,128)(2,1)S(1)} %copy-done.8, ...), custom_call_target="tpu_custom_call" | custom-call | flops 12884901888 | bytes 7864320 | tf_op jit(solution)/shard_map/pallas_call | solution.py:160
  94.3 3.1 %collective-permute-done.17.refs_2_ = bf16[1088,128]{1,0:T(8,128)(2,1)S(1)} collective-permute-done((bf16[1088,128]{1,0:T(8,128)(2,1)S(1)}, bf16[1088,128]{1,0:T(8,128)(2,1)S(1)}, u32[]{:S(2)}, u32[]{:S(2)}) %collective-permute-start.17) | collective-permute-done | bytes 278560 | tf_op jit(solution)/shard_map/ppermute | solution.py:27
  101.4 3.3 %collective-permute-start.27 = (bf16[512,256]{1,0:T(8,128)(2,1)S(1)}, bf16[512,256]{1,0:T(8,128)(2,1)S(1)}, u32[]{:S(2)}, u32[]{:S(2)}) collective-permute-start(bf16[512,256]{1,0:T(8,128)(2,1)S(1)} %shard_map.92), channel_id=1, source_target_pairs={{0,16},{16,0},{1,17},{17,1},{2,18},{18,2},{3,19},{19,3},{4,20},{20... | collective-permute-start | bytes 786440 | tf_op jit(solution)/shard_map/ppermute | solution.py:31
  106.9 3.5 %collective-permute-done.24.refs_2_ = bf16[1600,128]{1,0:T(8,128)(2,1)S(1)} collective-permute-done((bf16[1600,128]{1,0:T(8,128)(2,1)S(1)}, bf16[1600,128]{1,0:T(8,128)(2,1)S(1)}, u32[]{:S(2)}, u32[]{:S(2)}) %collective-permute-start.24) | collective-permute-done | bytes 409632 | tf_op jit(solution)/shard_map/ppermute | solution.py:27
  110.4 6.3 %collective-permute-done.25.refs_3_ = bf16[1600,128]{1,0:T(8,128)(2,1)S(1)} collective-permute-done((bf16[1600,128]{1,0:T(8,128)(2,1)S(1)}, bf16[1600,128]{1,0:T(8,128)(2,1)S(1)}, u32[]{:S(2)}, u32[]{:S(2)}) %collective-permute-start.25) | collective-permute-done | bytes 409632 | tf_op jit(solution)/shard_map/ppermute | solution.py:27
  116.7 2.2 %shard_map.91.refs_0_ = bf16[512,384]{1,0:T(8,128)(2,1)} custom-call(bf16[1600,128]{1,0:T(8,128)(2,1)S(1)} %get-tuple-element.85.refs_0_, bf16[1600,128]{1,0:T(8,128)(2,1)S(1)} %collective-permute-done.23.refs_1_, bf16[1600,128]{1,0:T(8,128)(2,1)S(1)} %collective-permute-done.24.refs_2_, bf16[1600,128]{1,0:T(8,128)(2,1)S(1)} %collective-permute-done.25.refs_3_), custom_call_target="tpu_custom_call" | custom-call | flops 1 | bytes 1 | tf_op jit(solution)/shard_map/pallas_call | solution.py:203
  118.9 3.7 %collective-permute-start.31 = (bf16[512,384]{1,0:T(8,128)(2,1)}, bf16[512,384]{1,0:T(8,128)(2,1)}, u32[]{:S(2)}, u32[]{:S(2)}) collective-permute-start(bf16[512,384]{1,0:T(8,128)(2,1)} %shard_map.91.refs_0_), channel_id=1, source_target_pairs={{0,32},{32,0},{1,33},{33,1},{2,34},{34,2},{3,35},{35,3},{4,36},{36... | collective-permute-start | bytes 1179656 | tf_op jit(solution)/shard_map/ppermute | solution.py:31
  122.6 1.7 %collective-permute-start.26 = (bf16[512,384]{1,0:T(8,128)(2,1)}, bf16[512,384]{1,0:T(8,128)(2,1)}, u32[]{:S(2)}, u32[]{:S(2)}) collective-permute-start(bf16[512,384]{1,0:T(8,128)(2,1)} %shard_map.91.refs_0_), channel_id=1, source_target_pairs={{0,64},{64,0},{1,65},{65,1},{2,66},{66,2},{3,67},{67,3},{4,68},{68... | collective-permute-start | bytes 1179656 | tf_op jit(solution)/shard_map/ppermute | solution.py:31
  129.4 5.6 %shard_map.93.refs_4_ = f32[512,1280]{1,0:T(8,128)S(1)} custom-call(s32[2]{0:T(128)S(1)} %pad_add_fusion.at_ref, bf16[512,384]{1,0:T(8,128)(2,1)} %shard_map.91.refs_0_, bf16[512,256]{1,0:T(8,128)(2,1)S(1)} %collective-permute-done.27.refs_1_, bf16[512,256]{1,0:T(8,128)(2,1)} %collective-permute-done.28.refs_2_, ...), custom_call_target="tpu_custom_call" | custom-call | flops 1 | bytes 1 | tf_op jit(solution)/shard_map/pallas_call | solution.py:267
  135.4 1.6 %collective-permute-done.32.refs_1_ = bf16[512,384]{1,0:T(8,128)(2,1)S(1)} collective-permute-done((bf16[512,384]{1,0:T(8,128)(2,1)}, bf16[512,384]{1,0:T(8,128)(2,1)S(1)}, u32[]{:S(2)}, u32[]{:S(2)}) %collective-permute-start.32) | collective-permute-done | bytes 393248 | tf_op jit(solution)/shard_map/ppermute | solution.py:31
  137.0 3.7 %shard_map.94 = (bf16[256,1280]{1,0:T(8,128)(2,1)}, bf16[256,1280]{1,0:T(8,128)(2,1)}) custom-call(s32[2]{0:T(128)S(1)} %pad_add_fusion.at_ref, bf16[512,384]{1,0:T(8,128)(2,1)} %collective-permute-done.26.refs_0_, bf16[512,384]{1,0:T(8,128)(2,1)S(1)} %collective-permute-done.32.refs_1_, bf16[640,1280]{1,0:T(8,128)(2,1)S(1)} %collective-permute-done.20.refs_7_.refs_2_, ...), custom_call_target="tpu_custom_call" | custom-call | flops 1 | bytes 1 | tf_op jit(solution)/shard_map/pallas_call | solution.py:267
  (67 shorter events, 23.9 us)
Async XLA Ops:
  3.8 10.1 %collective-permute-start.2 = (bf16[1024,128]{1,0:T(8,128)(2,1)}, bf16[1024,128]{1,0:T(8,128)(2,1)S(1)}, u32[]{:S(2)}, u32[]{:S(2)}) collective-permute-start(bf16[1024,128]{1,0:T(8,128)(2,1)} %get-tuple-element.49), channel_id=1, source_target_pairs={{0,16},{16,0},{1,17},{17,1},{2,18},{18,2},{3,19},{19,3},{4,20},{20... | collective-permute-start | bytes 786440 | tf_op jit(solution)/shard_map/ppermute | solution.py:31
  7.4 19.6 %collective-permute-start.8 = (bf16[3072,128]{1,0:T(8,128)(2,1)}, bf16[3072,128]{1,0:T(8,128)(2,1)S(1)}, u32[]{:S(2)}, u32[]{:S(2)}) collective-permute-start(bf16[3072,128]{1,0:T(8,128)(2,1)} %get-tuple-element.55.refs_4_.refs_8_), channel_id=1, source_target_pairs={{0,4},{4,8},{8,12},{12,0},{1,5},{5,9},{9,13},{13,1},{2,6},{6,10},{... | collective-permute-start | bytes 2359304 | tf_op jit(solution)/shard_map/ppermute | solution.py:27
  8.7 18.4 %collective-permute-start.9 = (bf16[3072,128]{1,0:T(8,128)(2,1)}, bf16[3072,128]{1,0:T(8,128)(2,1)S(1)}, u32[]{:S(2)}, u32[]{:S(2)}) collective-permute-start(bf16[3072,128]{1,0:T(8,128)(2,1)} %get-tuple-element.55.refs_4_.refs_8_), channel_id=1, source_target_pairs={{0,12},{4,0},{8,4},{12,8},{1,13},{5,1},{9,5},{13,9},{2,14},{6,2},{... | collective-permute-start | bytes 2359304 | tf_op jit(solution)/shard_map/ppermute | solution.py:27
  10.2 11.9 %collective-permute-start = (bf16[1536,128]{1,0:T(8,128)(2,1)}, bf16[1536,128]{1,0:T(8,128)(2,1)S(1)}, u32[]{:S(2)}, u32[]{:S(2)}) collective-permute-start(bf16[1536,128]{1,0:T(8,128)(2,1)} %get-tuple-element.73.refs_0_), channel_id=1, source_target_pairs={{0,1},{1,2},{2,3},{3,0},{4,5},{5,6},{6,7},{7,4},{8,9},{9,10},{10,1... | collective-permute-start | bytes 1179656 | tf_op jit(solution)/shard_map/ppermute | solution.py:27
  11.8 10.3 %collective-permute-start.1 = (bf16[1536,128]{1,0:T(8,128)(2,1)}, bf16[1536,128]{1,0:T(8,128)(2,1)S(1)}, u32[]{:S(2)}, u32[]{:S(2)}) collective-permute-start(bf16[1536,128]{1,0:T(8,128)(2,1)} %get-tuple-element.73.refs_0_), channel_id=1, source_target_pairs={{0,3},{1,0},{2,1},{3,2},{4,7},{5,4},{6,5},{7,6},{8,11},{9,8},{10,9... | collective-permute-start | bytes 1179656 | tf_op jit(solution)/shard_map/ppermute | solution.py:27
  13.9 27.5 %collective-permute-start.7 = (bf16[3072,128]{1,0:T(8,128)(2,1)}, bf16[3072,128]{1,0:T(8,128)(2,1)S(1)}, u32[]{:S(2)}, u32[]{:S(2)}) collective-permute-start(bf16[3072,128]{1,0:T(8,128)(2,1)} %get-tuple-element.54), channel_id=1, source_target_pairs={{0,16},{16,0},{1,17},{17,1},{2,18},{18,2},{3,19},{19,3},{4,20},{20... | collective-permute-start | bytes 2359304 | tf_op jit(solution)/shard_map/ppermute | solution.py:31
  22.1 10.1 %collective-permute-start.3 = (bf16[1536,128]{1,0:T(8,128)(2,1)S(1)}, bf16[1536,128]{1,0:T(8,128)(2,1)S(1)}, u32[]{:S(2)}, u32[]{:S(2)}) collective-permute-start(bf16[1536,128]{1,0:T(8,128)(2,1)S(1)} %copy-done.4), channel_id=1, source_target_pairs={{0,2},{1,3},{2,0},{3,1},{4,6},{5,7},{6,4},{7,5},{8,10},{9,11},{10,... | collective-permute-start | bytes 1179656 | tf_op jit(solution)/shard_map/ppermute | solution.py:27
  27.1 15.2 %collective-permute-start.10 = (bf16[1536,128]{1,0:T(8,128)(2,1)S(1)}, bf16[1536,128]{1,0:T(8,128)(2,1)S(1)}, u32[]{:S(2)}, u32[]{:S(2)}) collective-permute-start(bf16[1536,128]{1,0:T(8,128)(2,1)S(1)} %slice.16), channel_id=1, source_target_pairs={{0,4},{4,8},{8,12},{12,0},{1,5},{5,9},{9,13},{13,1},{2,6},{6,10},{... | collective-permute-start | bytes 1179656 | tf_op jit(solution)/shard_map/ppermute | solution.py:27
  28.1 14.2 %collective-permute-start.11 = (bf16[1536,128]{1,0:T(8,128)(2,1)S(1)}, bf16[1536,128]{1,0:T(8,128)(2,1)S(1)}, u32[]{:S(2)}, u32[]{:S(2)}) collective-permute-start(bf16[1536,128]{1,0:T(8,128)(2,1)S(1)} %slice.17), channel_id=1, source_target_pairs={{0,12},{4,0},{8,4},{12,8},{1,13},{5,1},{9,5},{13,9},{2,14},{6,2},{... | collective-permute-start | bytes 1179656 | tf_op jit(solution)/shard_map/ppermute | solution.py:27
  32.2 6.7 %collective-permute-start.4 = (bf16[1024,128]{1,0:T(8,128)(2,1)S(1)}, bf16[1024,128]{1,0:T(8,128)(2,1)S(1)}, u32[]{:S(2)}, u32[]{:S(2)}) collective-permute-start(bf16[1024,128]{1,0:T(8,128)(2,1)S(1)} %collective-permute-done.2.refs_0_), channel_id=1, source_target_pairs={{0,1},{1,2},{2,3},{3,0},{4,5},{5,6},{6,7},{7,4},{8,9},{9,10},{10,1... | collective-permute-start | bytes 786440 | tf_op jit(solution)/shard_map/ppermute | solution.py:27
  32.2 6.7 %collective-permute-start.5 = (bf16[1024,128]{1,0:T(8,128)(2,1)S(1)}, bf16[1024,128]{1,0:T(8,128)(2,1)S(1)}, u32[]{:S(2)}, u32[]{:S(2)}) collective-permute-start(bf16[1024,128]{1,0:T(8,128)(2,1)S(1)} %collective-permute-done.2.refs_0_), channel_id=1, source_target_pairs={{0,3},{1,0},{2,1},{3,2},{4,7},{5,4},{6,5},{7,6},{8,11},{9,8},{10,9... | collective-permute-start | bytes 786440 | tf_op jit(solution)/shard_map/ppermute | solution.py:27
  38.9 21.9 %collective-permute-start.6 = (bf16[1024,128]{1,0:T(8,128)(2,1)S(1)}, bf16[1024,128]{1,0:T(8,128)(2,1)S(1)}, u32[]{:S(2)}, u32[]{:S(2)}) collective-permute-start(bf16[1024,128]{1,0:T(8,128)(2,1)S(1)} %collective-permute-done.2.refs_0_), channel_id=1, source_target_pairs={{0,2},{1,3},{2,0},{3,1},{4,6},{5,7},{6,4},{7,5},{8,10},{9,11},{10,... | collective-permute-start | bytes 786440 | tf_op jit(solution)/shard_map/ppermute | solution.py:27
  41.4 33.4 %collective-permute-start.19 = (bf16[640,1280]{1,0:T(8,128)(2,1)S(1)}, bf16[640,1280]{1,0:T(8,128)(2,1)S(1)}, u32[]{:S(2)}, u32[]{:S(2)}) collective-permute-start(bf16[640,1280]{1,0:T(8,128)(2,1)S(1)} %get-tuple-element.81), channel_id=1, source_target_pairs={{0,80},{16,64},{64,16},{80,0},{1,81},{17,65},{65,17},{81,1},{2,82}... | collective-permute-start | bytes 4915208 | tf_op jit(solution)/shard_map/ppermute | solution.py:339
  42.3 32.5 %collective-permute-start.20 = (bf16[640,1280]{1,0:T(8,128)(2,1)S(1)}, bf16[640,1280]{1,0:T(8,128)(2,1)S(1)}, u32[]{:S(2)}, u32[]{:S(2)}) collective-permute-start(bf16[640,1280]{1,0:T(8,128)(2,1)S(1)} %get-tuple-element.82), channel_id=1, source_target_pairs={{0,64},{64,0},{1,65},{65,1},{2,66},{66,2},{3,67},{67,3},{4,68},{68... | collective-permute-start | bytes 4915208 | tf_op jit(solution)/shard_map/ppermute | solution.py:31
  42.4 15.6 %collective-permute-start.12 = (bf16[3072,128]{1,0:T(8,128)(2,1)S(1)}, bf16[3072,128]{1,0:T(8,128)(2,1)S(1)}, u32[]{:S(2)}, u32[]{:S(2)}) collective-permute-start(bf16[3072,128]{1,0:T(8,128)(2,1)S(1)} %collective-permute-done.7.refs_4_.refs_8_), channel_id=1, source_target_pairs={{0,4},{4,8},{8,12},{12,0},{1,5},{5,9},{9,13},{13,1},{2,6},{6,10},{... | collective-permute-start | bytes 2359304 | tf_op jit(solution)/shard_map/ppermute | solution.py:27
  44.0 14.0 %collective-permute-start.13 = (bf16[3072,128]{1,0:T(8,128)(2,1)S(1)}, bf16[3072,128]{1,0:T(8,128)(2,1)S(1)}, u32[]{:S(2)}, u32[]{:S(2)}) collective-permute-start(bf16[3072,128]{1,0:T(8,128)(2,1)S(1)} %collective-permute-done.7.refs_4_.refs_8_), channel_id=1, source_target_pairs={{0,12},{4,0},{8,4},{12,8},{1,13},{5,1},{9,5},{13,9},{2,14},{6,2},{... | collective-permute-start | bytes 2359304 | tf_op jit(solution)/shard_map/ppermute | solution.py:27
  58.1 9.7 %collective-permute-start.14 = (bf16[1536,128]{1,0:T(8,128)(2,1)S(1)}, bf16[1536,128]{1,0:T(8,128)(2,1)S(1)}, u32[]{:S(2)}, u32[]{:S(2)}) collective-permute-start(bf16[1536,128]{1,0:T(8,128)(2,1)S(1)} %slice.18), channel_id=1, source_target_pairs={{0,4},{4,8},{8,12},{12,0},{1,5},{5,9},{9,13},{13,1},{2,6},{6,10},{... | collective-permute-start | bytes 1179656 | tf_op jit(solution)/shard_map/ppermute | solution.py:27
  59.5 8.3 %collective-permute-start.15 = (bf16[1536,128]{1,0:T(8,128)(2,1)S(1)}, bf16[1536,128]{1,0:T(8,128)(2,1)S(1)}, u32[]{:S(2)}, u32[]{:S(2)}) collective-permute-start(bf16[1536,128]{1,0:T(8,128)(2,1)S(1)} %slice.19), channel_id=1, source_target_pairs={{0,12},{4,0},{8,4},{12,8},{1,13},{5,1},{9,5},{13,9},{2,14},{6,2},{... | collective-permute-start | bytes 1179656 | tf_op jit(solution)/shard_map/ppermute | solution.py:27
  74.8 22.6 %collective-permute-start.21 = (bf16[640,1280]{1,0:T(8,128)(2,1)S(1)}, bf16[640,1280]{1,0:T(8,128)(2,1)S(1)}, u32[]{:S(2)}, u32[]{:S(2)}) collective-permute-start(bf16[640,1280]{1,0:T(8,128)(2,1)S(1)} %get-tuple-element.83), channel_id=1, source_target_pairs={{0,32},{32,0},{1,33},{33,1},{2,34},{34,2},{3,35},{35,3},{4,36},{36... | collective-permute-start | bytes 4915208 | tf_op jit(solution)/shard_map/ppermute | solution.py:31
  82.1 15.3 %collective-permute-start.22 = (bf16[640,1280]{1,0:T(8,128)(2,1)S(1)}, bf16[640,1280]{1,0:T(8,128)(2,1)S(1)}, u32[]{:S(2)}, u32[]{:S(2)}) collective-permute-start(bf16[640,1280]{1,0:T(8,128)(2,1)S(1)} %collective-permute-done.19), channel_id=1, source_target_pairs={{0,32},{32,0},{1,33},{33,1},{2,34},{34,2},{3,35},{35,3},{4,36},{36... | collective-permute-start | bytes 4915208 | tf_op jit(solution)/shard_map/ppermute | solution.py:31
  82.2 12.1 %collective-permute-start.16 = (bf16[1088,128]{1,0:T(8,128)(2,1)S(1)}, bf16[1088,128]{1,0:T(8,128)(2,1)S(1)}, u32[]{:S(2)}, u32[]{:S(2)}) collective-permute-start(bf16[1088,128]{1,0:T(8,128)(2,1)S(1)} %get-tuple-element.70), channel_id=1, source_target_pairs={{0,3},{1,0},{2,1},{3,2},{4,7},{5,4},{6,5},{7,6},{8,11},{9,8},{10,9... | collective-permute-start | bytes 835592 | tf_op jit(solution)/shard_map/ppermute | solution.py:27
  82.7 14.7 %collective-permute-start.17 = (bf16[1088,128]{1,0:T(8,128)(2,1)S(1)}, bf16[1088,128]{1,0:T(8,128)(2,1)S(1)}, u32[]{:S(2)}, u32[]{:S(2)}) collective-permute-start(bf16[1088,128]{1,0:T(8,128)(2,1)S(1)} %get-tuple-element.71), channel_id=1, source_target_pairs={{0,1},{1,2},{2,3},{3,0},{4,5},{5,6},{6,7},{7,4},{8,9},{9,10},{10,1... | collective-permute-start | bytes 835592 | tf_op jit(solution)/shard_map/ppermute | solution.py:27
  83.7 13.7 %collective-permute-start.18 = (bf16[1088,128]{1,0:T(8,128)(2,1)S(1)}, bf16[1088,128]{1,0:T(8,128)(2,1)S(1)}, u32[]{:S(2)}, u32[]{:S(2)}) collective-permute-start(bf16[1088,128]{1,0:T(8,128)(2,1)S(1)} %get-tuple-element.72), channel_id=1, source_target_pairs={{0,2},{1,3},{2,0},{3,1},{4,6},{5,7},{6,4},{7,5},{8,10},{9,11},{10,... | collective-permute-start | bytes 835592 | tf_op jit(solution)/shard_map/ppermute | solution.py:27
  97.4 9.5 %collective-permute-start.23 = (bf16[1600,128]{1,0:T(8,128)(2,1)S(1)}, bf16[1600,128]{1,0:T(8,128)(2,1)S(1)}, u32[]{:S(2)}, u32[]{:S(2)}) collective-permute-start(bf16[1600,128]{1,0:T(8,128)(2,1)S(1)} %get-tuple-element.86), channel_id=1, source_target_pairs={{0,3},{1,0},{2,1},{3,2},{4,7},{5,4},{6,5},{7,6},{8,11},{9,8},{10,9... | collective-permute-start | bytes 1228808 | tf_op jit(solution)/shard_map/ppermute | solution.py:27
  98.5 11.9 %collective-permute-start.24 = (bf16[1600,128]{1,0:T(8,128)(2,1)S(1)}, bf16[1600,128]{1,0:T(8,128)(2,1)S(1)}, u32[]{:S(2)}, u32[]{:S(2)}) collective-permute-start(bf16[1600,128]{1,0:T(8,128)(2,1)S(1)} %get-tuple-element.87), channel_id=1, source_target_pairs={{0,1},{1,2},{2,3},{3,0},{4,5},{5,6},{6,7},{7,4},{8,9},{9,10},{10,1... | collective-permute-start | bytes 1228808 | tf_op jit(solution)/shard_map/ppermute | solution.py:27
  99.0 17.7 %collective-permute-start.25 = (bf16[1600,128]{1,0:T(8,128)(2,1)S(1)}, bf16[1600,128]{1,0:T(8,128)(2,1)S(1)}, u32[]{:S(2)}, u32[]{:S(2)}) collective-permute-start(bf16[1600,128]{1,0:T(8,128)(2,1)S(1)} %get-tuple-element.88), channel_id=1, source_target_pairs={{0,2},{1,3},{2,0},{3,1},{4,6},{5,7},{6,4},{7,5},{8,10},{9,11},{10,... | collective-permute-start | bytes 1228808 | tf_op jit(solution)/shard_map/ppermute | solution.py:27
  101.4 22.9 %collective-permute-start.27 = (bf16[512,256]{1,0:T(8,128)(2,1)S(1)}, bf16[512,256]{1,0:T(8,128)(2,1)S(1)}, u32[]{:S(2)}, u32[]{:S(2)}) collective-permute-start(bf16[512,256]{1,0:T(8,128)(2,1)S(1)} %shard_map.92), channel_id=1, source_target_pairs={{0,16},{16,0},{1,17},{17,1},{2,18},{18,2},{3,19},{19,3},{4,20},{20... | collective-permute-start | bytes 786440 | tf_op jit(solution)/shard_map/ppermute | solution.py:31
  104.7 19.9 %collective-permute-start.28 = (bf16[512,256]{1,0:T(8,128)(2,1)S(1)}, bf16[512,256]{1,0:T(8,128)(2,1)}, u32[]{:S(2)}, u32[]{:S(2)}) collective-permute-start(bf16[512,256]{1,0:T(8,128)(2,1)S(1)} %shard_map.92), channel_id=1, source_target_pairs={{0,80},{16,64},{64,16},{80,0},{1,81},{17,65},{65,17},{81,1},{2,82}... | collective-permute-start | bytes 786440 | tf_op jit(solution)/shard_map/ppermute | solution.py:350
  118.9 7.6 %collective-permute-start.31 = (bf16[512,384]{1,0:T(8,128)(2,1)}, bf16[512,384]{1,0:T(8,128)(2,1)}, u32[]{:S(2)}, u32[]{:S(2)}) collective-permute-start(bf16[512,384]{1,0:T(8,128)(2,1)} %shard_map.91.refs_0_), channel_id=1, source_target_pairs={{0,32},{32,0},{1,33},{33,1},{2,34},{34,2},{3,35},{35,3},{4,36},{36... | collective-permute-start | bytes 1179656 | tf_op jit(solution)/shard_map/ppermute | solution.py:31
  122.6 12.4 %collective-permute-start.26 = (bf16[512,384]{1,0:T(8,128)(2,1)}, bf16[512,384]{1,0:T(8,128)(2,1)}, u32[]{:S(2)}, u32[]{:S(2)}) collective-permute-start(bf16[512,384]{1,0:T(8,128)(2,1)} %shard_map.91.refs_0_), channel_id=1, source_target_pairs={{0,64},{64,0},{1,65},{65,1},{2,66},{66,2},{3,67},{67,3},{4,68},{68... | collective-permute-start | bytes 1179656 | tf_op jit(solution)/shard_map/ppermute | solution.py:31
  124.6 2.0 %collective-permute-start.30 = (bf16[512,256]{1,0:T(8,128)(2,1)}, bf16[512,256]{1,0:T(8,128)(2,1)}, u32[]{:S(2)}, u32[]{:S(2)}) collective-permute-start(bf16[512,256]{1,0:T(8,128)(2,1)} %collective-permute-done.28.refs_2_), channel_id=1, source_target_pairs={{0,32},{32,0},{1,33},{33,1},{2,34},{34,2},{3,35},{35,3},{4,36},{36... | collective-permute-start | bytes 786440 | tf_op jit(solution)/shard_map/ppermute | solution.py:31
  135.0 2.0 %collective-permute-start.32 = (bf16[512,384]{1,0:T(8,128)(2,1)}, bf16[512,384]{1,0:T(8,128)(2,1)S(1)}, u32[]{:S(2)}, u32[]{:S(2)}) collective-permute-start(bf16[512,384]{1,0:T(8,128)(2,1)} %collective-permute-done.26.refs_0_), channel_id=1, source_target_pairs={{0,32},{32,0},{1,33},{33,1},{2,34},{34,2},{3,35},{35,3},{4,36},{36... | collective-permute-start | bytes 1179656 | tf_op jit(solution)/shard_map/ppermute | solution.py:31
  (10 other events, 106.4 us)

commit v6 on v5

--- a/solution.py
+++ b/solution.py
@@ -335,7 +335,7 @@
     mine, theirs = after((mine, theirs), keys_in)
     early_own = attend(query_own, keys_own)
     keys_in = ring(after(keys_in, keys_own), "y", early_own)
-    query_in = gather(after(query_in, query_own), "z")
+    query_in = gather(after(query_in, query_own), "z", early_own)
     mine, theirs = other(mine, "xl"), lax.ppermute(theirs, ("xl", "xh"), DIAGONAL)
 
     in_parts = attend(query_in, keys_in, attend(query_in, keys_own))

time: 141 us -> 149 us (1.057)
  waiting for transfers between devices: 30.3 us -> 42.3 us
  starting transfers between devices: 52 us -> 49.6 us
  local copies, waits for them, and re-layouts: 9.52 us -> 7.54 us
    ppermute x1, waiting for transfers between devices: 0.04 us -> 15.6 us  [per_device(): lax.ppermute(theirs, ('xl', 'xh'), DIAGONAL)]
    ppermute x20, waiting for transfers between devices: 26.9 us -> 19.3 us  [shift(): lax.ppermute(array, axis, [(i, (i + by) % NEAR) for i in range(NEAR)])]
    ppermute x11, starting transfers between devices: 22.9 us -> 15.5 us  [other(): return lax.ppermute(array, axis, [(0, 1), (1, 0)])]
    ppermute x11, waiting for transfers between devices: 3.33 us -> 7.4 us  [other(): return lax.ppermute(array, axis, [(0, 1), (1, 0)])]
    ppermute x20, starting transfers between devices: 27.3 us -> 29.7 us  [shift(): lax.ppermute(array, axis, [(i, (i + by) % NEAR) for i in range(NEAR)])]
    unnamed x18, local copies, waits for them, and re-layouts: 4.87 us -> 2.89 us
    ppermute x1, starting transfers between devices: 0.94 us -> 2.48 us  [per_device(): lax.ppermute(theirs, ('xl', 'xh'), DIAGONAL)]
  transfers between devices with their start and end apart: 33 -> 33, of which waited for: 14 -> 13; matrix products, arithmetic and copies ran while one was open for 3% -> 3% of each run, Pallas kernels for 29% -> 28%
where the time goes in v6:
time: 149 us
  starting transfers between devices  49.6 us (33%)
  Pallas kernels  48.2 us (32%)
  waiting for transfers between devices  42.3 us (28%)
  local copies, waits for them, and re-layouts  7.54 us (5%)
    pallas_call x4, Pallas kernels, attend(): pl.pallas_call(functools.partial(attend_kernel, slices, len(blocks), head...  32.2 us
    ppermute x20, starting transfers between devices, shift(): lax.ppermute(array, axis, [(i, (i + by) % NEAR) for i in range(NEAR)])  29.7 us
    ppermute x20, waiting for transfers between devices, shift(): lax.ppermute(array, axis, [(i, (i + by) % NEAR) for i in range(NEAR)])  19.3 us
    ppermute x1, waiting for transfers between devices, per_device(): lax.ppermute(theirs, ('xl', 'xh'), DIAGONAL)  15.6 us
    ppermute x11, starting transfers between devices, other(): return lax.ppermute(array, axis, [(0, 1), (1, 0)])  15.5 us
    pallas_call x2, Pallas kernels, project(): pl.pallas_call(functools.partial(project_kernel, terms, len(pieces), len(...  9.34 us
    ppermute x11, waiting for transfers between devices, other(): return lax.ppermute(array, axis, [(0, 1), (1, 0)])  7.4 us
    dynamic_slice x1, local copies, waits for them, and re-layouts, weight_slices(): lax.dynamic_slice_in_dim(out_weight, at * width, width, axis=1)  4.54 us
  transfers between devices with their start and end apart: 33, of which 13 were waited for; matrix products, arithmetic and copies ran while one was open for 3% of the time, Pallas kernels for 28%

profile of v6, /device:TPU:1, one launch (start us, length us, event | category | flops | bytes accessed | tf_op | source)
XLA Modules:
  0.0 148.6 jit_solution(2336515603362536676)
XLA Ops:
  0.6 3.2 %shard_map.86 = (bf16[3072,128]{1,0:T(8,128)(2,1)}, bf16[1024,128]{1,0:T(8,128)(2,1)}, bf16[3072,128]{1,0:T(8,128)(2,1)}, bf16[1536,128]{1,0:T(8,128)(2,1)}) custom-call(s32[1]{0:T(128)} %bitcast.at_ref, bf16[256,640]{1,0:T(8,128)(2,1)} %refs_0_.1, bf16[256,640]{1,0:T(8,128)(2,1)} %refs_1_.1, bf16[256,640]{1,0:T(8,128)(2,1)} %refs_2_.1, ...), custom_call_target="tpu_custom_call" | custom-call | flops 1 | bytes 1 | tf_op jit(solution)/shard_map/pallas_call | solution.py:312
  3.8 2.1 %collective-permute-start.6 = (bf16[3072,128]{1,0:T(8,128)(2,1)}, bf16[3072,128]{1,0:T(8,128)(2,1)S(1)}, u32[]{:S(2)}, u32[]{:S(2)}) collective-permute-start(bf16[3072,128]{1,0:T(8,128)(2,1)} %get-tuple-element.52.refs_4_.refs_8_), channel_id=1, source_target_pairs={{0,4},{4,8},{8,12},{12,0},{1,5},{5,9},{9,13},{13,1},{2,6},{6,10},{... | collective-permute-start | bytes 2359304 | tf_op jit(solution)/shard_map/ppermute | solution.py:27
  7.4 2.7 %collective-permute-start.2 = (bf16[1024,128]{1,0:T(8,128)(2,1)}, bf16[1024,128]{1,0:T(8,128)(2,1)S(1)}, u32[]{:S(2)}, u32[]{:S(2)}) collective-permute-start(bf16[1024,128]{1,0:T(8,128)(2,1)} %get-tuple-element.49), channel_id=1, source_target_pairs={{0,16},{16,0},{1,17},{17,1},{2,18},{18,2},{3,19},{19,3},{4,20},{20... | collective-permute-start | bytes 786440 | tf_op jit(solution)/shard_map/ppermute | solution.py:31
  10.2 1.6 %collective-permute-start = (bf16[1536,128]{1,0:T(8,128)(2,1)}, bf16[1536,128]{1,0:T(8,128)(2,1)S(1)}, u32[]{:S(2)}, u32[]{:S(2)}) collective-permute-start(bf16[1536,128]{1,0:T(8,128)(2,1)} %get-tuple-element.73.refs_0_), channel_id=1, source_target_pairs={{0,1},{1,2},{2,3},{3,0},{4,5},{5,6},{6,7},{7,4},{8,9},{9,10},{10,1... | collective-permute-start | bytes 1179656 | tf_op jit(solution)/shard_map/ppermute | solution.py:27
  11.8 2.1 %collective-permute-start.1 = (bf16[1536,128]{1,0:T(8,128)(2,1)}, bf16[1536,128]{1,0:T(8,128)(2,1)S(1)}, u32[]{:S(2)}, u32[]{:S(2)}) collective-permute-start(bf16[1536,128]{1,0:T(8,128)(2,1)} %get-tuple-element.73.refs_0_), channel_id=1, source_target_pairs={{0,3},{1,0},{2,1},{3,2},{4,7},{5,4},{6,5},{7,6},{8,11},{9,8},{10,9... | collective-permute-start | bytes 1179656 | tf_op jit(solution)/shard_map/ppermute | solution.py:27
  13.9 1.9 %collective-permute-done.2.refs_0_ = bf16[1024,128]{1,0:T(8,128)(2,1)S(1)} collective-permute-done((bf16[1024,128]{1,0:T(8,128)(2,1)}, bf16[1024,128]{1,0:T(8,128)(2,1)S(1)}, u32[]{:S(2)}, u32[]{:S(2)}) %collective-permute-start.2) | collective-permute-done | bytes 262176 | tf_op jit(solution)/shard_map/ppermute | solution.py:31
  15.8 2.7 %collective-permute-start.11 = (bf16[3072,128]{1,0:T(8,128)(2,1)}, bf16[3072,128]{1,0:T(8,128)(2,1)S(1)}, u32[]{:S(2)}, u32[]{:S(2)}) collective-permute-start(bf16[3072,128]{1,0:T(8,128)(2,1)} %get-tuple-element.61), channel_id=1, source_target_pairs={{0,16},{16,0},{1,17},{17,1},{2,18},{18,2},{3,19},{19,3},{4,20},{20... | collective-permute-start | bytes 2359304 | tf_op jit(solution)/shard_map/ppermute | solution.py:31
  18.5 4.5 %constant_dynamic-slice_fusion = (bf16[640,1280]{1,0:T(8,128)(2,1)S(1)}, bf16[640,1280]{1,0:T(8,128)(2,1)S(1)}, bf16[640,1280]{1,0:T(8,128)(2,1)}, bf16[640,1280]{1,0:T(8,128)(2,1)S(1)}) fusion(bf16[640,5120]{1,0:T(8,128)(2,1)} %param.13, s32[]{:T(128)S(6)} %select_n.15, s32[]{:T(128)S(6)} %select_n.13, s32[]{:T(128)S(6)} %select_n.12, s32[]{:T(128)S(6)} %select_n.14), kind=kLoop, calls=%fused_computation | loop fusion | bytes 13107216 | tf_op jit(solution)/shard_map/dynamic_slice | solution.py:287
  23.1 3.7 %collective-permute-start.3 = (bf16[1536,128]{1,0:T(8,128)(2,1)S(1)}, bf16[1536,128]{1,0:T(8,128)(2,1)S(1)}, u32[]{:S(2)}, u32[]{:S(2)}) collective-permute-start(bf16[1536,128]{1,0:T(8,128)(2,1)S(1)} %copy-done.4), channel_id=1, source_target_pairs={{0,2},{1,3},{2,0},{3,1},{4,6},{5,7},{6,4},{7,5},{8,10},{9,11},{10,... | collective-permute-start | bytes 1179656 | tf_op jit(solution)/shard_map/ppermute | solution.py:27
  26.9 2.7 %collective-permute-start.9 = (bf16[1536,128]{1,0:T(8,128)(2,1)S(1)}, bf16[1536,128]{1,0:T(8,128)(2,1)S(1)}, u32[]{:S(2)}, u32[]{:S(2)}) collective-permute-start(bf16[1536,128]{1,0:T(8,128)(2,1)S(1)} %slice.17), channel_id=1, source_target_pairs={{0,12},{4,0},{8,4},{12,8},{1,13},{5,1},{9,5},{13,9},{2,14},{6,2},{... | collective-permute-start | bytes 1179656 | tf_op jit(solution)/shard_map/ppermute | solution.py:27
  29.6 4.2 %collective-permute-done.3.refs_3_ = bf16[1536,128]{1,0:T(8,128)(2,1)S(1)} collective-permute-done((bf16[1536,128]{1,0:T(8,128)(2,1)S(1)}, bf16[1536,128]{1,0:T(8,128)(2,1)S(1)}, u32[]{:S(2)}, u32[]{:S(2)}) %collective-permute-start.3) | collective-permute-done | bytes 393248 | tf_op jit(solution)/shard_map/ppermute | solution.py:27
  34.5 2.1 %collective-permute-start.5 = (bf16[1024,128]{1,0:T(8,128)(2,1)S(1)}, bf16[1024,128]{1,0:T(8,128)(2,1)S(1)}, u32[]{:S(2)}, u32[]{:S(2)}) collective-permute-start(bf16[1024,128]{1,0:T(8,128)(2,1)S(1)} %collective-permute-done.2.refs_0_), channel_id=1, source_target_pairs={{0,3},{1,0},{2,1},{3,2},{4,7},{5,4},{6,5},{7,6},{8,11},{9,8},{10,9... | collective-permute-start | bytes 786440 | tf_op jit(solution)/shard_map/ppermute | solution.py:27
  36.8 2.7 %collective-permute-start.13 = (bf16[3072,128]{1,0:T(8,128)(2,1)S(1)}, bf16[3072,128]{1,0:T(8,128)(2,1)S(1)}, u32[]{:S(2)}, u32[]{:S(2)}) collective-permute-start(bf16[3072,128]{1,0:T(8,128)(2,1)S(1)} %collective-permute-done.11.refs_4_.refs_8_), channel_id=1, source_target_pairs={{0,12},{4,0},{8,4},{12,8},{1,13},{5,1},{9,5},{13,9},{2,14},{6,2},{... | collective-permute-start | bytes 2359304 | tf_op jit(solution)/shard_map/ppermute | solution.py:27
  39.4 8.9 %shard_map.87 = (bf16[1600,128]{1,0:T(8,128)(2,1)S(1)}, bf16[1600,128]{1,0:T(8,128)(2,1)S(1)}, bf16[1600,128]{1,0:T(8,128)(2,1)S(1)}, bf16[1600,128]{1,0:T(8,128)(2,1)S(1)}) custom-call(bf16[1536,128]{1,0:T(8,128)(2,1)S(1)} %copy-done.4, bf16[1536,128]{1,0:T(8,128)(2,1)S(1)} %collective-permute-done.refs_1_, ...), custom_call_target="tpu_custom_call" | custom-call | flops 12884901888 | bytes 7864320 | tf_op jit(solution)/shard_map/pallas_call | solution.py:160
  48.4 2.1 %collective-permute-start.10 = (bf16[1024,128]{1,0:T(8,128)(2,1)S(1)}, bf16[1024,128]{1,0:T(8,128)(2,1)S(1)}, u32[]{:S(2)}, u32[]{:S(2)}) collective-permute-start(bf16[1024,128]{1,0:T(8,128)(2,1)S(1)} %collective-permute-done.2.refs_0_), channel_id=1, source_target_pairs={{0,2},{1,3},{2,0},{3,1},{4,6},{5,7},{6,4},{7,5},{8,10},{9,11},{10,... | collective-permute-start | bytes 786440 | tf_op jit(solution)/shard_map/ppermute | solution.py:27
  50.5 2.5 %collective-permute-start.19 = (bf16[640,1280]{1,0:T(8,128)(2,1)S(1)}, bf16[640,1280]{1,0:T(8,128)(2,1)S(1)}, u32[]{:S(2)}, u32[]{:S(2)}) collective-permute-start(bf16[640,1280]{1,0:T(8,128)(2,1)S(1)} %get-tuple-element.81), channel_id=1, source_target_pairs={{0,80},{16,64},{64,16},{80,0},{1,81},{17,65},{65,17},{81,1},{2,82}... | collective-permute-start | bytes 4915208 | tf_op jit(solution)/shard_map/ppermute | solution.py:339
  53.6 2.7 %collective-permute-start.15 = (bf16[1536,128]{1,0:T(8,128)(2,1)S(1)}, bf16[1536,128]{1,0:T(8,128)(2,1)S(1)}, u32[]{:S(2)}, u32[]{:S(2)}) collective-permute-start(bf16[1536,128]{1,0:T(8,128)(2,1)S(1)} %slice.19), channel_id=1, source_target_pairs={{0,12},{4,0},{8,4},{12,8},{1,13},{5,1},{9,5},{13,9},{2,14},{6,2},{... | collective-permute-start | bytes 1179656 | tf_op jit(solution)/shard_map/ppermute | solution.py:27
  56.2 6.0 %shard_map.88 = (bf16[1088,128]{1,0:T(8,128)(2,1)S(1)}, bf16[1088,128]{1,0:T(8,128)(2,1)S(1)}, bf16[1088,128]{1,0:T(8,128)(2,1)S(1)}, bf16[1088,128]{1,0:T(8,128)(2,1)S(1)}) custom-call(bf16[1024,128]{1,0:T(8,128)(2,1)S(1)} %collective-permute-done.2.refs_0_, bf16[1024,128]{1,0:T(8,128)(2,1)S(1)} %collective-permute-done.4.refs_1_, ...), custom_call_target="tpu_custom_call" | custom-call | flops 8589934592 | bytes 5242880 | tf_op jit(solution)/shard_map/pallas_call | solution.py:160
  62.2 7.0 %shard_map.89 = (bf16[1088,128]{1,0:T(8,128)(2,1)S(1)}, bf16[1088,128]{1,0:T(8,128)(2,1)S(1)}, bf16[1088,128]{1,0:T(8,128)(2,1)S(1)}, bf16[1088,128]{1,0:T(8,128)(2,1)S(1)}) custom-call(bf16[1024,128]{1,0:T(8,128)(2,1)S(1)} %collective-permute-done.2.refs_0_, bf16[1024,128]{1,0:T(8,128)(2,1)S(1)} %collective-permute-done.4.refs_1_, ...), custom_call_target="tpu_custom_call" | custom-call | flops 8589934592 | bytes 5242880 | tf_op jit(solution)/shard_map/pallas_call | solution.py:160
  69.2 15.6 %collective-permute-done.19 = bf16[640,1280]{1,0:T(8,128)(2,1)S(1)} collective-permute-done((bf16[640,1280]{1,0:T(8,128)(2,1)S(1)}, bf16[640,1280]{1,0:T(8,128)(2,1)S(1)}, u32[]{:S(2)}, u32[]{:S(2)}) %collective-permute-start.19) | collective-permute-done | bytes 1638432 | tf_op jit(solution)/shard_map/ppermute | solution.py:339
  84.8 1.9 %collective-permute-done.20.refs_7_.refs_2_ = bf16[640,1280]{1,0:T(8,128)(2,1)S(1)} collective-permute-done((bf16[640,1280]{1,0:T(8,128)(2,1)S(1)}, bf16[640,1280]{1,0:T(8,128)(2,1)S(1)}, u32[]{:S(2)}, u32[]{:S(2)}) %collective-permute-start.20) | collective-permute-done | bytes 1638432 | tf_op jit(solution)/shard_map/ppermute | solution.py:31
  86.7 4.4 %collective-permute-start.21 = (bf16[640,1280]{1,0:T(8,128)(2,1)S(1)}, bf16[640,1280]{1,0:T(8,128)(2,1)S(1)}, u32[]{:S(2)}, u32[]{:S(2)}) collective-permute-start(bf16[640,1280]{1,0:T(8,128)(2,1)S(1)} %get-tuple-element.83), channel_id=1, source_target_pairs={{0,32},{32,0},{1,33},{33,1},{2,34},{34,2},{3,35},{35,3},{4,36},{36... | collective-permute-start | bytes 4915208 | tf_op jit(solution)/shard_map/ppermute | solution.py:31
  93.7 10.4 %shard_map.90 = (bf16[1600,128]{1,0:T(8,128)(2,1)S(1)}, bf16[1600,128]{1,0:T(8,128)(2,1)S(1)}, bf16[1600,128]{1,0:T(8,128)(2,1)S(1)}, bf16[1600,128]{1,0:T(8,128)(2,1)S(1)}) custom-call(bf16[1536,128]{1,0:T(8,128)(2,1)S(1)} %copy-done.4, bf16[1536,128]{1,0:T(8,128)(2,1)S(1)} %copy-done.6, bf16[1536,128]{1,0:T(8,128)(2,1)S(1)} %copy-done.8, ...), custom_call_target="tpu_custom_call" | custom-call | flops 12884901888 | bytes 7864320 | tf_op jit(solution)/shard_map/pallas_call | solution.py:160
  104.1 1.8 %collective-permute-done.18.refs_3_ = bf16[1088,128]{1,0:T(8,128)(2,1)S(1)} collective-permute-done((bf16[1088,128]{1,0:T(8,128)(2,1)S(1)}, bf16[1088,128]{1,0:T(8,128)(2,1)S(1)}, u32[]{:S(2)}, u32[]{:S(2)}) %collective-permute-start.18) | collective-permute-done | bytes 278560 | tf_op jit(solution)/shard_map/ppermute | solution.py:27
  110.8 1.9 %collective-permute-start.28 = (bf16[512,256]{1,0:T(8,128)(2,1)S(1)}, bf16[512,256]{1,0:T(8,128)(2,1)}, u32[]{:S(2)}, u32[]{:S(2)}) collective-permute-start(bf16[512,256]{1,0:T(8,128)(2,1)S(1)} %shard_map.92), channel_id=1, source_target_pairs={{0,80},{16,64},{64,16},{80,0},{1,81},{17,65},{65,17},{81,1},{2,82}... | collective-permute-start | bytes 786440 | tf_op jit(solution)/shard_map/ppermute | solution.py:350
  112.7 2.6 %collective-permute-done.23.refs_1_ = bf16[1600,128]{1,0:T(8,128)(2,1)S(1)} collective-permute-done((bf16[1600,128]{1,0:T(8,128)(2,1)S(1)}, bf16[1600,128]{1,0:T(8,128)(2,1)S(1)}, u32[]{:S(2)}, u32[]{:S(2)}) %collective-permute-start.23) | collective-permute-done | bytes 409632 | tf_op jit(solution)/shard_map/ppermute | solution.py:27
  115.3 3.8 %collective-permute-done.24.refs_2_ = bf16[1600,128]{1,0:T(8,128)(2,1)S(1)} collective-permute-done((bf16[1600,128]{1,0:T(8,128)(2,1)S(1)}, bf16[1600,128]{1,0:T(8,128)(2,1)S(1)}, u32[]{:S(2)}, u32[]{:S(2)}) %collective-permute-start.24) | collective-permute-done | bytes 409632 | tf_op jit(solution)/shard_map/ppermute | solution.py:27
  119.1 6.3 %collective-permute-done.25.refs_3_ = bf16[1600,128]{1,0:T(8,128)(2,1)S(1)} collective-permute-done((bf16[1600,128]{1,0:T(8,128)(2,1)S(1)}, bf16[1600,128]{1,0:T(8,128)(2,1)S(1)}, u32[]{:S(2)}, u32[]{:S(2)}) %collective-permute-start.25) | collective-permute-done | bytes 409632 | tf_op jit(solution)/shard_map/ppermute | solution.py:27
  125.4 2.2 %shard_map.91.refs_0_ = bf16[512,384]{1,0:T(8,128)(2,1)} custom-call(bf16[1600,128]{1,0:T(8,128)(2,1)S(1)} %get-tuple-element.85.refs_0_, bf16[1600,128]{1,0:T(8,128)(2,1)S(1)} %collective-permute-done.23.refs_1_, bf16[1600,128]{1,0:T(8,128)(2,1)S(1)} %collective-permute-done.24.refs_2_, bf16[1600,128]{1,0:T(8,128)(2,1)S(1)} %collective-permute-done.25.refs_3_), custom_call_target="tpu_custom_call" | custom-call | flops 1 | bytes 1 | tf_op jit(solution)/shard_map/pallas_call | solution.py:203
  127.6 3.8 %collective-permute-start.31 = (bf16[512,384]{1,0:T(8,128)(2,1)}, bf16[512,384]{1,0:T(8,128)(2,1)}, u32[]{:S(2)}, u32[]{:S(2)}) collective-permute-start(bf16[512,384]{1,0:T(8,128)(2,1)} %shard_map.91.refs_0_), channel_id=1, source_target_pairs={{0,32},{32,0},{1,33},{33,1},{2,34},{34,2},{3,35},{35,3},{4,36},{36... | collective-permute-start | bytes 1179656 | tf_op jit(solution)/shard_map/ppermute | solution.py:31
  136.7 5.6 %shard_map.93.refs_4_ = f32[512,1280]{1,0:T(8,128)S(1)} custom-call(s32[2]{0:T(128)S(1)} %pad_add_fusion.at_ref, bf16[512,384]{1,0:T(8,128)(2,1)} %shard_map.91.refs_0_, bf16[512,256]{1,0:T(8,128)(2,1)S(1)} %collective-permute-done.27.refs_1_, bf16[512,256]{1,0:T(8,128)(2,1)} %collective-permute-done.28.refs_2_, ...), custom_call_target="tpu_custom_call" | custom-call | flops 1 | bytes 1 | tf_op jit(solution)/shard_map/pallas_call | solution.py:267
  144.8 3.7 %shard_map.94 = (bf16[256,1280]{1,0:T(8,128)(2,1)}, bf16[256,1280]{1,0:T(8,128)(2,1)}) custom-call(s32[2]{0:T(128)S(1)} %pad_add_fusion.at_ref, bf16[512,384]{1,0:T(8,128)(2,1)} %collective-permute-done.26.refs_0_, bf16[512,384]{1,0:T(8,128)(2,1)S(1)} %collective-permute-done.32.refs_1_, bf16[640,1280]{1,0:T(8,128)(2,1)S(1)} %collective-permute-done.20.refs_7_.refs_2_, ...), custom_call_target="tpu_custom_call" | custom-call | flops 1 | bytes 1 | tf_op jit(solution)/shard_map/pallas_call | solution.py:267
  (67 shorter events, 18.2 us)
Async XLA Ops:
  3.8 22.9 %collective-permute-start.6 = (bf16[3072,128]{1,0:T(8,128)(2,1)}, bf16[3072,128]{1,0:T(8,128)(2,1)S(1)}, u32[]{:S(2)}, u32[]{:S(2)}) collective-permute-start(bf16[3072,128]{1,0:T(8,128)(2,1)} %get-tuple-element.52.refs_4_.refs_8_), channel_id=1, source_target_pairs={{0,4},{4,8},{8,12},{12,0},{1,5},{5,9},{9,13},{13,1},{2,6},{6,10},{... | collective-permute-start | bytes 2359304 | tf_op jit(solution)/shard_map/ppermute | solution.py:27
  6.0 20.8 %collective-permute-start.7 = (bf16[3072,128]{1,0:T(8,128)(2,1)}, bf16[3072,128]{1,0:T(8,128)(2,1)S(1)}, u32[]{:S(2)}, u32[]{:S(2)}) collective-permute-start(bf16[3072,128]{1,0:T(8,128)(2,1)} %get-tuple-element.52.refs_4_.refs_8_), channel_id=1, source_target_pairs={{0,12},{4,0},{8,4},{12,8},{1,13},{5,1},{9,5},{13,9},{2,14},{6,2},{... | collective-permute-start | bytes 2359304 | tf_op jit(solution)/shard_map/ppermute | solution.py:27
  7.4 8.4 %collective-permute-start.2 = (bf16[1024,128]{1,0:T(8,128)(2,1)}, bf16[1024,128]{1,0:T(8,128)(2,1)S(1)}, u32[]{:S(2)}, u32[]{:S(2)}) collective-permute-start(bf16[1024,128]{1,0:T(8,128)(2,1)} %get-tuple-element.49), channel_id=1, source_target_pairs={{0,16},{16,0},{1,17},{17,1},{2,18},{18,2},{3,19},{19,3},{4,20},{20... | collective-permute-start | bytes 786440 | tf_op jit(solution)/shard_map/ppermute | solution.py:31
  10.2 12.9 %collective-permute-start = (bf16[1536,128]{1,0:T(8,128)(2,1)}, bf16[1536,128]{1,0:T(8,128)(2,1)S(1)}, u32[]{:S(2)}, u32[]{:S(2)}) collective-permute-start(bf16[1536,128]{1,0:T(8,128)(2,1)} %get-tuple-element.73.refs_0_), channel_id=1, source_target_pairs={{0,1},{1,2},{2,3},{3,0},{4,5},{5,6},{6,7},{7,4},{8,9},{9,10},{10,1... | collective-permute-start | bytes 1179656 | tf_op jit(solution)/shard_map/ppermute | solution.py:27
  11.8 11.3 %collective-permute-start.1 = (bf16[1536,128]{1,0:T(8,128)(2,1)}, bf16[1536,128]{1,0:T(8,128)(2,1)S(1)}, u32[]{:S(2)}, u32[]{:S(2)}) collective-permute-start(bf16[1536,128]{1,0:T(8,128)(2,1)} %get-tuple-element.73.refs_0_), channel_id=1, source_target_pairs={{0,3},{1,0},{2,1},{3,2},{4,7},{5,4},{6,5},{7,6},{8,11},{9,8},{10,9... | collective-permute-start | bytes 1179656 | tf_op jit(solution)/shard_map/ppermute | solution.py:27
  15.8 20.8 %collective-permute-start.11 = (bf16[3072,128]{1,0:T(8,128)(2,1)}, bf16[3072,128]{1,0:T(8,128)(2,1)S(1)}, u32[]{:S(2)}, u32[]{:S(2)}) collective-permute-start(bf16[3072,128]{1,0:T(8,128)(2,1)} %get-tuple-element.61), channel_id=1, source_target_pairs={{0,16},{16,0},{1,17},{17,1},{2,18},{18,2},{3,19},{19,3},{4,20},{20... | collective-permute-start | bytes 2359304 | tf_op jit(solution)/shard_map/ppermute | solution.py:31
  23.1 10.7 %collective-permute-start.3 = (bf16[1536,128]{1,0:T(8,128)(2,1)S(1)}, bf16[1536,128]{1,0:T(8,128)(2,1)S(1)}, u32[]{:S(2)}, u32[]{:S(2)}) collective-permute-start(bf16[1536,128]{1,0:T(8,128)(2,1)S(1)} %copy-done.4), channel_id=1, source_target_pairs={{0,2},{1,3},{2,0},{3,1},{4,6},{5,7},{6,4},{7,5},{8,10},{9,11},{10,... | collective-permute-start | bytes 1179656 | tf_op jit(solution)/shard_map/ppermute | solution.py:27
  26.8 9.8 %collective-permute-start.8 = (bf16[1536,128]{1,0:T(8,128)(2,1)S(1)}, bf16[1536,128]{1,0:T(8,128)(2,1)S(1)}, u32[]{:S(2)}, u32[]{:S(2)}) collective-permute-start(bf16[1536,128]{1,0:T(8,128)(2,1)S(1)} %slice.16), channel_id=1, source_target_pairs={{0,4},{4,8},{8,12},{12,0},{1,5},{5,9},{9,13},{13,1},{2,6},{6,10},{... | collective-permute-start | bytes 1179656 | tf_op jit(solution)/shard_map/ppermute | solution.py:27
  26.9 9.7 %collective-permute-start.9 = (bf16[1536,128]{1,0:T(8,128)(2,1)S(1)}, bf16[1536,128]{1,0:T(8,128)(2,1)S(1)}, u32[]{:S(2)}, u32[]{:S(2)}) collective-permute-start(bf16[1536,128]{1,0:T(8,128)(2,1)S(1)} %slice.17), channel_id=1, source_target_pairs={{0,12},{4,0},{8,4},{12,8},{1,13},{5,1},{9,5},{13,9},{2,14},{6,2},{... | collective-permute-start | bytes 1179656 | tf_op jit(solution)/shard_map/ppermute | solution.py:27
  33.8 14.6 %collective-permute-start.4 = (bf16[1024,128]{1,0:T(8,128)(2,1)S(1)}, bf16[1024,128]{1,0:T(8,128)(2,1)S(1)}, u32[]{:S(2)}, u32[]{:S(2)}) collective-permute-start(bf16[1024,128]{1,0:T(8,128)(2,1)S(1)} %collective-permute-done.2.refs_0_), channel_id=1, source_target_pairs={{0,1},{1,2},{2,3},{3,0},{4,5},{5,6},{6,7},{7,4},{8,9},{9,10},{10,1... | collective-permute-start | bytes 786440 | tf_op jit(solution)/shard_map/ppermute | solution.py:27
  34.5 13.8 %collective-permute-start.5 = (bf16[1024,128]{1,0:T(8,128)(2,1)S(1)}, bf16[1024,128]{1,0:T(8,128)(2,1)S(1)}, u32[]{:S(2)}, u32[]{:S(2)}) collective-permute-start(bf16[1024,128]{1,0:T(8,128)(2,1)S(1)} %collective-permute-done.2.refs_0_), channel_id=1, source_target_pairs={{0,3},{1,0},{2,1},{3,2},{4,7},{5,4},{6,5},{7,6},{8,11},{9,8},{10,9... | collective-permute-start | bytes 786440 | tf_op jit(solution)/shard_map/ppermute | solution.py:27
  36.7 16.7 %collective-permute-start.12 = (bf16[3072,128]{1,0:T(8,128)(2,1)S(1)}, bf16[3072,128]{1,0:T(8,128)(2,1)S(1)}, u32[]{:S(2)}, u32[]{:S(2)}) collective-permute-start(bf16[3072,128]{1,0:T(8,128)(2,1)S(1)} %collective-permute-done.11.refs_4_.refs_8_), channel_id=1, source_target_pairs={{0,4},{4,8},{8,12},{12,0},{1,5},{5,9},{9,13},{13,1},{2,6},{6,10},{... | collective-permute-start | bytes 2359304 | tf_op jit(solution)/shard_map/ppermute | solution.py:27
  36.8 16.7 %collective-permute-start.13 = (bf16[3072,128]{1,0:T(8,128)(2,1)S(1)}, bf16[3072,128]{1,0:T(8,128)(2,1)S(1)}, u32[]{:S(2)}, u32[]{:S(2)}) collective-permute-start(bf16[3072,128]{1,0:T(8,128)(2,1)S(1)} %collective-permute-done.11.refs_4_.refs_8_), channel_id=1, source_target_pairs={{0,12},{4,0},{8,4},{12,8},{1,13},{5,1},{9,5},{13,9},{2,14},{6,2},{... | collective-permute-start | bytes 2359304 | tf_op jit(solution)/shard_map/ppermute | solution.py:27
  48.4 7.8 %collective-permute-start.10 = (bf16[1024,128]{1,0:T(8,128)(2,1)S(1)}, bf16[1024,128]{1,0:T(8,128)(2,1)S(1)}, u32[]{:S(2)}, u32[]{:S(2)}) collective-permute-start(bf16[1024,128]{1,0:T(8,128)(2,1)S(1)} %collective-permute-done.2.refs_0_), channel_id=1, source_target_pairs={{0,2},{1,3},{2,0},{3,1},{4,6},{5,7},{6,4},{7,5},{8,10},{9,11},{10,... | collective-permute-start | bytes 786440 | tf_op jit(solution)/shard_map/ppermute | solution.py:27
  50.5 34.3 %collective-permute-start.19 = (bf16[640,1280]{1,0:T(8,128)(2,1)S(1)}, bf16[640,1280]{1,0:T(8,128)(2,1)S(1)}, u32[]{:S(2)}, u32[]{:S(2)}) collective-permute-start(bf16[640,1280]{1,0:T(8,128)(2,1)S(1)} %get-tuple-element.81), channel_id=1, source_target_pairs={{0,80},{16,64},{64,16},{80,0},{1,81},{17,65},{65,17},{81,1},{2,82}... | collective-permute-start | bytes 4915208 | tf_op jit(solution)/shard_map/ppermute | solution.py:339
  52.9 33.8 %collective-permute-start.20 = (bf16[640,1280]{1,0:T(8,128)(2,1)S(1)}, bf16[640,1280]{1,0:T(8,128)(2,1)S(1)}, u32[]{:S(2)}, u32[]{:S(2)}) collective-permute-start(bf16[640,1280]{1,0:T(8,128)(2,1)S(1)} %get-tuple-element.82), channel_id=1, source_target_pairs={{0,64},{64,0},{1,65},{65,1},{2,66},{66,2},{3,67},{67,3},{4,68},{68... | collective-permute-start | bytes 4915208 | tf_op jit(solution)/shard_map/ppermute | solution.py:31
  53.5 8.7 %collective-permute-start.14 = (bf16[1536,128]{1,0:T(8,128)(2,1)S(1)}, bf16[1536,128]{1,0:T(8,128)(2,1)S(1)}, u32[]{:S(2)}, u32[]{:S(2)}) collective-permute-start(bf16[1536,128]{1,0:T(8,128)(2,1)S(1)} %slice.18), channel_id=1, source_target_pairs={{0,4},{4,8},{8,12},{12,0},{1,5},{5,9},{9,13},{13,1},{2,6},{6,10},{... | collective-permute-start | bytes 1179656 | tf_op jit(solution)/shard_map/ppermute | solution.py:27
  53.6 8.6 %collective-permute-start.15 = (bf16[1536,128]{1,0:T(8,128)(2,1)S(1)}, bf16[1536,128]{1,0:T(8,128)(2,1)S(1)}, u32[]{:S(2)}, u32[]{:S(2)}) collective-permute-start(bf16[1536,128]{1,0:T(8,128)(2,1)S(1)} %slice.19), channel_id=1, source_target_pairs={{0,12},{4,0},{8,4},{12,8},{1,13},{5,1},{9,5},{13,9},{2,14},{6,2},{... | collective-permute-start | bytes 1179656 | tf_op jit(solution)/shard_map/ppermute | solution.py:27
  86.7 19.2 %collective-permute-start.21 = (bf16[640,1280]{1,0:T(8,128)(2,1)S(1)}, bf16[640,1280]{1,0:T(8,128)(2,1)S(1)}, u32[]{:S(2)}, u32[]{:S(2)}) collective-permute-start(bf16[640,1280]{1,0:T(8,128)(2,1)S(1)} %get-tuple-element.83), channel_id=1, source_target_pairs={{0,32},{32,0},{1,33},{33,1},{2,34},{34,2},{3,35},{35,3},{4,36},{36... | collective-permute-start | bytes 4915208 | tf_op jit(solution)/shard_map/ppermute | solution.py:31
  91.2 14.8 %collective-permute-start.22 = (bf16[640,1280]{1,0:T(8,128)(2,1)S(1)}, bf16[640,1280]{1,0:T(8,128)(2,1)S(1)}, u32[]{:S(2)}, u32[]{:S(2)}) collective-permute-start(bf16[640,1280]{1,0:T(8,128)(2,1)S(1)} %collective-permute-done.19), channel_id=1, source_target_pairs={{0,32},{32,0},{1,33},{33,1},{2,34},{34,2},{3,35},{35,3},{4,36},{36... | collective-permute-start | bytes 4915208 | tf_op jit(solution)/shard_map/ppermute | solution.py:31
  91.2 12.9 %collective-permute-start.16 = (bf16[1088,128]{1,0:T(8,128)(2,1)S(1)}, bf16[1088,128]{1,0:T(8,128)(2,1)S(1)}, u32[]{:S(2)}, u32[]{:S(2)}) collective-permute-start(bf16[1088,128]{1,0:T(8,128)(2,1)S(1)} %get-tuple-element.70), channel_id=1, source_target_pairs={{0,3},{1,0},{2,1},{3,2},{4,7},{5,4},{6,5},{7,6},{8,11},{9,8},{10,9... | collective-permute-start | bytes 835592 | tf_op jit(solution)/shard_map/ppermute | solution.py:27
  91.4 12.7 %collective-permute-start.17 = (bf16[1088,128]{1,0:T(8,128)(2,1)S(1)}, bf16[1088,128]{1,0:T(8,128)(2,1)S(1)}, u32[]{:S(2)}, u32[]{:S(2)}) collective-permute-start(bf16[1088,128]{1,0:T(8,128)(2,1)S(1)} %get-tuple-element.71), channel_id=1, source_target_pairs={{0,1},{1,2},{2,3},{3,0},{4,5},{5,6},{6,7},{7,4},{8,9},{9,10},{10,1... | collective-permute-start | bytes 835592 | tf_op jit(solution)/shard_map/ppermute | solution.py:27
  92.6 13.3 %collective-permute-start.18 = (bf16[1088,128]{1,0:T(8,128)(2,1)S(1)}, bf16[1088,128]{1,0:T(8,128)(2,1)S(1)}, u32[]{:S(2)}, u32[]{:S(2)}) collective-permute-start(bf16[1088,128]{1,0:T(8,128)(2,1)S(1)} %get-tuple-element.72), channel_id=1, source_target_pairs={{0,2},{1,3},{2,0},{3,1},{4,6},{5,7},{6,4},{7,5},{8,10},{9,11},{10,... | collective-permute-start | bytes 835592 | tf_op jit(solution)/shard_map/ppermute | solution.py:27
  106.0 9.3 %collective-permute-start.23 = (bf16[1600,128]{1,0:T(8,128)(2,1)S(1)}, bf16[1600,128]{1,0:T(8,128)(2,1)S(1)}, u32[]{:S(2)}, u32[]{:S(2)}) collective-permute-start(bf16[1600,128]{1,0:T(8,128)(2,1)S(1)} %get-tuple-element.86), channel_id=1, source_target_pairs={{0,3},{1,0},{2,1},{3,2},{4,7},{5,4},{6,5},{7,6},{8,11},{9,8},{10,9... | collective-permute-start | bytes 1228808 | tf_op jit(solution)/shard_map/ppermute | solution.py:27
  107.3 11.8 %collective-permute-start.24 = (bf16[1600,128]{1,0:T(8,128)(2,1)S(1)}, bf16[1600,128]{1,0:T(8,128)(2,1)S(1)}, u32[]{:S(2)}, u32[]{:S(2)}) collective-permute-start(bf16[1600,128]{1,0:T(8,128)(2,1)S(1)} %get-tuple-element.87), channel_id=1, source_target_pairs={{0,1},{1,2},{2,3},{3,0},{4,5},{5,6},{6,7},{7,4},{8,9},{9,10},{10,1... | collective-permute-start | bytes 1228808 | tf_op jit(solution)/shard_map/ppermute | solution.py:27
  107.5 17.9 %collective-permute-start.25 = (bf16[1600,128]{1,0:T(8,128)(2,1)S(1)}, bf16[1600,128]{1,0:T(8,128)(2,1)S(1)}, u32[]{:S(2)}, u32[]{:S(2)}) collective-permute-start(bf16[1600,128]{1,0:T(8,128)(2,1)S(1)} %get-tuple-element.88), channel_id=1, source_target_pairs={{0,2},{1,3},{2,0},{3,1},{4,6},{5,7},{6,4},{7,5},{8,10},{9,11},{10,... | collective-permute-start | bytes 1228808 | tf_op jit(solution)/shard_map/ppermute | solution.py:27
  110.2 21.2 %collective-permute-start.27 = (bf16[512,256]{1,0:T(8,128)(2,1)S(1)}, bf16[512,256]{1,0:T(8,128)(2,1)S(1)}, u32[]{:S(2)}, u32[]{:S(2)}) collective-permute-start(bf16[512,256]{1,0:T(8,128)(2,1)S(1)} %shard_map.92), channel_id=1, source_target_pairs={{0,16},{16,0},{1,17},{17,1},{2,18},{18,2},{3,19},{19,3},{4,20},{20... | collective-permute-start | bytes 786440 | tf_op jit(solution)/shard_map/ppermute | solution.py:31
  110.8 20.9 %collective-permute-start.28 = (bf16[512,256]{1,0:T(8,128)(2,1)S(1)}, bf16[512,256]{1,0:T(8,128)(2,1)}, u32[]{:S(2)}, u32[]{:S(2)}) collective-permute-start(bf16[512,256]{1,0:T(8,128)(2,1)S(1)} %shard_map.92), channel_id=1, source_target_pairs={{0,80},{16,64},{64,16},{80,0},{1,81},{17,65},{65,17},{81,1},{2,82}... | collective-permute-start | bytes 786440 | tf_op jit(solution)/shard_map/ppermute | solution.py:350
  127.6 6.2 %collective-permute-start.31 = (bf16[512,384]{1,0:T(8,128)(2,1)}, bf16[512,384]{1,0:T(8,128)(2,1)}, u32[]{:S(2)}, u32[]{:S(2)}) collective-permute-start(bf16[512,384]{1,0:T(8,128)(2,1)} %shard_map.91.refs_0_), channel_id=1, source_target_pairs={{0,32},{32,0},{1,33},{33,1},{2,34},{34,2},{3,35},{35,3},{4,36},{36... | collective-permute-start | bytes 1179656 | tf_op jit(solution)/shard_map/ppermute | solution.py:31
  131.4 11.1 %collective-permute-start.26 = (bf16[512,384]{1,0:T(8,128)(2,1)}, bf16[512,384]{1,0:T(8,128)(2,1)}, u32[]{:S(2)}, u32[]{:S(2)}) collective-permute-start(bf16[512,384]{1,0:T(8,128)(2,1)} %shard_map.91.refs_0_), channel_id=1, source_target_pairs={{0,64},{64,0},{1,65},{65,1},{2,66},{66,2},{3,67},{67,3},{4,68},{68... | collective-permute-start | bytes 1179656 | tf_op jit(solution)/shard_map/ppermute | solution.py:31
  131.4 2.2 %collective-permute-start.29 = (bf16[512,256]{1,0:T(8,128)(2,1)S(1)}, bf16[512,256]{1,0:T(8,128)(2,1)}, u32[]{:S(2)}, u32[]{:S(2)}) collective-permute-start(bf16[512,256]{1,0:T(8,128)(2,1)S(1)} %collective-permute-done.27.refs_1_), channel_id=1, source_target_pairs={{0,32},{32,0},{1,33},{33,1},{2,34},{34,2},{3,35},{35,3},{4,36},{36... | collective-permute-start | bytes 786440 | tf_op jit(solution)/shard_map/ppermute | solution.py:31
  142.5 2.3 %collective-permute-start.32 = (bf16[512,384]{1,0:T(8,128)(2,1)}, bf16[512,384]{1,0:T(8,128)(2,1)S(1)}, u32[]{:S(2)}, u32[]{:S(2)}) collective-permute-start(bf16[512,384]{1,0:T(8,128)(2,1)} %collective-permute-done.26.refs_0_), channel_id=1, source_target_pairs={{0,32},{32,0},{1,33},{33,1},{2,34},{34,2},{3,35},{35,3},{4,36},{36... | collective-permute-start | bytes 1179656 | tf_op jit(solution)/shard_map/ppermute | solution.py:31
  (10 other events, 171.1 us)

commit v7 on v6

--- a/solution.py
+++ b/solution.py
@@ -335,7 +335,8 @@
     mine, theirs = after((mine, theirs), keys_in)
     early_own = attend(query_own, keys_own)
     keys_in = ring(after(keys_in, keys_own), "y", early_own)
-    query_in = gather(after(query_in, query_own), "z", early_own)
+    query_in = after(query_in, query_own)
+    query_in = [query_in] + [shift(query_in, "z", by) for by in (1, -1, 2)]
     mine, theirs = other(mine, "xl"), lax.ppermute(theirs, ("xl", "xh"), DIAGONAL)
 
     in_parts = attend(query_in, keys_in, attend(query_in, keys_own))

time: 149 us -> 158 us (1.060)
  local copies, waits for them, and re-layouts: 7.54 us -> 12.5 us
  Pallas kernels: 48.2 us -> 50.2 us
  starting transfers between devices: 49.6 us -> 51.3 us
    ppermute x1, waiting for transfers between devices: 15.6 us -> 1.35 us  [per_device(): lax.ppermute(theirs, ('xl', 'xh'), DIAGONAL)]
    ppermute x20, waiting for transfers between devices: 19.3 us -> 29.4 us  [shift(): lax.ppermute(array, axis, [(i, (i + by) % NEAR) for i in range(NEAR)])]
    ppermute x11, waiting for transfers between devices: 7.4 us -> 12.2 us  [other(): return lax.ppermute(array, axis, [(0, 1), (1, 0)])]
    unnamed x18 -> x26, local copies, waits for them, and re-layouts: 2.89 us -> 6.4 us
    ppermute x11, starting transfers between devices: 15.5 us -> 18.2 us  [other(): return lax.ppermute(array, axis, [(0, 1), (1, 0)])]
    pallas_call x4, Pallas kernels: 32.2 us -> 34.2 us  [attend(): pl.pallas_call(functools.partial(attend_kernel, slices, len(blocks), head...]
  transfers between devices with their start and end apart: 33 -> 33, of which waited for: 13 -> 15; matrix products, arithmetic and copies ran while one was open for 3% -> 4% of each run, Pallas kernels for 28% -> 27%
where the time goes in v7:
time: 158 us
  starting transfers between devices  51.3 us (32%)
  Pallas kernels  50.2 us (32%)
  waiting for transfers between devices  42.9 us (27%)
  local copies, waits for them, and re-layouts  12.5 us (8%)
    pallas_call x4, Pallas kernels, attend(): pl.pallas_call(functools.partial(attend_kernel, slices, len(blocks), head...  34.2 us
    ppermute x20, waiting for transfers between devices, shift(): lax.ppermute(array, axis, [(i, (i + by) % NEAR) for i in range(NEAR)])  29.4 us
    ppermute x20, starting transfers between devices, shift(): lax.ppermute(array, axis, [(i, (i + by) % NEAR) for i in range(NEAR)])  28.8 us
    ppermute x11, starting transfers between devices, other(): return lax.ppermute(array, axis, [(0, 1), (1, 0)])  18.2 us
    ppermute x11, waiting for transfers between devices, other(): return lax.ppermute(array, axis, [(0, 1), (1, 0)])  12.2 us
    pallas_call x2, Pallas kernels, project(): pl.pallas_call(functools.partial(project_kernel, terms, len(pieces), len(...  9.34 us
    unnamed x26, local copies, waits for them, and re-layouts  6.4 us
    dynamic_slice x1, local copies, waits for them, and re-layouts, weight_slices(): lax.dynamic_slice_in_dim(out_weight, at * width, width, axis=1)  4.54 us
  transfers between devices with their start and end apart: 33, of which 15 were waited for; matrix products, arithmetic and copies ran while one was open for 4% of the time, Pallas kernels for 27%

profile of v7, /device:TPU:1, one launch (start us, length us, event | category | flops | bytes accessed | tf_op | source)
XLA Modules:
  0.0 158.0 jit_solution(14124048869846674729)
XLA Ops:
  0.6 3.2 %shard_map.86 = (bf16[3072,128]{1,0:T(8,128)(2,1)}, bf16[1024,128]{1,0:T(8,128)(2,1)}, bf16[3072,128]{1,0:T(8,128)(2,1)}, bf16[1536,128]{1,0:T(8,128)(2,1)}) custom-call(s32[1]{0:T(128)} %bitcast.at_ref, bf16[256,640]{1,0:T(8,128)(2,1)} %refs_0_.1, bf16[256,640]{1,0:T(8,128)(2,1)} %refs_1_.1, bf16[256,640]{1,0:T(8,128)(2,1)} %refs_2_.1, ...), custom_call_target="tpu_custom_call" | custom-call | flops 1 | bytes 1 | tf_op jit(solution)/shard_map/pallas_call | solution.py:312
  3.8 2.1 %collective-permute-start.8 = (bf16[3072,128]{1,0:T(8,128)(2,1)}, bf16[3072,128]{1,0:T(8,128)(2,1)S(1)}, u32[]{:S(2)}, u32[]{:S(2)}) collective-permute-start(bf16[3072,128]{1,0:T(8,128)(2,1)} %get-tuple-element.53.refs_4_.refs_8_), channel_id=1, source_target_pairs={{0,4},{4,8},{8,12},{12,0},{1,5},{5,9},{9,13},{13,1},{2,6},{6,10},{... | collective-permute-start | bytes 2359304 | tf_op jit(solution)/shard_map/ppermute | solution.py:27
  7.4 2.7 %collective-permute-start.2 = (bf16[1024,128]{1,0:T(8,128)(2,1)}, bf16[1024,128]{1,0:T(8,128)(2,1)S(1)}, u32[]{:S(2)}, u32[]{:S(2)}) collective-permute-start(bf16[1024,128]{1,0:T(8,128)(2,1)} %get-tuple-element.48), channel_id=1, source_target_pairs={{0,16},{16,0},{1,17},{17,1},{2,18},{18,2},{3,19},{19,3},{4,20},{20... | collective-permute-start | bytes 786440 | tf_op jit(solution)/shard_map/ppermute | solution.py:31
  10.2 5.7 %collective-permute-done.2.refs_0_ = bf16[1024,128]{1,0:T(8,128)(2,1)S(1)} collective-permute-done((bf16[1024,128]{1,0:T(8,128)(2,1)}, bf16[1024,128]{1,0:T(8,128)(2,1)S(1)}, u32[]{:S(2)}, u32[]{:S(2)}) %collective-permute-start.2) | collective-permute-done | bytes 262176 | tf_op jit(solution)/shard_map/ppermute | solution.py:31
  15.8 2.7 %collective-permute-start.7 = (bf16[3072,128]{1,0:T(8,128)(2,1)}, bf16[3072,128]{1,0:T(8,128)(2,1)S(1)}, u32[]{:S(2)}, u32[]{:S(2)}) collective-permute-start(bf16[3072,128]{1,0:T(8,128)(2,1)} %get-tuple-element.52), channel_id=1, source_target_pairs={{0,16},{16,0},{1,17},{17,1},{2,18},{18,2},{3,19},{19,3},{4,20},{20... | collective-permute-start | bytes 2359304 | tf_op jit(solution)/shard_map/ppermute | solution.py:31
  18.5 6.2 %collective-permute-done.8.refs_5_.refs_9_ = bf16[3072,128]{1,0:T(8,128)(2,1)S(1)} collective-permute-done((bf16[3072,128]{1,0:T(8,128)(2,1)}, bf16[3072,128]{1,0:T(8,128)(2,1)S(1)}, u32[]{:S(2)}, u32[]{:S(2)}) %collective-permute-start.8) | collective-permute-done | bytes 786464 | tf_op jit(solution)/shard_map/ppermute | solution.py:27
  26.3 2.6 %collective-permute-start.11 = (bf16[1536,128]{1,0:T(8,128)(2,1)}, bf16[1536,128]{1,0:T(8,128)(2,1)}, u32[]{:S(2)}, u32[]{:S(2)}) collective-permute-start(bf16[1536,128]{1,0:T(8,128)(2,1)} %slice.17), channel_id=1, source_target_pairs={{0,12},{4,0},{8,4},{12,8},{1,13},{5,1},{9,5},{13,9},{2,14},{6,2},{... | collective-permute-start | bytes 1179656 | tf_op jit(solution)/shard_map/ppermute | solution.py:27
  30.5 2.1 %collective-permute-start.1 = (bf16[1536,128]{1,0:T(8,128)(2,1)}, bf16[1536,128]{1,0:T(8,128)(2,1)S(1)}, u32[]{:S(2)}, u32[]{:S(2)}) collective-permute-start(bf16[1536,128]{1,0:T(8,128)(2,1)} %get-tuple-element.71.refs_0_), channel_id=1, source_target_pairs={{0,3},{1,0},{2,1},{3,2},{4,7},{5,4},{6,5},{7,6},{8,11},{9,8},{10,9... | collective-permute-start | bytes 1179656 | tf_op jit(solution)/shard_map/ppermute | solution.py:27
  32.6 1.9 %collective-permute-done.7.refs_4_.refs_8_ = bf16[3072,128]{1,0:T(8,128)(2,1)S(1)} collective-permute-done((bf16[3072,128]{1,0:T(8,128)(2,1)}, bf16[3072,128]{1,0:T(8,128)(2,1)S(1)}, u32[]{:S(2)}, u32[]{:S(2)}) %collective-permute-start.7) | collective-permute-done | bytes 786464 | tf_op jit(solution)/shard_map/ppermute | solution.py:31
  34.6 2.5 %collective-permute-done.10.refs_7_ = bf16[1536,128]{1,0:T(8,128)(2,1)} collective-permute-done((bf16[1536,128]{1,0:T(8,128)(2,1)}, bf16[1536,128]{1,0:T(8,128)(2,1)}, u32[]{:S(2)}, u32[]{:S(2)}) %collective-permute-start.10) | collective-permute-done | bytes 393248 | tf_op jit(solution)/shard_map/ppermute | solution.py:27
  37.0 2.7 %collective-permute-start.13 = (bf16[3072,128]{1,0:T(8,128)(2,1)S(1)}, bf16[3072,128]{1,0:T(8,128)(2,1)S(1)}, u32[]{:S(2)}, u32[]{:S(2)}) collective-permute-start(bf16[3072,128]{1,0:T(8,128)(2,1)S(1)} %collective-permute-done.7.refs_4_.refs_8_), channel_id=1, source_target_pairs={{0,12},{4,0},{8,4},{12,8},{1,13},{5,1},{9,5},{13,9},{2,14},{6,2},{... | collective-permute-start | bytes 2359304 | tf_op jit(solution)/shard_map/ppermute | solution.py:27
  39.7 4.5 %constant_dynamic-slice_fusion = (bf16[640,1280]{1,0:T(8,128)(2,1)S(1)}, bf16[640,1280]{1,0:T(8,128)(2,1)S(1)}, bf16[640,1280]{1,0:T(8,128)(2,1)}, bf16[640,1280]{1,0:T(8,128)(2,1)S(1)}) fusion(bf16[640,5120]{1,0:T(8,128)(2,1)} %param.13, s32[]{:T(128)S(6)} %select_n.15, s32[]{:T(128)S(6)} %select_n.13, s32[]{:T(128)S(6)} %select_n.12, s32[]{:T(128)S(6)} %select_n.14), kind=kLoop, calls=%fused_computation | loop fusion | bytes 13107216 | tf_op jit(solution)/shard_map/dynamic_slice | solution.py:287
  45.8 3.4 %collective-permute-start.3 = (bf16[1536,128]{1,0:T(8,128)(2,1)S(1)}, bf16[1536,128]{1,0:T(8,128)(2,1)S(1)}, u32[]{:S(2)}, u32[]{:S(2)}) collective-permute-start(bf16[1536,128]{1,0:T(8,128)(2,1)S(1)} %copy-done.6), channel_id=1, source_target_pairs={{0,2},{1,3},{2,0},{3,1},{4,6},{5,7},{6,4},{7,5},{8,10},{9,11},{10,... | collective-permute-start | bytes 1179656 | tf_op jit(solution)/shard_map/ppermute | solution.py:27
  49.2 6.5 %collective-permute-done.3.refs_3_ = bf16[1536,128]{1,0:T(8,128)(2,1)S(1)} collective-permute-done((bf16[1536,128]{1,0:T(8,128)(2,1)S(1)}, bf16[1536,128]{1,0:T(8,128)(2,1)S(1)}, u32[]{:S(2)}, u32[]{:S(2)}) %collective-permute-start.3) | collective-permute-done | bytes 393248 | tf_op jit(solution)/shard_map/ppermute | solution.py:27
  56.4 2.1 %collective-permute-start.5 = (bf16[1024,128]{1,0:T(8,128)(2,1)S(1)}, bf16[1024,128]{1,0:T(8,128)(2,1)S(1)}, u32[]{:S(2)}, u32[]{:S(2)}) collective-permute-start(bf16[1024,128]{1,0:T(8,128)(2,1)S(1)} %collective-permute-done.2.refs_0_), channel_id=1, source_target_pairs={{0,3},{1,0},{2,1},{3,2},{4,7},{5,4},{6,5},{7,6},{8,11},{9,8},{10,9... | collective-permute-start | bytes 786440 | tf_op jit(solution)/shard_map/ppermute | solution.py:27
  59.8 2.5 %collective-permute-start.19 = (bf16[640,1280]{1,0:T(8,128)(2,1)S(1)}, bf16[640,1280]{1,0:T(8,128)(2,1)S(1)}, u32[]{:S(2)}, u32[]{:S(2)}) collective-permute-start(bf16[640,1280]{1,0:T(8,128)(2,1)S(1)} %get-tuple-element.79), channel_id=1, source_target_pairs={{0,80},{16,64},{64,16},{80,0},{1,81},{17,65},{65,17},{81,1},{2,82}... | collective-permute-start | bytes 4915208 | tf_op jit(solution)/shard_map/ppermute | solution.py:340
  64.3 9.9 %shard_map.87 = (bf16[1600,128]{1,0:T(8,128)(2,1)S(1)}, bf16[1600,128]{1,0:T(8,128)(2,1)S(1)}, bf16[1600,128]{1,0:T(8,128)(2,1)S(1)}, bf16[1600,128]{1,0:T(8,128)(2,1)S(1)}) custom-call(bf16[1536,128]{1,0:T(8,128)(2,1)S(1)} %copy-done.6, bf16[1536,128]{1,0:T(8,128)(2,1)S(1)} %copy-done.8, bf16[1536,128]{1,0:T(8,128)(2,1)S(1)} %copy-done.11, ...), custom_call_target="tpu_custom_call" | custom-call | flops 12884901888 | bytes 7864320 | tf_op jit(solution)/shard_map/pallas_call | solution.py:160
  74.5 2.7 %collective-permute-start.15 = (bf16[1536,128]{1,0:T(8,128)(2,1)S(1)}, bf16[1536,128]{1,0:T(8,128)(2,1)S(1)}, u32[]{:S(2)}, u32[]{:S(2)}) collective-permute-start(bf16[1536,128]{1,0:T(8,128)(2,1)S(1)} %slice.19), channel_id=1, source_target_pairs={{0,12},{4,0},{8,4},{12,8},{1,13},{5,1},{9,5},{13,9},{2,14},{6,2},{... | collective-permute-start | bytes 1179656 | tf_op jit(solution)/shard_map/ppermute | solution.py:27
  77.1 6.9 %shard_map.88 = (bf16[1088,128]{1,0:T(8,128)(2,1)S(1)}, bf16[1088,128]{1,0:T(8,128)(2,1)S(1)}, bf16[1088,128]{1,0:T(8,128)(2,1)S(1)}, bf16[1088,128]{1,0:T(8,128)(2,1)S(1)}) custom-call(bf16[1024,128]{1,0:T(8,128)(2,1)S(1)} %collective-permute-done.2.refs_0_, bf16[1024,128]{1,0:T(8,128)(2,1)S(1)} %collective-permute-done.4.refs_1_, ...), custom_call_target="tpu_custom_call" | custom-call | flops 8589934592 | bytes 5242880 | tf_op jit(solution)/shard_map/pallas_call | solution.py:160
  84.1 7.0 %shard_map.89 = (bf16[1088,128]{1,0:T(8,128)(2,1)S(1)}, bf16[1088,128]{1,0:T(8,128)(2,1)S(1)}, bf16[1088,128]{1,0:T(8,128)(2,1)S(1)}, bf16[1088,128]{1,0:T(8,128)(2,1)S(1)}) custom-call(bf16[1024,128]{1,0:T(8,128)(2,1)S(1)} %collective-permute-done.2.refs_0_, bf16[1024,128]{1,0:T(8,128)(2,1)S(1)} %collective-permute-done.4.refs_1_, ...), custom_call_target="tpu_custom_call" | custom-call | flops 8589934592 | bytes 5242880 | tf_op jit(solution)/shard_map/pallas_call | solution.py:160
  93.4 7.1 %collective-permute-start.21 = (bf16[640,1280]{1,0:T(8,128)(2,1)S(1)}, bf16[640,1280]{1,0:T(8,128)(2,1)S(1)}, u32[]{:S(2)}, u32[]{:S(2)}) collective-permute-start(bf16[640,1280]{1,0:T(8,128)(2,1)S(1)} %get-tuple-element.81), channel_id=1, source_target_pairs={{0,32},{32,0},{1,33},{33,1},{2,34},{34,2},{3,35},{35,3},{4,36},{36... | collective-permute-start | bytes 4915208 | tf_op jit(solution)/shard_map/ppermute | solution.py:31
  102.0 1.7 %collective-permute-start.18 = (bf16[1088,128]{1,0:T(8,128)(2,1)S(1)}, bf16[1088,128]{1,0:T(8,128)(2,1)S(1)}, u32[]{:S(2)}, u32[]{:S(2)}) collective-permute-start(bf16[1088,128]{1,0:T(8,128)(2,1)S(1)} %get-tuple-element.70), channel_id=1, source_target_pairs={{0,2},{1,3},{2,0},{3,1},{4,6},{5,7},{6,4},{7,5},{8,10},{9,11},{10,... | collective-permute-start | bytes 835592 | tf_op jit(solution)/shard_map/ppermute | solution.py:27
  103.7 10.4 %shard_map.90 = (bf16[1600,128]{1,0:T(8,128)(2,1)S(1)}, bf16[1600,128]{1,0:T(8,128)(2,1)S(1)}, bf16[1600,128]{1,0:T(8,128)(2,1)S(1)}, bf16[1600,128]{1,0:T(8,128)(2,1)S(1)}) custom-call(bf16[1536,128]{1,0:T(8,128)(2,1)S(1)} %copy-done.6, bf16[1536,128]{1,0:T(8,128)(2,1)S(1)} %copy-done.9, bf16[1536,128]{1,0:T(8,128)(2,1)S(1)} %copy-done.12, ...), custom_call_target="tpu_custom_call" | custom-call | flops 12884901888 | bytes 7864320 | tf_op jit(solution)/shard_map/pallas_call | solution.py:160
  120.2 1.9 %collective-permute-start.28 = (bf16[512,256]{1,0:T(8,128)(2,1)S(1)}, bf16[512,256]{1,0:T(8,128)(2,1)}, u32[]{:S(2)}, u32[]{:S(2)}) collective-permute-start(bf16[512,256]{1,0:T(8,128)(2,1)S(1)} %shard_map.92), channel_id=1, source_target_pairs={{0,80},{16,64},{64,16},{80,0},{1,81},{17,65},{65,17},{81,1},{2,82}... | collective-permute-start | bytes 786440 | tf_op jit(solution)/shard_map/ppermute | solution.py:351
  122.1 2.8 %collective-permute-done.23.refs_1_ = bf16[1600,128]{1,0:T(8,128)(2,1)S(1)} collective-permute-done((bf16[1600,128]{1,0:T(8,128)(2,1)S(1)}, bf16[1600,128]{1,0:T(8,128)(2,1)S(1)}, u32[]{:S(2)}, u32[]{:S(2)}) %collective-permute-start.23) | collective-permute-done | bytes 409632 | tf_op jit(solution)/shard_map/ppermute | solution.py:27
  124.9 3.6 %collective-permute-done.24.refs_2_ = bf16[1600,128]{1,0:T(8,128)(2,1)S(1)} collective-permute-done((bf16[1600,128]{1,0:T(8,128)(2,1)S(1)}, bf16[1600,128]{1,0:T(8,128)(2,1)S(1)}, u32[]{:S(2)}, u32[]{:S(2)}) %collective-permute-start.24) | collective-permute-done | bytes 409632 | tf_op jit(solution)/shard_map/ppermute | solution.py:27
  128.5 6.3 %collective-permute-done.25.refs_3_ = bf16[1600,128]{1,0:T(8,128)(2,1)S(1)} collective-permute-done((bf16[1600,128]{1,0:T(8,128)(2,1)S(1)}, bf16[1600,128]{1,0:T(8,128)(2,1)S(1)}, u32[]{:S(2)}, u32[]{:S(2)}) %collective-permute-start.25) | collective-permute-done | bytes 409632 | tf_op jit(solution)/shard_map/ppermute | solution.py:27
  134.8 2.2 %shard_map.91.refs_0_ = bf16[512,384]{1,0:T(8,128)(2,1)} custom-call(bf16[1600,128]{1,0:T(8,128)(2,1)S(1)} %get-tuple-element.83.refs_0_, bf16[1600,128]{1,0:T(8,128)(2,1)S(1)} %collective-permute-done.23.refs_1_, bf16[1600,128]{1,0:T(8,128)(2,1)S(1)} %collective-permute-done.24.refs_2_, bf16[1600,128]{1,0:T(8,128)(2,1)S(1)} %collective-permute-done.25.refs_3_), custom_call_target="tpu_custom_call" | custom-call | flops 1 | bytes 1 | tf_op jit(solution)/shard_map/pallas_call | solution.py:203
  137.0 3.8 %collective-permute-start.31 = (bf16[512,384]{1,0:T(8,128)(2,1)}, bf16[512,384]{1,0:T(8,128)(2,1)}, u32[]{:S(2)}, u32[]{:S(2)}) collective-permute-start(bf16[512,384]{1,0:T(8,128)(2,1)} %shard_map.91.refs_0_), channel_id=1, source_target_pairs={{0,32},{32,0},{1,33},{33,1},{2,34},{34,2},{3,35},{35,3},{4,36},{36... | collective-permute-start | bytes 1179656 | tf_op jit(solution)/shard_map/ppermute | solution.py:31
  141.4 1.6 %collective-permute-done.29.refs_3_ = bf16[512,256]{1,0:T(8,128)(2,1)} collective-permute-done((bf16[512,256]{1,0:T(8,128)(2,1)S(1)}, bf16[512,256]{1,0:T(8,128)(2,1)}, u32[]{:S(2)}, u32[]{:S(2)}) %collective-permute-start.29) | collective-permute-done | bytes 262176 | tf_op jit(solution)/shard_map/ppermute | solution.py:31
  146.1 5.6 %shard_map.93.refs_4_ = f32[512,1280]{1,0:T(8,128)S(1)} custom-call(s32[2]{0:T(128)S(1)} %pad_add_fusion.at_ref, bf16[512,384]{1,0:T(8,128)(2,1)} %shard_map.91.refs_0_, bf16[512,256]{1,0:T(8,128)(2,1)S(1)} %collective-permute-done.27.refs_1_, bf16[512,256]{1,0:T(8,128)(2,1)} %collective-permute-done.28.refs_2_, ...), custom_call_target="tpu_custom_call" | custom-call | flops 1 | bytes 1 | tf_op jit(solution)/shard_map/pallas_call | solution.py:267
  154.2 3.7 %shard_map.94 = (bf16[256,1280]{1,0:T(8,128)(2,1)}, bf16[256,1280]{1,0:T(8,128)(2,1)}) custom-call(s32[2]{0:T(128)S(1)} %pad_add_fusion.at_ref, bf16[512,384]{1,0:T(8,128)(2,1)} %collective-permute-done.26.refs_0_, bf16[512,384]{1,0:T(8,128)(2,1)S(1)} %collective-permute-done.32.refs_1_, bf16[640,1280]{1,0:T(8,128)(2,1)S(1)} %collective-permute-done.20.refs_7_.refs_2_, ...), custom_call_target="tpu_custom_call" | custom-call | flops 1 | bytes 1 | tf_op jit(solution)/shard_map/pallas_call | solution.py:267
  (75 shorter events, 26.4 us)
Async XLA Ops:
  3.8 20.9 %collective-permute-start.8 = (bf16[3072,128]{1,0:T(8,128)(2,1)}, bf16[3072,128]{1,0:T(8,128)(2,1)S(1)}, u32[]{:S(2)}, u32[]{:S(2)}) collective-permute-start(bf16[3072,128]{1,0:T(8,128)(2,1)} %get-tuple-element.53.refs_4_.refs_8_), channel_id=1, source_target_pairs={{0,4},{4,8},{8,12},{12,0},{1,5},{5,9},{9,13},{13,1},{2,6},{6,10},{... | collective-permute-start | bytes 2359304 | tf_op jit(solution)/shard_map/ppermute | solution.py:27
  6.0 19.5 %collective-permute-start.9 = (bf16[3072,128]{1,0:T(8,128)(2,1)}, bf16[3072,128]{1,0:T(8,128)(2,1)S(1)}, u32[]{:S(2)}, u32[]{:S(2)}) collective-permute-start(bf16[3072,128]{1,0:T(8,128)(2,1)} %get-tuple-element.53.refs_4_.refs_8_), channel_id=1, source_target_pairs={{0,12},{4,0},{8,4},{12,8},{1,13},{5,1},{9,5},{13,9},{2,14},{6,2},{... | collective-permute-start | bytes 2359304 | tf_op jit(solution)/shard_map/ppermute | solution.py:27
  7.4 8.4 %collective-permute-start.2 = (bf16[1024,128]{1,0:T(8,128)(2,1)}, bf16[1024,128]{1,0:T(8,128)(2,1)S(1)}, u32[]{:S(2)}, u32[]{:S(2)}) collective-permute-start(bf16[1024,128]{1,0:T(8,128)(2,1)} %get-tuple-element.48), channel_id=1, source_target_pairs={{0,16},{16,0},{1,17},{17,1},{2,18},{18,2},{3,19},{19,3},{4,20},{20... | collective-permute-start | bytes 786440 | tf_op jit(solution)/shard_map/ppermute | solution.py:31
  15.8 18.7 %collective-permute-start.7 = (bf16[3072,128]{1,0:T(8,128)(2,1)}, bf16[3072,128]{1,0:T(8,128)(2,1)S(1)}, u32[]{:S(2)}, u32[]{:S(2)}) collective-permute-start(bf16[3072,128]{1,0:T(8,128)(2,1)} %get-tuple-element.52), channel_id=1, source_target_pairs={{0,16},{16,0},{1,17},{17,1},{2,18},{18,2},{3,19},{19,3},{4,20},{20... | collective-permute-start | bytes 2359304 | tf_op jit(solution)/shard_map/ppermute | solution.py:31
  26.3 10.8 %collective-permute-start.10 = (bf16[1536,128]{1,0:T(8,128)(2,1)}, bf16[1536,128]{1,0:T(8,128)(2,1)}, u32[]{:S(2)}, u32[]{:S(2)}) collective-permute-start(bf16[1536,128]{1,0:T(8,128)(2,1)} %slice.16), channel_id=1, source_target_pairs={{0,4},{4,8},{8,12},{12,0},{1,5},{5,9},{9,13},{13,1},{2,6},{6,10},{... | collective-permute-start | bytes 1179656 | tf_op jit(solution)/shard_map/ppermute | solution.py:27
  26.3 10.7 %collective-permute-start.11 = (bf16[1536,128]{1,0:T(8,128)(2,1)}, bf16[1536,128]{1,0:T(8,128)(2,1)}, u32[]{:S(2)}, u32[]{:S(2)}) collective-permute-start(bf16[1536,128]{1,0:T(8,128)(2,1)} %slice.17), channel_id=1, source_target_pairs={{0,12},{4,0},{8,4},{12,8},{1,13},{5,1},{9,5},{13,9},{2,14},{6,2},{... | collective-permute-start | bytes 1179656 | tf_op jit(solution)/shard_map/ppermute | solution.py:27
  29.0 15.3 %collective-permute-start = (bf16[1536,128]{1,0:T(8,128)(2,1)}, bf16[1536,128]{1,0:T(8,128)(2,1)S(1)}, u32[]{:S(2)}, u32[]{:S(2)}) collective-permute-start(bf16[1536,128]{1,0:T(8,128)(2,1)} %get-tuple-element.71.refs_0_), channel_id=1, source_target_pairs={{0,1},{1,2},{2,3},{3,0},{4,5},{5,6},{6,7},{7,4},{8,9},{9,10},{10,1... | collective-permute-start | bytes 1179656 | tf_op jit(solution)/shard_map/ppermute | solution.py:27
  30.5 14.5 %collective-permute-start.1 = (bf16[1536,128]{1,0:T(8,128)(2,1)}, bf16[1536,128]{1,0:T(8,128)(2,1)S(1)}, u32[]{:S(2)}, u32[]{:S(2)}) collective-permute-start(bf16[1536,128]{1,0:T(8,128)(2,1)} %get-tuple-element.71.refs_0_), channel_id=1, source_target_pairs={{0,3},{1,0},{2,1},{3,2},{4,7},{5,4},{6,5},{7,6},{8,11},{9,8},{10,9... | collective-permute-start | bytes 1179656 | tf_op jit(solution)/shard_map/ppermute | solution.py:27
  37.0 22.8 %collective-permute-start.12 = (bf16[3072,128]{1,0:T(8,128)(2,1)S(1)}, bf16[3072,128]{1,0:T(8,128)(2,1)S(1)}, u32[]{:S(2)}, u32[]{:S(2)}) collective-permute-start(bf16[3072,128]{1,0:T(8,128)(2,1)S(1)} %collective-permute-done.7.refs_4_.refs_8_), channel_id=1, source_target_pairs={{0,4},{4,8},{8,12},{12,0},{1,5},{5,9},{9,13},{13,1},{2,6},{6,10},{... | collective-permute-start | bytes 2359304 | tf_op jit(solution)/shard_map/ppermute | solution.py:27
  37.0 25.3 %collective-permute-start.13 = (bf16[3072,128]{1,0:T(8,128)(2,1)S(1)}, bf16[3072,128]{1,0:T(8,128)(2,1)S(1)}, u32[]{:S(2)}, u32[]{:S(2)}) collective-permute-start(bf16[3072,128]{1,0:T(8,128)(2,1)S(1)} %collective-permute-done.7.refs_4_.refs_8_), channel_id=1, source_target_pairs={{0,12},{4,0},{8,4},{12,8},{1,13},{5,1},{9,5},{13,9},{2,14},{6,2},{... | collective-permute-start | bytes 2359304 | tf_op jit(solution)/shard_map/ppermute | solution.py:27
  45.8 9.9 %collective-permute-start.3 = (bf16[1536,128]{1,0:T(8,128)(2,1)S(1)}, bf16[1536,128]{1,0:T(8,128)(2,1)S(1)}, u32[]{:S(2)}, u32[]{:S(2)}) collective-permute-start(bf16[1536,128]{1,0:T(8,128)(2,1)S(1)} %copy-done.6), channel_id=1, source_target_pairs={{0,2},{1,3},{2,0},{3,1},{4,6},{5,7},{6,4},{7,5},{8,10},{9,11},{10,... | collective-permute-start | bytes 1179656 | tf_op jit(solution)/shard_map/ppermute | solution.py:27
  55.7 18.7 %collective-permute-start.4 = (bf16[1024,128]{1,0:T(8,128)(2,1)S(1)}, bf16[1024,128]{1,0:T(8,128)(2,1)S(1)}, u32[]{:S(2)}, u32[]{:S(2)}) collective-permute-start(bf16[1024,128]{1,0:T(8,128)(2,1)S(1)} %collective-permute-done.2.refs_0_), channel_id=1, source_target_pairs={{0,1},{1,2},{2,3},{3,0},{4,5},{5,6},{6,7},{7,4},{8,9},{9,10},{10,1... | collective-permute-start | bytes 786440 | tf_op jit(solution)/shard_map/ppermute | solution.py:27
  56.4 18.0 %collective-permute-start.5 = (bf16[1024,128]{1,0:T(8,128)(2,1)S(1)}, bf16[1024,128]{1,0:T(8,128)(2,1)S(1)}, u32[]{:S(2)}, u32[]{:S(2)}) collective-permute-start(bf16[1024,128]{1,0:T(8,128)(2,1)S(1)} %collective-permute-done.2.refs_0_), channel_id=1, source_target_pairs={{0,3},{1,0},{2,1},{3,2},{4,7},{5,4},{6,5},{7,6},{8,11},{9,8},{10,9... | collective-permute-start | bytes 786440 | tf_op jit(solution)/shard_map/ppermute | solution.py:27
  58.5 18.6 %collective-permute-start.6 = (bf16[1024,128]{1,0:T(8,128)(2,1)S(1)}, bf16[1024,128]{1,0:T(8,128)(2,1)S(1)}, u32[]{:S(2)}, u32[]{:S(2)}) collective-permute-start(bf16[1024,128]{1,0:T(8,128)(2,1)S(1)} %collective-permute-done.2.refs_0_), channel_id=1, source_target_pairs={{0,2},{1,3},{2,0},{3,1},{4,6},{5,7},{6,4},{7,5},{8,10},{9,11},{10,... | collective-permute-start | bytes 786440 | tf_op jit(solution)/shard_map/ppermute | solution.py:27
  59.8 32.6 %collective-permute-start.19 = (bf16[640,1280]{1,0:T(8,128)(2,1)S(1)}, bf16[640,1280]{1,0:T(8,128)(2,1)S(1)}, u32[]{:S(2)}, u32[]{:S(2)}) collective-permute-start(bf16[640,1280]{1,0:T(8,128)(2,1)S(1)} %get-tuple-element.79), channel_id=1, source_target_pairs={{0,80},{16,64},{64,16},{80,0},{1,81},{17,65},{65,17},{81,1},{2,82}... | collective-permute-start | bytes 4915208 | tf_op jit(solution)/shard_map/ppermute | solution.py:340
  62.3 31.1 %collective-permute-start.20 = (bf16[640,1280]{1,0:T(8,128)(2,1)S(1)}, bf16[640,1280]{1,0:T(8,128)(2,1)S(1)}, u32[]{:S(2)}, u32[]{:S(2)}) collective-permute-start(bf16[640,1280]{1,0:T(8,128)(2,1)S(1)} %get-tuple-element.80), channel_id=1, source_target_pairs={{0,64},{64,0},{1,65},{65,1},{2,66},{66,2},{3,67},{67,3},{4,68},{68... | collective-permute-start | bytes 4915208 | tf_op jit(solution)/shard_map/ppermute | solution.py:31
  74.4 9.7 %collective-permute-start.14 = (bf16[1536,128]{1,0:T(8,128)(2,1)S(1)}, bf16[1536,128]{1,0:T(8,128)(2,1)S(1)}, u32[]{:S(2)}, u32[]{:S(2)}) collective-permute-start(bf16[1536,128]{1,0:T(8,128)(2,1)S(1)} %slice.18), channel_id=1, source_target_pairs={{0,4},{4,8},{8,12},{12,0},{1,5},{5,9},{9,13},{13,1},{2,6},{6,10},{... | collective-permute-start | bytes 1179656 | tf_op jit(solution)/shard_map/ppermute | solution.py:27
  74.5 9.6 %collective-permute-start.15 = (bf16[1536,128]{1,0:T(8,128)(2,1)S(1)}, bf16[1536,128]{1,0:T(8,128)(2,1)S(1)}, u32[]{:S(2)}, u32[]{:S(2)}) collective-permute-start(bf16[1536,128]{1,0:T(8,128)(2,1)S(1)} %slice.19), channel_id=1, source_target_pairs={{0,12},{4,0},{8,4},{12,8},{1,13},{5,1},{9,5},{13,9},{2,14},{6,2},{... | collective-permute-start | bytes 1179656 | tf_op jit(solution)/shard_map/ppermute | solution.py:27
  93.4 22.2 %collective-permute-start.21 = (bf16[640,1280]{1,0:T(8,128)(2,1)S(1)}, bf16[640,1280]{1,0:T(8,128)(2,1)S(1)}, u32[]{:S(2)}, u32[]{:S(2)}) collective-permute-start(bf16[640,1280]{1,0:T(8,128)(2,1)S(1)} %get-tuple-element.81), channel_id=1, source_target_pairs={{0,32},{32,0},{1,33},{33,1},{2,34},{34,2},{3,35},{35,3},{4,36},{36... | collective-permute-start | bytes 4915208 | tf_op jit(solution)/shard_map/ppermute | solution.py:31
  100.5 15.1 %collective-permute-start.22 = (bf16[640,1280]{1,0:T(8,128)(2,1)S(1)}, bf16[640,1280]{1,0:T(8,128)(2,1)S(1)}, u32[]{:S(2)}, u32[]{:S(2)}) collective-permute-start(bf16[640,1280]{1,0:T(8,128)(2,1)S(1)} %collective-permute-done.19), channel_id=1, source_target_pairs={{0,32},{32,0},{1,33},{33,1},{2,34},{34,2},{3,35},{35,3},{4,36},{36... | collective-permute-start | bytes 4915208 | tf_op jit(solution)/shard_map/ppermute | solution.py:31
  100.5 13.5 %collective-permute-start.16 = (bf16[1088,128]{1,0:T(8,128)(2,1)S(1)}, bf16[1088,128]{1,0:T(8,128)(2,1)S(1)}, u32[]{:S(2)}, u32[]{:S(2)}) collective-permute-start(bf16[1088,128]{1,0:T(8,128)(2,1)S(1)} %get-tuple-element.68), channel_id=1, source_target_pairs={{0,3},{1,0},{2,1},{3,2},{4,7},{5,4},{6,5},{7,6},{8,11},{9,8},{10,9... | collective-permute-start | bytes 835592 | tf_op jit(solution)/shard_map/ppermute | solution.py:27
  101.1 12.9 %collective-permute-start.17 = (bf16[1088,128]{1,0:T(8,128)(2,1)S(1)}, bf16[1088,128]{1,0:T(8,128)(2,1)S(1)}, u32[]{:S(2)}, u32[]{:S(2)}) collective-permute-start(bf16[1088,128]{1,0:T(8,128)(2,1)S(1)} %get-tuple-element.69), channel_id=1, source_target_pairs={{0,1},{1,2},{2,3},{3,0},{4,5},{5,6},{6,7},{7,4},{8,9},{9,10},{10,1... | collective-permute-start | bytes 835592 | tf_op jit(solution)/shard_map/ppermute | solution.py:27
  102.0 13.6 %collective-permute-start.18 = (bf16[1088,128]{1,0:T(8,128)(2,1)S(1)}, bf16[1088,128]{1,0:T(8,128)(2,1)S(1)}, u32[]{:S(2)}, u32[]{:S(2)}) collective-permute-start(bf16[1088,128]{1,0:T(8,128)(2,1)S(1)} %get-tuple-element.70), channel_id=1, source_target_pairs={{0,2},{1,3},{2,0},{3,1},{4,6},{5,7},{6,4},{7,5},{8,10},{9,11},{10,... | collective-permute-start | bytes 835592 | tf_op jit(solution)/shard_map/ppermute | solution.py:27
  115.6 9.2 %collective-permute-start.23 = (bf16[1600,128]{1,0:T(8,128)(2,1)S(1)}, bf16[1600,128]{1,0:T(8,128)(2,1)S(1)}, u32[]{:S(2)}, u32[]{:S(2)}) collective-permute-start(bf16[1600,128]{1,0:T(8,128)(2,1)S(1)} %get-tuple-element.84), channel_id=1, source_target_pairs={{0,3},{1,0},{2,1},{3,2},{4,7},{5,4},{6,5},{7,6},{8,11},{9,8},{10,9... | collective-permute-start | bytes 1228808 | tf_op jit(solution)/shard_map/ppermute | solution.py:27
  116.7 11.8 %collective-permute-start.24 = (bf16[1600,128]{1,0:T(8,128)(2,1)S(1)}, bf16[1600,128]{1,0:T(8,128)(2,1)S(1)}, u32[]{:S(2)}, u32[]{:S(2)}) collective-permute-start(bf16[1600,128]{1,0:T(8,128)(2,1)S(1)} %get-tuple-element.85), channel_id=1, source_target_pairs={{0,1},{1,2},{2,3},{3,0},{4,5},{5,6},{6,7},{7,4},{8,9},{9,10},{10,1... | collective-permute-start | bytes 1228808 | tf_op jit(solution)/shard_map/ppermute | solution.py:27
  117.2 17.6 %collective-permute-start.25 = (bf16[1600,128]{1,0:T(8,128)(2,1)S(1)}, bf16[1600,128]{1,0:T(8,128)(2,1)S(1)}, u32[]{:S(2)}, u32[]{:S(2)}) collective-permute-start(bf16[1600,128]{1,0:T(8,128)(2,1)S(1)} %get-tuple-element.86), channel_id=1, source_target_pairs={{0,2},{1,3},{2,0},{3,1},{4,6},{5,7},{6,4},{7,5},{8,10},{9,11},{10,... | collective-permute-start | bytes 1228808 | tf_op jit(solution)/shard_map/ppermute | solution.py:27
  119.6 21.2 %collective-permute-start.27 = (bf16[512,256]{1,0:T(8,128)(2,1)S(1)}, bf16[512,256]{1,0:T(8,128)(2,1)S(1)}, u32[]{:S(2)}, u32[]{:S(2)}) collective-permute-start(bf16[512,256]{1,0:T(8,128)(2,1)S(1)} %shard_map.92), channel_id=1, source_target_pairs={{0,16},{16,0},{1,17},{17,1},{2,18},{18,2},{3,19},{19,3},{4,20},{20... | collective-permute-start | bytes 786440 | tf_op jit(solution)/shard_map/ppermute | solution.py:31
  120.2 20.9 %collective-permute-start.28 = (bf16[512,256]{1,0:T(8,128)(2,1)S(1)}, bf16[512,256]{1,0:T(8,128)(2,1)}, u32[]{:S(2)}, u32[]{:S(2)}) collective-permute-start(bf16[512,256]{1,0:T(8,128)(2,1)S(1)} %shard_map.92), channel_id=1, source_target_pairs={{0,80},{16,64},{64,16},{80,0},{1,81},{17,65},{65,17},{81,1},{2,82}... | collective-permute-start | bytes 786440 | tf_op jit(solution)/shard_map/ppermute | solution.py:351
  137.0 6.2 %collective-permute-start.31 = (bf16[512,384]{1,0:T(8,128)(2,1)}, bf16[512,384]{1,0:T(8,128)(2,1)}, u32[]{:S(2)}, u32[]{:S(2)}) collective-permute-start(bf16[512,384]{1,0:T(8,128)(2,1)} %shard_map.91.refs_0_), channel_id=1, source_target_pairs={{0,32},{32,0},{1,33},{33,1},{2,34},{34,2},{3,35},{35,3},{4,36},{36... | collective-permute-start | bytes 1179656 | tf_op jit(solution)/shard_map/ppermute | solution.py:31
  140.8 11.1 %collective-permute-start.26 = (bf16[512,384]{1,0:T(8,128)(2,1)}, bf16[512,384]{1,0:T(8,128)(2,1)}, u32[]{:S(2)}, u32[]{:S(2)}) collective-permute-start(bf16[512,384]{1,0:T(8,128)(2,1)} %shard_map.91.refs_0_), channel_id=1, source_target_pairs={{0,64},{64,0},{1,65},{65,1},{2,66},{66,2},{3,67},{67,3},{4,68},{68... | collective-permute-start | bytes 1179656 | tf_op jit(solution)/shard_map/ppermute | solution.py:31
  140.8 2.2 %collective-permute-start.29 = (bf16[512,256]{1,0:T(8,128)(2,1)S(1)}, bf16[512,256]{1,0:T(8,128)(2,1)}, u32[]{:S(2)}, u32[]{:S(2)}) collective-permute-start(bf16[512,256]{1,0:T(8,128)(2,1)S(1)} %collective-permute-done.27.refs_1_), channel_id=1, source_target_pairs={{0,32},{32,0},{1,33},{33,1},{2,34},{34,2},{3,35},{35,3},{4,36},{36... | collective-permute-start | bytes 786440 | tf_op jit(solution)/shard_map/ppermute | solution.py:31
  151.9 2.3 %collective-permute-start.32 = (bf16[512,384]{1,0:T(8,128)(2,1)}, bf16[512,384]{1,0:T(8,128)(2,1)S(1)}, u32[]{:S(2)}, u32[]{:S(2)}) collective-permute-start(bf16[512,384]{1,0:T(8,128)(2,1)} %collective-permute-done.26.refs_0_), channel_id=1, source_target_pairs={{0,32},{32,0},{1,33},{33,1},{2,34},{34,2},{3,35},{35,3},{4,36},{36... | collective-permute-start | bytes 1179656 | tf_op jit(solution)/shard_map/ppermute | solution.py:31
  (14 other events, 131.4 us)
